TPU v7x, 256 devices: a whole 4x4x8 slice. The times are simulated.
256 devices in a mesh: dp: 16 (over z_lo, y), tensor: 16 (over x, z_hi, core).
Axes of the slice: x: 4, y: 4, z: 8 (z_hi: 2, z_lo: 4; z = z_hi * 4 + z_lo), core: 2. Of those that a mesh axis runs over, the one named last changes fastest.
Arguments:
- gradient: bfloat16 [16, 2048, 8192], P('dp', 'tensor'), may hold values from -80 to 80
- error_feed: float32 [16, 2048, 8192], P('dp', 'tensor'), may hold values from -4 to 4
- factor_old: float32 [8192, 64], P('tensor'), may hold values from -0.0625 to 0.0625
Outputs:
- error_new: float32 [16, 2048, 8192], P('dp', 'tensor')
- left_factor: float32 [2048, 64], P('tensor')
- right_factor: float32 [8192, 64], P('tensor')
All inputs are finite; a program needn't handle non-finite values.
Results may differ from a plain program's by a relative error of at most 0.0003.
Values sent between devices are 32-bit elements; how exact they have to be, the bound alone decides.
No kernel may reach another device: no remote copies, remote signals or barrier semaphores. Data moves between devices by JAX's collectives and lax.ppermute only.
A program may use at most 64 MiB of HBM per device.

v0:
```python
import jax
import jax.numpy as jnp
from jax import lax
from jax.sharding import PartitionSpec as P


def cross_product(left, right):
    return lax.dot_general(
        left,
        right,
        (((0,), (0,)), ((), ())),
        precision=lax.Precision.HIGHEST,
        preferred_element_type=jnp.float32,
    )


def body(gradient, error_feed, factor_old):
    highest = lax.Precision.HIGHEST
    merged = gradient[0].astype(jnp.float32) + error_feed[0]
    local_left = jnp.dot(
        merged,
        lax.all_gather(factor_old, "tensor", axis=0, tiled=True),
        precision=highest,
        preferred_element_type=jnp.float32,
    )
    left_sum = lax.psum(local_left, "dp")
    gram = lax.psum(cross_product(left_sum, left_sum), "tensor")
    lower = jnp.linalg.cholesky(gram)
    left_factor = jax.scipy.linalg.solve_triangular(lower, left_sum.T, lower=True).T
    replicas = lax.axis_size("dp")
    shard_cols = merged.shape[1] // lax.axis_size("tensor")
    term = cross_product(merged, left_factor)
    summed = lax.psum(lax.psum(term, "tensor"), "dp")
    right_full = summed / replicas
    right_factor = lax.dynamic_slice_in_dim(
        right_full, lax.axis_index("tensor") * shard_cols, shard_cols, 0
    )
    approx = lax.dot_general(
        left_factor,
        right_full,
        (((1,), (1,)), ((), ())),
        precision=highest,
        preferred_element_type=jnp.float32,
    )
    error_new = (merged - approx)[None]
    return (error_new, left_factor, right_factor)


def solution(mesh):
    return jax.shard_map(
        body,
        mesh=mesh,
        in_specs=(P("dp", "tensor", None), P("dp", "tensor", None), P("tensor", None)),
        out_specs=(P("dp", "tensor", None), P("tensor", None), P("tensor", None)),
        check_vma=False,
    )
```

profile of v0, /device:TPU:1, one launch (start us, length us, event | category | flops | bytes accessed | tf_op | source)
XLA Modules:
  0.0 631.4 jit_solution(12215850355170925263)
XLA Ops:
  7.2 0.0 all-gather.2.cloned.1.call-start
  7.2 0.7 all-gather.2.cloned.1.call-update
  7.9 0.0 copy-start.1
  7.9 0.0 all-reduce.3.cloned.1.call-start
  8.0 70.0 %all-gather.2.cloned.1.call-done = f32[8192,64]{0,1:T(8,128)} async-done(((f32[512,64]{0,1:T(8,128)}), f32[8192,64]{0,1:T(8,128)}) %all-gather.2.cloned.1.call-update) | async-done | bytes 2097168 | tf_op jit(solution)/shard_map/all_gather | solution.py:22
  77.9 7.9 %fusion.3 = f32[128,64]{0,1:T(8,128)S(1)} fusion(f32[8192,64]{0,1:T(8,128)} %all-gather.2.cloned.1.call-done, f32[1,128,8192]{2,1,0:T(8,128)} %param.4, bf16[1,128,8192]{2,1,0:T(8,128)(2,1)} %param.3), kind=kOutput, calls=%fused_computation.4 | convolution fusion | flops 807403520 | bytes 8421376 | tf_op jit(solution)/shard_map/dot_general | solution.py:20
  85.8 61.9 %psum.28 = f32[128,64]{0,1:T(8,128)S(1)} all-reduce(f32[128,64]{0,1:T(8,128)S(1)} %fusion.3), channel_id=1, replica_groups=mesh['dp'=16,'tensor'=16] {'dp'}, use_global_device_ids=true, to_apply=%region_0.0 | all-reduce | flops 8192 | bytes 65536 | tf_op jit(solution)/shard_map/psum | solution.py:26
  147.7 0.2 fusion.9
  147.9 90.4 %psum.29 = f32[64,64]{0,1:T(8,128)S(1)} all-reduce(f32[64,64]{0,1:T(8,128)S(1)} %fusion.9), channel_id=1, replica_groups=mesh['dp'=16,'tensor'=16] {'tensor'}, use_global_device_ids=true, to_apply=%region_1.0 | all-reduce | flops 4096 | bytes 32768 | tf_op jit(solution)/shard_map/psum | solution.py:27
  238.3 0.1 copy.7
  238.4 5.8 cholesky.16
  244.3 0.6 compare_reduce_fusion
  244.9 0.7 fusion.5
  245.6 4.9 custom-call.7
  250.5 0.3 fusion.6
  250.7 0.0 copy-done.1
  250.7 0.0 copy-start.2
  250.7 6.2 fusion.1
  257.0 0.0 all-reduce.3.cloned.1.call-update
  257.0 0.2 all-reduce.5.cloned.1.call-start
  257.2 194.9 %all-reduce.3.cloned.1.call-done = f32[8192,64]{0,1:T(8,128)} async-done(((f32[8192,64]{0,1:T(8,128)}), f32[8192,64]{0,1:T(8,128)}) %all-reduce.3.cloned.1.call-update) | async-done | bytes 2097168 | tf_op jit(solution)/shard_map/psum | solution.py:33
  452.2 0.0 all-reduce.5.cloned.1.call-update
  452.2 162.2 %all-reduce.5.cloned.1.call-done = f32[8192,64]{0,1:T(8,128)} async-done(((f32[8192,64]{0,1:T(8,128)}), f32[8192,64]{0,1:T(8,128)}) %all-reduce.5.cloned.1.call-update) | async-done | bytes 2097168 | tf_op jit(solution)/shard_map/psum | solution.py:33
  614.4 0.0 copy-start
  614.4 1.9 broadcast_multiply_fusion
  616.3 0.7 constant_dynamic-slice_fusion
  616.9 0.0 copy-done.2
  616.9 0.2 copy-done
  617.2 7.7 %fusion = f32[1,128,8192]{2,1,0:T(8,128)} fusion(f32[64,128]{1,0:T(8,128)S(1)} %fusion.6, f32[1,128,8192]{2,1,0:T(8,128)S(1)} %copy-done, bf16[1,128,8192]{2,1,0:T(8,128)(2,1)S(1)} %copy-done.1, f32[8192,64]{0,1:T(8,128)} %all-reduce.5.cloned.1.call-done), kind=kOutput, calls=%fused_computation.1 | convolution fusion | flops 808976384 | bytes 12615680 | tf_op jit(solution)/shard_map/dot_general | solution.py:38
  (2 shorter events, 0.0 us)
Async XLA Ops:
  7.2 70.7 %all-gather.2.cloned.1.call-start = ((), (), s32[]{:S(2)}) async-start(), calls=%async_computation | async-start | bytes 2228224 | tf_op jit(solution)/shard_map/all_gather | solution.py:22
  7.9 242.8 %copy-start.1 = (bf16[1,128,8192]{2,1,0:T(8,128)(2,1)S(1)}, bf16[1,128,8192]{2,1,0:T(8,128)(2,1)}, u32[]{:S(2)}) copy-start(bf16[1,128,8192]{2,1,0:T(8,128)(2,1)} %param.3) | copy-start | bytes 6291460
  7.9 444.3 %all-reduce.3.cloned.1.call-start = ((), (), s32[]{:S(2)}) async-start(), calls=%async_computation.1 | async-start | bytes 4194304 | tf_op jit(solution)/shard_map/psum | solution.py:33
  250.7 366.2 %copy-start.2 = (f32[64,128]{1,0:T(8,128)}, f32[64,128]{1,0:T(8,128)S(1)}, u32[]{:S(2)}) copy-start(f32[64,128]{1,0:T(8,128)S(1)} %fusion.6) | copy-start | bytes 98308
  257.0 357.4 %all-reduce.5.cloned.1.call-start = ((), (), s32[]{:S(2)}) async-start(), calls=%async_computation.2 | async-start | bytes 4194304 | tf_op jit(solution)/shard_map/psum | solution.py:33
  614.4 2.8 copy-start
Sparse Core Ops, SparseCore 0:
  10.7 67.1 all-gather.1
  257.1 194.9 all-reduce.2
  454.8 159.4 all-reduce.4
where the time goes:
time: 640 us; the launch traced here: 631 us
  waiting for transfers between devices  428 us (67%)
  blocking collectives  152 us (24%)
  matrix products  22.2 us (3%)
  other arithmetic  14 us (2%)
  between operations  13.8 us (2%)
    psum x2, waiting for transfers between devices, body(): summed = lax.psum(lax.psum(term, 'tensor'), 'dp')  357 us
    psum x1, blocking collectives, body(): gram = lax.psum(cross_product(left_sum, left_sum), 'tensor')  90.4 us
    all_gather x1, waiting for transfers between devices, body(): lax.all_gather(factor_old, 'tensor', axis=0, tiled=True)  70 us
    psum x1, blocking collectives, body(): left_sum = lax.psum(local_left, 'dp')  61.9 us
  transfers between devices with their start and end apart: 3, of which 3 were waited for; matrix products, arithmetic and copies ran while one was open for 0% of the time, Pallas kernels for 0%

commit v1 on v0

v1 whole, which is shorter than its diff:
```python
import functools

import jax
import jax.numpy as jnp
import numpy as np
from jax import lax
from jax.experimental import pallas as pl
from jax.experimental.pallas import tpu as pltpu
from jax.sharding import Mesh, PartitionSpec as P

AXES = ("zlo", "y", "x", "zhi", "core")
SIZES = (4, 4, 4, 2, 2)
ROWS, COLS, RANK, BLOCK = 128, 8192, 64, 512
CHUNKS, WIDE, EXTRA = 16, 256, 16
HALF = COLS // 2
LIMIT = 48 * 1024 * 1024
F32, BF16 = jnp.float32, jnp.bfloat16
VMEM = pl.BlockSpec(memory_space=pltpu.VMEM)


def shift(value, zlo=0, y=0, x=0, zhi=0, core=0):
    pairs = []
    for source in np.ndindex(*SIZES):
        target = tuple(a ^ b for a, b in zip(source, (zlo, y, x, zhi, core)))
        pairs.append((int(np.ravel_multi_index(source, SIZES)), int(np.ravel_multi_index(target, SIZES))))
    return lax.ppermute(value, AXES, pairs)


def ring(value, axis):
    return [shift(value, **{axis: step}) for step in (1, 2, 3)]


def total(value, axis):
    one, two, three = ring(value, axis)
    return (value + one) + (two + three)


def split(value):
    high = value.astype(BF16)
    return high, (value - high.astype(F32)).astype(BF16)


def dot(left, right, contract=((1,), (0,)), precision=None):
    return lax.dot_general(left, right, (contract, ((), ())), precision=precision, preferred_element_type=F32)


def call(kernel, out_shape, **kw):
    return pl.pallas_call(
        kernel,
        out_shape=out_shape,
        compiler_params=pltpu.CompilerParams(vmem_limit_bytes=LIMIT),
        **kw,
    )


def left_kernel(slots, first, *refs):
    merged, out = refs[0], refs[-1]
    factors = refs[1:-1] if first else refs[2:-1]
    x, zhi, core = lax.axis_index("x"), lax.axis_index("zhi"), lax.axis_index("core")
    acc = jnp.zeros((2 * ROWS, 2 * RANK), F32)
    for (sx, sc), factor in zip(slots, factors):
        for sh in range(2):
            block = (x ^ sx) * 4 + (zhi ^ sh) * 2 + (core ^ sc)
            part = merged[:, pl.ds(pl.multiple_of(block * BLOCK, BLOCK), BLOCK)]
            rows = jnp.concatenate(split(part), 0)
            cols = jnp.concatenate(split(factor[sh]), 0)
            acc = acc + dot(rows, cols, ((1,), (1,)))
    both = acc[:ROWS] + acc[ROWS:]
    turned = both.T
    result = turned[:RANK] + turned[RANK:]
    out[...] = result if first else refs[1][...] + result


def left_part(slots, merged, factors, before=None):
    first = before is None
    args = [merged] + ([] if first else [before]) + list(factors)
    return call(
        functools.partial(left_kernel, slots, first),
        jax.ShapeDtypeStruct((RANK, ROWS), F32),
        in_specs=[VMEM] * len(args),
        out_specs=VMEM,
    )(*args)


def cross_kernel(flip, with_gram, merged, left, out):
    core = lax.axis_index("core") ^ flip
    high, low = split(left[...])
    lhs = jnp.concatenate([jnp.concatenate([high, high], 1), jnp.concatenate([low, low], 1)], 0)
    for chunk in range(CHUNKS):
        start = pl.multiple_of(core * HALF + chunk * WIDE, WIDE)
        rhs = jnp.concatenate(split(merged[:, pl.ds(start, WIDE)]), 0)
        both = dot(lhs, rhs)
        out[chunk * RANK : (chunk + 1) * RANK, :] = both[:RANK] + both[RANK:]
    if with_gram:
        gram = dot(left[...], left[...], ((1,), (1,)), lax.Precision.HIGHEST)
        out[CHUNKS * RANK :, :] = jnp.concatenate([gram[q * EXTRA : (q + 1) * EXTRA] for q in range(4)], 1)


def cross_part(flip, with_gram, merged, left):
    height = CHUNKS * RANK + (EXTRA if with_gram else 0)
    return call(
        functools.partial(cross_kernel, flip, with_gram),
        jax.ShapeDtypeStruct((height, WIDE), F32),
        in_specs=[VMEM] * 2,
        out_specs=VMEM,
    )(merged, left)


def pack_kernel(own, sent, received, out):
    gram = sent[CHUNKS * RANK :, :] + received[CHUNKS * RANK :, :]
    for chunk in range(CHUNKS):
        rows = slice(chunk * RANK, (chunk + 1) * RANK)
        out[chunk, :RANK] = own[rows, :] + received[rows, :]
        out[chunk, RANK:] = gram


def sum_kernel(parts, out):
    terms = [parts[i] for i in range(CHUNKS)]
    while len(terms) > 1:
        terms = [terms[i] + terms[i + 1] for i in range(0, len(terms), 2)]
    out[...] = terms[0]


def factor_kernel(summed, left, inverse, left_out):
    packed = summed[RANK:, :] * 0.25
    gram = jnp.concatenate([packed[:, q * RANK : (q + 1) * RANK] for q in range(4)], 0)
    row = lax.broadcasted_iota(jnp.int32, (RANK, RANK), 0)
    col = lax.broadcasted_iota(jnp.int32, (RANK, RANK), 1)
    work = jnp.concatenate([gram, jnp.where(row == col, 1.0, 0.0).astype(F32)], 1)
    group = 4
    done = []
    for base in range(0, RANK, group):
        top = (base // 8) * 8
        low = work[top - top :, :]
        cols = [jnp.broadcast_to(low[:, base + j : base + j + 1], low.shape) for j in range(group)]
        rows = [low[base - top + j : base - top + j + 1, :] for j in range(group)]
        cells = [[cols[j][base - top + i : base - top + i + 1, :] for j in range(i + 1)] for i in range(group)]
        inverses, ratios = [], {}
        reduced = {}
        for j in range(group):
            for i in range(j, group):
                value = cells[i][j]
                for m in range(j):
                    value = value - ratios[i, m] * reduced[j, m]
                reduced[i, j] = value
            inverses.append(1.0 / reduced[j, j])
            for i in range(j + 1, group):
                ratios[i, j] = reduced[i, j] * inverses[j]
        update = None
        for j in range(group):
            for m in range(j):
                rows[j] = rows[j] - ratios[j, m] * rows[m]
                cols[j] = cols[j] - ratios[j, m] * cols[m]
            term = cols[j] * (rows[j] * inverses[j])
            update = term if update is None else update + term
        for j in range(group):
            done.append(rows[j] * lax.rsqrt(reduced[j, j]))
        if base + group < RANK:
            work = low - update
            drop = ((base + group) // 8) * 8 - top
            work = work[drop:, :]
    inv = jnp.concatenate(done, 0)[:, RANK:]
    inverse[...] = inv
    left_out[...] = dot(inv, left[...], precision=lax.Precision.HIGHEST)


def spread_kernel(own, one, two, three, inverse, out):
    value = ((own[:RANK] + one[:RANK]) + (two[:RANK] + three[:RANK])) * (1.0 / 16.0)
    right = dot(inverse[...], value, precision=lax.Precision.HIGHEST)
    for chunk in range(CHUNKS):
        out[chunk] = right


STEP = 1024
PER = STEP // WIDE


def error_kernel(last, *refs):
    if last:
        merged, left, right, other, _, out, mine = refs
    else:
        merged, left, right, out = refs
    step = pl.program_id(0)
    flip = 1 if last else 0
    core = lax.axis_index("core") ^ flip
    high, low = split(left[...])
    lhs = jnp.concatenate([high, high, low], 0)
    for k in range(PER):
        chunk = step * PER + k
        top, bottom = split(right[chunk])
        approx = dot(lhs, jnp.concatenate([top, bottom, top], 0), ((0,), (0,)))
        start = pl.multiple_of(core * HALF + chunk * WIDE, WIDE)
        out[0, :, k * WIDE : (k + 1) * WIDE] = merged[:, pl.ds(start, WIDE)] - approx
    if last:
        block = lax.axis_index("x") * 4 + lax.axis_index("zhi") * 2 + lax.axis_index("core")
        first = 2 * (block % 8)
        here = block // 8 == core

        @pl.when((step == 0) & here)
        def _():
            mine[:, :WIDE] = right[first]
            mine[:, WIDE:] = right[first + 1]

        @pl.when((step == 0) & jnp.logical_not(here))
        def _():
            mine[:, :WIDE] = other[first]
            mine[:, WIDE:] = other[first + 1]


def error_part(merged, left, right, other=None, before=None):
    last = before is not None
    flip = 1 if last else 0
    out_spec = pl.BlockSpec(
        (1, ROWS, STEP), lambda i: (0, 0, (lax.axis_index("core") ^ flip) * (HALF // STEP) + i)
    )
    out_shape = [jax.ShapeDtypeStruct((1, ROWS, COLS), F32)]
    out_specs = [out_spec]
    args, in_specs, alias = [merged, left, right], [VMEM] * 3, {}
    if last:
        args += [other, before]
        in_specs += [VMEM, pl.BlockSpec(memory_space=pl.ANY)]
        out_shape.append(jax.ShapeDtypeStruct((RANK, BLOCK), F32))
        out_specs.append(VMEM)
        alias = {4: 0}
    return call(
        functools.partial(error_kernel, last),
        out_shape,
        grid=(HALF // STEP,),
        in_specs=in_specs,
        out_specs=out_specs,
        input_output_aliases=alias,
    )(*args)


def exchange(value):
    return lax.all_to_all(value, ("x", "y"), split_axis=0, concat_axis=0, tiled=True)


def body(gradient, error_feed, factor_old):
    with jax.named_scope("gather_factor"):
        own = factor_old.T
        pair = jnp.stack([own, shift(own, zlo=2, zhi=1)])
        held = [pair] + ring(pair, "x")
        other = [shift(part, core=1) for part in held]
    merged = gradient[0].astype(F32) + error_feed[0]
    with jax.named_scope("left_sum"):
        part = left_part([(0, 0), (0, 1)], merged, [held[0], other[0]])
        slots = [(s, c) for c in (0, 1) for s in (1, 2, 3)]
        part = left_part(slots, merged, held[1:] + other[1:], part)
        left_sum = total(total(part, "y"), "zlo")
    with jax.named_scope("right_sum"):
        sent = cross_part(1, True, merged, left_sum)
        received = shift(sent, core=1)
        kept = cross_part(0, False, merged, left_sum)
        packed = call(
            pack_kernel,
            jax.ShapeDtypeStruct((CHUNKS, RANK + EXTRA, WIDE), F32),
            in_specs=[VMEM] * 3,
            out_specs=VMEM,
        )(kept, sent, received)
        swapped = exchange(packed)
        summed = call(
            sum_kernel,
            jax.ShapeDtypeStruct((RANK + EXTRA, WIDE), F32),
            in_specs=[VMEM],
            out_specs=VMEM,
        )(swapped)
        summed = summed + shift(summed, zlo=2, zhi=1)
        one, two, three = ring(summed, "zlo")
    with jax.named_scope("cholesky"):
        inverse, left_turned = call(
            factor_kernel,
            [jax.ShapeDtypeStruct((RANK, RANK), F32), jax.ShapeDtypeStruct((RANK, ROWS), F32)],
            in_specs=[VMEM] * 2,
            out_specs=[VMEM] * 2,
        )(summed, left_sum)
    with jax.named_scope("right_factor"):
        spread = call(
            spread_kernel,
            jax.ShapeDtypeStruct((CHUNKS, RANK, WIDE), F32),
            in_specs=[VMEM] * 5,
            out_specs=VMEM,
        )(summed, one, two, three, inverse)
        right = exchange(spread)
        right_other = shift(right, core=1)
    with jax.named_scope("error"):
        (part,) = error_part(merged, left_turned, right)
        error_new, right_turned = error_part(merged, left_turned, right_other, right, part)
    return (error_new, left_turned.T, right_turned.T)


def solution(mesh):
    fine = Mesh(mesh.devices.reshape(SIZES), AXES)
    rows = ("x", "zhi", "core")
    return jax.shard_map(
        body,
        mesh=fine,
        in_specs=(P(("zlo", "y"), rows, None), P(("zlo", "y"), rows, None), P(rows, None)),
        out_specs=(P(("zlo", "y"), rows, None), P(rows, None), P(rows, None)),
        check_vma=False,
    )
```

time: 640 us -> 123 us (0.19); the launches traced: 631 us -> 123 us
  waiting for transfers between devices: 428 us -> 25.5 us
  blocking collectives: 152 us -> 42.1 us
  starting transfers between devices: 0.3 us -> 36.4 us
  matrix products: 22.2 us -> 0 us
  Pallas kernels: 0 us -> 13.1 us
  between operations: 13.8 us -> 0.75 us
  other arithmetic: 14 us -> 4.24 us
    psum x2 -> x0, waiting for transfers between devices: 357 us -> none  [body(): summed = lax.psum(lax.psum(term, 'tensor'), 'dp')]
    psum x2 -> x0, blocking collectives: 152 us -> none  [the longest x1 90.4 us: body(): gram = lax.psum(cross_product(left_sum, left_sum), 'tensor')]
    all_gather x1 -> x0, waiting for transfers between devices: 70 us -> none  [body(): lax.all_gather(factor_old, 'tensor', axis=0, tiled=True)]
    all_to_all x0 -> x2, blocking collectives: none -> 42.1 us  [exchange(): lax.all_to_all(value, ('x', 'y'), split_axis=0, concat_axis=0, tiled=True)]
    ppermute x0 -> x20, starting transfers between devices: none -> 36.4 us  [shift(): return lax.ppermute(value, AXES, pairs)]
    ppermute x0 -> x20, waiting for transfers between devices: none -> 25.5 us  [shift(): return lax.ppermute(value, AXES, pairs)]
    dot_general x4 -> x0, matrix products: 22 us -> none  [the longest x1 7.88 us: body(): jnp.dot(merged, lax.all_gather(factor_old, 'tensor', axis=0, tiled=True),...]
    pallas_call x0 -> x10, Pallas kernels: none -> 13.1 us  [the longest x2 7.04 us: error_part(): call(functools.partial(error_kernel, last), out_shape, grid=(HALF // STEP...]
  transfers between devices with their start and end apart: 3 -> 20, of which waited for: 3 -> 9; matrix products, arithmetic and copies ran while one was open for 0% -> 3% of each run, Pallas kernels for 0% -> 5%
where the time goes in v1:
time: 123 us
  blocking collectives  42.1 us (34%)
  starting transfers between devices  36.4 us (30%)
  waiting for transfers between devices  25.5 us (21%)
  Pallas kernels  13.1 us (11%)
  other arithmetic  4.24 us (3%)
    all_to_all x2, blocking collectives, exchange(): lax.all_to_all(value, ('x', 'y'), split_axis=0, concat_axis=0, tiled=True)  42.1 us
    ppermute x20, starting transfers between devices, shift(): return lax.ppermute(value, AXES, pairs)  36.4 us
    ppermute x20, waiting for transfers between devices, shift(): return lax.ppermute(value, AXES, pairs)  25.5 us
    pallas_call x2, Pallas kernels, error_part(): call(functools.partial(error_kernel, last), out_shape, grid=(HALF // STEP...  7.04 us
    add x1, other arithmetic, body(): merged = gradient[0].astype(F32) + error_feed[0]  3.28 us
    pallas_call x1, Pallas kernels, body(): call(factor_kernel, [jax.ShapeDtypeStruct((RANK, RANK), F32), jax.ShapeDt...  2.96 us
  transfers between devices with their start and end apart: 20, of which 9 were waited for; matrix products, arithmetic and copies ran while one was open for 3% of the time, Pallas kernels for 5%

profile of v1, /device:TPU:1, one launch (start us, length us, event | category | flops | bytes accessed | tf_op | source)
XLA Modules:
  0.0 122.8 jit_solution(8553016237674203294)
XLA Ops:
  0.6 6.9 %collective-permute-start = (f32[64,512]{1,0:T(8,128)}, f32[64,512]{1,0:T(8,128)S(1)}, u32[]{:S(2)}, u32[]{:S(2)}) collective-permute-start(f32[64,512]{1,0:T(8,128)} %bitcast.9), channel_id=1, source_target_pairs={{0,130},{1,131},{2,128},{3,129},{4,134},{5,135},{6,132},{7,133},{8... | collective-permute-start | bytes 393224 | tf_op jit(solution)/shard_map/gather_factor/ppermute | solution.py:26
  7.6 5.9 %collective-permute-done = f32[64,512]{1,0:T(8,128)S(1)} collective-permute-done((f32[64,512]{1,0:T(8,128)}, f32[64,512]{1,0:T(8,128)S(1)}, u32[]{:S(2)}, u32[]{:S(2)}) %collective-permute-start) | collective-permute-done | bytes 131104 | tf_op jit(solution)/shard_map/gather_factor/ppermute | solution.py:26
  13.4 0.9 pad_maximum_fusion.refs_1_
  14.4 2.6 %collective-permute-start.4 = (f32[2,64,512]{2,1,0:T(8,128)S(1)}, f32[2,64,512]{2,1,0:T(8,128)S(1)}, u32[]{:S(2)}, u32[]{:S(2)}) collective-permute-start(f32[2,64,512]{2,1,0:T(8,128)S(1)} %pad_maximum_fusion.refs_1_), channel_id=1, source_target_pairs={{0,12},{1,13},{2,14},{3,15},{4,8},{5,9},{6,10},{7,11},{8,4},{9,5},... | collective-permute-start | bytes 786440 | tf_op jit(solution)/shard_map/gather_factor/ppermute | solution.py:26
  17.7 1.8 %collective-permute-start.1 = (f32[2,64,512]{2,1,0:T(8,128)S(1)}, f32[2,64,512]{2,1,0:T(8,128)S(1)}, u32[]{:S(2)}, u32[]{:S(2)}) collective-permute-start(f32[2,64,512]{2,1,0:T(8,128)S(1)} %pad_maximum_fusion.refs_1_), channel_id=1, source_target_pairs={{0,1},{1,0},{2,3},{3,2},{4,5},{5,4},{6,7},{7,6},{8,9},{9,8},{10,11... | collective-permute-start | bytes 786440 | tf_op jit(solution)/shard_map/gather_factor/ppermute | solution.py:26
  19.5 8.5 %collective-permute-done.4.refs_4_ = f32[2,64,512]{2,1,0:T(8,128)S(1)} collective-permute-done((f32[2,64,512]{2,1,0:T(8,128)S(1)}, f32[2,64,512]{2,1,0:T(8,128)S(1)}, u32[]{:S(2)}, u32[]{:S(2)}) %collective-permute-start.4) | collective-permute-done | bytes 262176 | tf_op jit(solution)/shard_map/gather_factor/ppermute | solution.py:26
  28.0 2.0 %collective-permute-start.7 = (f32[2,64,512]{2,1,0:T(8,128)S(1)}, f32[2,64,512]{2,1,0:T(8,128)S(1)}, u32[]{:S(2)}, u32[]{:S(2)}) collective-permute-start(f32[2,64,512]{2,1,0:T(8,128)S(1)} %collective-permute-done.4.refs_4_), channel_id=1, source_target_pairs={{0,1},{1,0},{2,3},{3,2},{4,5},{5,4},{6,7},{7,6},{8,9},{9,8},{10,11... | collective-permute-start | bytes 786440 | tf_op jit(solution)/shard_map/gather_factor/ppermute | solution.py:26
  30.0 0.6 collective-permute-start.5
  30.6 3.3 %add_bitcast_fusion.refs_0_.merged = f32[128,8192]{1,0:T(8,128)S(1)} fusion(f32[1,128,8192]{2,1,0:T(8,128)} %param.4, bf16[1,128,8192]{2,1,0:T(8,128)(2,1)} %param.3), kind=kLoop, calls=%fused_computation | loop fusion | flops 2097152 | bytes 10485760 | tf_op jit(solution)/shard_map/add | solution.py:245
  34.5 1.1 left_sum.3
  35.5 2.8 %collective-permute-start.10 = (f32[64,128]{1,0:T(8,128)S(1)}, f32[64,128]{1,0:T(8,128)S(1)}, u32[]{:S(2)}, u32[]{:S(2)}) collective-permute-start(f32[64,128]{1,0:T(8,128)S(1)} %left_sum.3), channel_id=1, source_target_pairs={{0,48},{1,49},{2,50},{3,51},{4,52},{5,53},{6,54},{7,55},{8,56},{9,... | collective-permute-start | bytes 98312 | tf_op jit(solution)/shard_map/left_sum/ppermute | solution.py:26
  39.0 0.6 collective-permute-done.10
  39.7 3.0 %collective-permute-done.9 = f32[64,128]{1,0:T(8,128)S(1)} collective-permute-done((f32[64,128]{1,0:T(8,128)S(1)}, f32[64,128]{1,0:T(8,128)S(1)}, u32[]{:S(2)}, u32[]{:S(2)}) %collective-permute-start.9) | collective-permute-done | bytes 32800 | tf_op jit(solution)/shard_map/left_sum/ppermute | solution.py:26
  42.6 1.7 %collective-permute-start.13 = (f32[64,128]{1,0:T(8,128)S(1)}, f32[64,128]{1,0:T(8,128)S(1)}, u32[]{:S(2)}, u32[]{:S(2)}) collective-permute-start(f32[64,128]{1,0:T(8,128)S(1)} %add_add_fusion.1), channel_id=1, source_target_pairs={{0,192},{1,193},{2,194},{3,195},{4,196},{5,197},{6,198},{7,199},{8... | collective-permute-start | bytes 98312 | tf_op jit(solution)/shard_map/left_sum/ppermute | solution.py:26
  44.4 1.0 collective-permute-start.12
  45.3 0.9 collective-permute-start.11
  46.3 1.0 collective-permute-done.13
  47.3 1.1 collective-permute-done.12
  49.0 3.2 %collective-permute-start.14 = (f32[1040,256]{1,0:T(8,128)S(1)}, f32[1040,256]{1,0:T(8,128)S(1)}, u32[]{:S(2)}, u32[]{:S(2)}) collective-permute-start(f32[1040,256]{1,0:T(8,128)S(1)} %right_sum.5.sent), channel_id=1, source_target_pairs={{0,1},{1,0},{2,3},{3,2},{4,5},{5,4},{6,7},{7,6},{8,9},{9,8},{10,11... | collective-permute-start | bytes 3194888 | tf_op jit(solution)/shard_map/right_sum/ppermute | solution.py:26
  52.7 1.9 %collective-permute-done.14.received = f32[1040,256]{1,0:T(8,128)S(1)} collective-permute-done((f32[1040,256]{1,0:T(8,128)S(1)}, f32[1040,256]{1,0:T(8,128)S(1)}, u32[]{:S(2)}, u32[]{:S(2)}) %collective-permute-start.14) | collective-permute-done | bytes 1064992 | tf_op jit(solution)/shard_map/right_sum/ppermute | solution.py:26
  54.7 24.2 %all_to_all.10.parts = f32[16,80,256]{2,1,0:T(8,128)S(1)} all-to-all(f32[16,80,256]{2,1,0:T(8,128)S(1)} %right_sum.6), channel_id=1, replica_groups=mesh['zlo'=4,'y'=4,'x'=4,'zhi'=2,'core'=2] {'x','y'}, dimensions={0} | all-to-all | bytes 2621440 | tf_op jit(solution)/shard_map/right_sum/all_to_all | solution.py:236
  79.0 2.8 %collective-permute-start.15 = (f32[80,256]{1,0:T(8,128)S(1)}, f32[80,256]{1,0:T(8,128)S(1)}, u32[]{:S(2)}, u32[]{:S(2)}) collective-permute-start(f32[80,256]{1,0:T(8,128)S(1)} %right_sum.7), channel_id=1, source_target_pairs={{0,130},{1,131},{2,128},{3,129},{4,134},{5,135},{6,132},{7,133},{8... | collective-permute-start | bytes 245768 | tf_op jit(solution)/shard_map/right_sum/ppermute | solution.py:26
  81.7 2.8 %collective-permute-done.15 = f32[80,256]{1,0:T(8,128)S(1)} collective-permute-done((f32[80,256]{1,0:T(8,128)S(1)}, f32[80,256]{1,0:T(8,128)S(1)}, u32[]{:S(2)}, u32[]{:S(2)}) %collective-permute-start.15) | collective-permute-done | bytes 81952 | tf_op jit(solution)/shard_map/right_sum/ppermute | solution.py:26
  84.6 1.6 %collective-permute-start.18 = (f32[80,256]{1,0:T(8,128)S(1)}, f32[80,256]{1,0:T(8,128)S(1)}, u32[]{:S(2)}, u32[]{:S(2)}) collective-permute-start(f32[80,256]{1,0:T(8,128)S(1)} %add.34.summed.own), channel_id=1, source_target_pairs={{0,192},{1,193},{2,194},{3,195},{4,196},{5,197},{6,198},{7,199},{8... | collective-permute-start | bytes 245768 | tf_op jit(solution)/shard_map/right_sum/ppermute | solution.py:26
  86.2 1.3 %collective-permute-start.17 = (f32[80,256]{1,0:T(8,128)S(1)}, f32[80,256]{1,0:T(8,128)S(1)}, u32[]{:S(2)}, u32[]{:S(2)}) collective-permute-start(f32[80,256]{1,0:T(8,128)S(1)} %add.34.summed.own), channel_id=1, source_target_pairs={{0,128},{1,129},{2,130},{3,131},{4,132},{5,133},{6,134},{7,135},{8... | collective-permute-start | bytes 245768 | tf_op jit(solution)/shard_map/right_sum/ppermute | solution.py:26
  87.5 0.9 collective-permute-start.16
  88.4 3.0 %cholesky.1 = (f32[64,64]{1,0:T(8,128)S(1)}, f32[64,128]{1,0:T(8,128)}) custom-call(f32[80,256]{1,0:T(8,128)S(1)} %add.34.summed.own, f32[64,128]{1,0:T(8,128)S(1)} %add_add_fusion.left), custom_call_target="tpu_custom_call" | custom-call | tf_op jit(solution)/shard_map/cholesky/pallas_call | solution.py:271
  92.2 17.9 %all_to_all.11.refs_2_.refs_3_ = f32[16,64,256]{2,1,0:T(8,128)S(1)} all-to-all(f32[16,64,256]{2,1,0:T(8,128)S(1)} %right_factor.1), channel_id=1, replica_groups=mesh['zlo'=4,'y'=4,'x'=4,'zhi'=2,'core'=2] {'x','y'}, dimensions={0} | all-to-all | bytes 2097152 | tf_op jit(solution)/shard_map/right_factor/all_to_all | solution.py:236
  110.1 4.9 %collective-permute-start.19 = (f32[16,64,256]{2,1,0:T(8,128)S(1)}, f32[16,64,256]{2,1,0:T(8,128)S(1)}, u32[]{:S(2)}, u32[]{:S(2)}) collective-permute-start(f32[16,64,256]{2,1,0:T(8,128)S(1)} %all_to_all.11.refs_2_.refs_3_), channel_id=1, source_target_pairs={{0,1},{1,0},{2,3},{3,2},{4,5},{5,4},{6,7},{7,6},{8,9},{9,8},{10,11... | collective-permute-start | bytes 3145736 | tf_op jit(solution)/shard_map/right_factor/ppermute | solution.py:26
  115.0 0.8 copy-done.1
  115.8 2.4 %error.2.refs_4_ = f32[1,128,8192]{2,1,0:T(8,128)} custom-call(f32[128,8192]{1,0:T(8,128)S(1)} %add_bitcast_fusion.refs_0_.merged, f32[64,128]{1,0:T(8,128)S(1)} %copy-done.1, f32[16,64,256]{2,1,0:T(8,128)S(1)} %all_to_all.11.refs_2_.refs_3_), custom_call_target="tpu_custom_call" | custom-call | tf_op jit(solution)/shard_map/error/pallas_call | solution.py:225
  118.2 4.7 %error.3 = (f32[1,128,8192]{2,1,0:T(8,128)}, f32[64,512]{1,0:T(8,128)}) custom-call(f32[128,8192]{1,0:T(8,128)} %copy-done, f32[64,128]{1,0:T(8,128)S(1)} %copy-done.1, f32[16,64,256]{2,1,0:T(8,128)S(1)} %collective-permute-done.19.refs_2_, f32[16,64,256]{2,1,0:T(8,128)S(1)} %all_to_all.11.refs_2_.refs_3_, ...), custom_call_target="tpu_custom_call", output_to_operand_aliasing={{0}: (4, {})} | custom-call | tf_op jit(solution)/shard_map/error/pallas_call | solution.py:225
  (29 shorter events, 4.1 us)
Async XLA Ops:
  0.6 12.8 %collective-permute-start = (f32[64,512]{1,0:T(8,128)}, f32[64,512]{1,0:T(8,128)S(1)}, u32[]{:S(2)}, u32[]{:S(2)}) collective-permute-start(f32[64,512]{1,0:T(8,128)} %bitcast.9), channel_id=1, source_target_pairs={{0,130},{1,131},{2,128},{3,129},{4,134},{5,135},{6,132},{7,133},{8... | collective-permute-start | bytes 393224 | tf_op jit(solution)/shard_map/gather_factor/ppermute | solution.py:26
  14.4 13.7 %collective-permute-start.4 = (f32[2,64,512]{2,1,0:T(8,128)S(1)}, f32[2,64,512]{2,1,0:T(8,128)S(1)}, u32[]{:S(2)}, u32[]{:S(2)}) collective-permute-start(f32[2,64,512]{2,1,0:T(8,128)S(1)} %pad_maximum_fusion.refs_1_), channel_id=1, source_target_pairs={{0,12},{1,13},{2,14},{3,15},{4,8},{5,9},{6,10},{7,11},{8,4},{9,5},... | collective-permute-start | bytes 786440 | tf_op jit(solution)/shard_map/gather_factor/ppermute | solution.py:26
  16.9 13.1 %collective-permute-start.3 = (f32[2,64,512]{2,1,0:T(8,128)S(1)}, f32[2,64,512]{2,1,0:T(8,128)S(1)}, u32[]{:S(2)}, u32[]{:S(2)}) collective-permute-start(f32[2,64,512]{2,1,0:T(8,128)S(1)} %pad_maximum_fusion.refs_1_), channel_id=1, source_target_pairs={{0,8},{1,9},{2,10},{3,11},{4,12},{5,13},{6,14},{7,15},{8,0},{9,1},... | collective-permute-start | bytes 786440 | tf_op jit(solution)/shard_map/gather_factor/ppermute | solution.py:26
  17.4 12.6 %collective-permute-start.2 = (f32[2,64,512]{2,1,0:T(8,128)S(1)}, f32[2,64,512]{2,1,0:T(8,128)S(1)}, u32[]{:S(2)}, u32[]{:S(2)}) collective-permute-start(f32[2,64,512]{2,1,0:T(8,128)S(1)} %pad_maximum_fusion.refs_1_), channel_id=1, source_target_pairs={{0,4},{1,5},{2,6},{3,7},{4,0},{5,1},{6,2},{7,3},{8,12},{9,13},{10,... | collective-permute-start | bytes 786440 | tf_op jit(solution)/shard_map/gather_factor/ppermute | solution.py:26
  17.7 16.2 %collective-permute-start.1 = (f32[2,64,512]{2,1,0:T(8,128)S(1)}, f32[2,64,512]{2,1,0:T(8,128)S(1)}, u32[]{:S(2)}, u32[]{:S(2)}) collective-permute-start(f32[2,64,512]{2,1,0:T(8,128)S(1)} %pad_maximum_fusion.refs_1_), channel_id=1, source_target_pairs={{0,1},{1,0},{2,3},{3,2},{4,5},{5,4},{6,7},{7,6},{8,9},{9,8},{10,11... | collective-permute-start | bytes 786440 | tf_op jit(solution)/shard_map/gather_factor/ppermute | solution.py:26
  28.0 6.4 %collective-permute-start.7 = (f32[2,64,512]{2,1,0:T(8,128)S(1)}, f32[2,64,512]{2,1,0:T(8,128)S(1)}, u32[]{:S(2)}, u32[]{:S(2)}) collective-permute-start(f32[2,64,512]{2,1,0:T(8,128)S(1)} %collective-permute-done.4.refs_4_), channel_id=1, source_target_pairs={{0,1},{1,0},{2,3},{3,2},{4,5},{5,4},{6,7},{7,6},{8,9},{9,8},{10,11... | collective-permute-start | bytes 786440 | tf_op jit(solution)/shard_map/gather_factor/ppermute | solution.py:26
  30.0 4.5 %collective-permute-start.6 = (f32[2,64,512]{2,1,0:T(8,128)S(1)}, f32[2,64,512]{2,1,0:T(8,128)S(1)}, u32[]{:S(2)}, u32[]{:S(2)}) collective-permute-start(f32[2,64,512]{2,1,0:T(8,128)S(1)} %collective-permute-done.3.refs_3_), channel_id=1, source_target_pairs={{0,1},{1,0},{2,3},{3,2},{4,5},{5,4},{6,7},{7,6},{8,9},{9,8},{10,11... | collective-permute-start | bytes 786440 | tf_op jit(solution)/shard_map/gather_factor/ppermute | solution.py:26
  30.0 4.5 %collective-permute-start.5 = (f32[2,64,512]{2,1,0:T(8,128)S(1)}, f32[2,64,512]{2,1,0:T(8,128)S(1)}, u32[]{:S(2)}, u32[]{:S(2)}) collective-permute-start(f32[2,64,512]{2,1,0:T(8,128)S(1)} %collective-permute-done.2.refs_2_), channel_id=1, source_target_pairs={{0,1},{1,0},{2,3},{3,2},{4,5},{5,4},{6,7},{7,6},{8,9},{9,8},{10,11... | collective-permute-start | bytes 786440 | tf_op jit(solution)/shard_map/gather_factor/ppermute | solution.py:26
  33.9 81.1 %copy-start = (f32[128,8192]{1,0:T(8,128)}, f32[128,8192]{1,0:T(8,128)S(1)}, u32[]{:S(2)}) copy-start(f32[128,8192]{1,0:T(8,128)S(1)} %add_bitcast_fusion.refs_0_.merged) | copy-start | bytes 12582916
  35.5 4.1 %collective-permute-start.10 = (f32[64,128]{1,0:T(8,128)S(1)}, f32[64,128]{1,0:T(8,128)S(1)}, u32[]{:S(2)}, u32[]{:S(2)}) collective-permute-start(f32[64,128]{1,0:T(8,128)S(1)} %left_sum.3), channel_id=1, source_target_pairs={{0,48},{1,49},{2,50},{3,51},{4,52},{5,53},{6,54},{7,55},{8,56},{9,... | collective-permute-start | bytes 98312 | tf_op jit(solution)/shard_map/left_sum/ppermute | solution.py:26
  38.4 4.3 %collective-permute-start.9 = (f32[64,128]{1,0:T(8,128)S(1)}, f32[64,128]{1,0:T(8,128)S(1)}, u32[]{:S(2)}, u32[]{:S(2)}) collective-permute-start(f32[64,128]{1,0:T(8,128)S(1)} %left_sum.3), channel_id=1, source_target_pairs={{0,32},{1,33},{2,34},{3,35},{4,36},{5,37},{6,38},{7,39},{8,40},{9,... | collective-permute-start | bytes 98312 | tf_op jit(solution)/shard_map/left_sum/ppermute | solution.py:26
  38.7 3.9 %collective-permute-start.8 = (f32[64,128]{1,0:T(8,128)S(1)}, f32[64,128]{1,0:T(8,128)S(1)}, u32[]{:S(2)}, u32[]{:S(2)}) collective-permute-start(f32[64,128]{1,0:T(8,128)S(1)} %left_sum.3), channel_id=1, source_target_pairs={{0,16},{1,17},{2,18},{3,19},{4,20},{5,21},{6,22},{7,23},{8,24},{9,... | collective-permute-start | bytes 98312 | tf_op jit(solution)/shard_map/left_sum/ppermute | solution.py:26
  42.6 4.7 %collective-permute-start.13 = (f32[64,128]{1,0:T(8,128)S(1)}, f32[64,128]{1,0:T(8,128)S(1)}, u32[]{:S(2)}, u32[]{:S(2)}) collective-permute-start(f32[64,128]{1,0:T(8,128)S(1)} %add_add_fusion.1), channel_id=1, source_target_pairs={{0,192},{1,193},{2,194},{3,195},{4,196},{5,197},{6,198},{7,199},{8... | collective-permute-start | bytes 98312 | tf_op jit(solution)/shard_map/left_sum/ppermute | solution.py:26
  44.4 4.1 %collective-permute-start.12 = (f32[64,128]{1,0:T(8,128)S(1)}, f32[64,128]{1,0:T(8,128)S(1)}, u32[]{:S(2)}, u32[]{:S(2)}) collective-permute-start(f32[64,128]{1,0:T(8,128)S(1)} %add_add_fusion.1), channel_id=1, source_target_pairs={{0,128},{1,129},{2,130},{3,131},{4,132},{5,133},{6,134},{7,135},{8... | collective-permute-start | bytes 98312 | tf_op jit(solution)/shard_map/left_sum/ppermute | solution.py:26
  45.3 3.1 %collective-permute-start.11 = (f32[64,128]{1,0:T(8,128)S(1)}, f32[64,128]{1,0:T(8,128)S(1)}, u32[]{:S(2)}, u32[]{:S(2)}) collective-permute-start(f32[64,128]{1,0:T(8,128)S(1)} %add_add_fusion.1), channel_id=1, source_target_pairs={{0,64},{1,65},{2,66},{3,67},{4,68},{5,69},{6,70},{7,71},{8,72},{9,... | collective-permute-start | bytes 98312 | tf_op jit(solution)/shard_map/left_sum/ppermute | solution.py:26
  49.0 5.5 %collective-permute-start.14 = (f32[1040,256]{1,0:T(8,128)S(1)}, f32[1040,256]{1,0:T(8,128)S(1)}, u32[]{:S(2)}, u32[]{:S(2)}) collective-permute-start(f32[1040,256]{1,0:T(8,128)S(1)} %right_sum.5.sent), channel_id=1, source_target_pairs={{0,1},{1,0},{2,3},{3,2},{4,5},{5,4},{6,7},{7,6},{8,9},{9,8},{10,11... | collective-permute-start | bytes 3194888 | tf_op jit(solution)/shard_map/right_sum/ppermute | solution.py:26
  79.0 5.6 %collective-permute-start.15 = (f32[80,256]{1,0:T(8,128)S(1)}, f32[80,256]{1,0:T(8,128)S(1)}, u32[]{:S(2)}, u32[]{:S(2)}) collective-permute-start(f32[80,256]{1,0:T(8,128)S(1)} %right_sum.7), channel_id=1, source_target_pairs={{0,130},{1,131},{2,128},{3,129},{4,134},{5,135},{6,132},{7,133},{8... | collective-permute-start | bytes 245768 | tf_op jit(solution)/shard_map/right_sum/ppermute | solution.py:26
  84.6 6.8 %collective-permute-start.18 = (f32[80,256]{1,0:T(8,128)S(1)}, f32[80,256]{1,0:T(8,128)S(1)}, u32[]{:S(2)}, u32[]{:S(2)}) collective-permute-start(f32[80,256]{1,0:T(8,128)S(1)} %add.34.summed.own), channel_id=1, source_target_pairs={{0,192},{1,193},{2,194},{3,195},{4,196},{5,197},{6,198},{7,199},{8... | collective-permute-start | bytes 245768 | tf_op jit(solution)/shard_map/right_sum/ppermute | solution.py:26
  86.2 5.8 %collective-permute-start.17 = (f32[80,256]{1,0:T(8,128)S(1)}, f32[80,256]{1,0:T(8,128)S(1)}, u32[]{:S(2)}, u32[]{:S(2)}) collective-permute-start(f32[80,256]{1,0:T(8,128)S(1)} %add.34.summed.own), channel_id=1, source_target_pairs={{0,128},{1,129},{2,130},{3,131},{4,132},{5,133},{6,134},{7,135},{8... | collective-permute-start | bytes 245768 | tf_op jit(solution)/shard_map/right_sum/ppermute | solution.py:26
  87.5 4.5 %collective-permute-start.16 = (f32[80,256]{1,0:T(8,128)S(1)}, f32[80,256]{1,0:T(8,128)S(1)}, u32[]{:S(2)}, u32[]{:S(2)}) collective-permute-start(f32[80,256]{1,0:T(8,128)S(1)} %add.34.summed.own), channel_id=1, source_target_pairs={{0,64},{1,65},{2,66},{3,67},{4,68},{5,69},{6,70},{7,71},{8,72},{9,... | collective-permute-start | bytes 245768 | tf_op jit(solution)/shard_map/right_sum/ppermute | solution.py:26
  110.1 8.0 %collective-permute-start.19 = (f32[16,64,256]{2,1,0:T(8,128)S(1)}, f32[16,64,256]{2,1,0:T(8,128)S(1)}, u32[]{:S(2)}, u32[]{:S(2)}) collective-permute-start(f32[16,64,256]{2,1,0:T(8,128)S(1)} %all_to_all.11.refs_2_.refs_3_), channel_id=1, source_target_pairs={{0,1},{1,0},{2,3},{3,2},{4,5},{5,4},{6,7},{7,6},{8,9},{9,8},{10,11... | collective-permute-start | bytes 3145736 | tf_op jit(solution)/shard_map/right_factor/ppermute | solution.py:26
  115.0 0.8 copy-start.1

commit v2 on v1

v2 whole, which is shorter than its diff:
```python
import functools

import jax
import jax.numpy as jnp
import numpy as np
from jax import lax
from jax.experimental import pallas as pl
from jax.experimental.pallas import tpu as pltpu
from jax.sharding import Mesh, PartitionSpec as P

AXES = ("zlo", "y", "x", "zhi", "core")
SIZES = (4, 4, 4, 2, 2)
ROWS, COLS, RANK, BLOCK = 128, 8192, 64, 512
HALF = COLS // 2
WIDE, LANES, EXTRA, RING = 256, 128, 16, 4
STEPS = (1, 3, 2)
PACKED = (2, 3, 1)
TALL, GRAM = RING * RANK, 2 * EXTRA
CHUNKS = HALF // WIDE
LIMIT = 8 * 1024 * 1024
F32, BF16 = jnp.float32, jnp.bfloat16
VMEM = pl.BlockSpec(memory_space=pltpu.VMEM)


def shift(value, zlo=0, y=0, x=0, zhi=0, core=0):
    pairs = []
    for source in np.ndindex(*SIZES):
        target = tuple(a ^ b for a, b in zip(source, (zlo, y, x, zhi, core)))
        pairs.append((int(np.ravel_multi_index(source, SIZES)), int(np.ravel_multi_index(target, SIZES))))
    return lax.ppermute(value, AXES, pairs)


def ring(value, axis):
    return [shift(value, **{axis: step}) for step in STEPS]


def total(value, axis):
    one, three, two = ring(value, axis)
    return (value + one) + (three + two)


def split(value):
    high = value.astype(BF16)
    return high, (value - high.astype(F32)).astype(BF16)


def dot(left, right, contract=((1,), (0,)), precision=None):
    return lax.dot_general(left, right, (contract, ((), ())), precision=precision, preferred_element_type=F32)


def call(kernel, out_shape, **kw):
    return pl.pallas_call(
        kernel,
        out_shape=out_shape,
        compiler_params=pltpu.CompilerParams(vmem_limit_bytes=LIMIT),
        **kw,
    )


def left_kernel(slots, first, *refs):
    merged, out = refs[-2:]
    factors = refs[:-2] if first else refs[1:-2]
    x, zhi, core = lax.axis_index("x"), lax.axis_index("zhi"), lax.axis_index("core")
    acc = jnp.zeros((2 * ROWS, 2 * RANK), F32)
    for (sx, sh, sc), factor in zip(slots, factors):
        block = (x ^ sx) * 4 + (zhi ^ sh) * 2 + (core ^ sc)
        part = merged[:, pl.ds(pl.multiple_of(block * BLOCK, BLOCK), BLOCK)]
        rows = jnp.concatenate(split(part), 0)
        cols = jnp.concatenate(split(factor[...]), 0)
        acc = acc + dot(rows, cols, ((1,), (1,)))
    both = acc[:ROWS] + acc[ROWS:]
    turned = both.T
    result = turned[:RANK] + turned[RANK:]
    out[...] = result if first else refs[0][...] + result


def left_part(slots, merged, factors, before=None):
    first = before is None
    args = ([] if first else [before]) + list(factors) + [merged]
    return call(
        functools.partial(left_kernel, slots, first),
        jax.ShapeDtypeStruct((RANK, ROWS), F32),
        in_specs=[VMEM] * len(args),
        out_specs=VMEM,
    )(*args)


def column(half, chunk):
    return pl.multiple_of(half * HALF + chunk * WIDE, WIDE)


def cross_kernel(flip, merged, left, by_x, by_y):
    half = lax.axis_index("core") ^ flip
    x, y = lax.axis_index("x"), lax.axis_index("y")
    high, low = split(left[...])
    lhs = jnp.concatenate([jnp.concatenate([high, high], 1), jnp.concatenate([low, low], 1)], 0)
    gram = dot(left[...], left[...], ((1,), (1,)), lax.Precision.HIGHEST)
    flat = jnp.concatenate([gram[:GRAM], gram[GRAM:]], 1)
    for sx in range(RING):
        for sy in range(RING):
            start = column(half, (x ^ sx) * RING + (y ^ sy))
            rhs = jnp.concatenate(split(merged[:, pl.ds(start, WIDE)]), 0)
            both = dot(lhs, rhs)
            both = both[:RANK] + both[RANK:]
            by_x[sx, sy * RANK : (sy + 1) * RANK] = both[:, :LANES]
            by_y[sy, sx * RANK : (sx + 1) * RANK] = both[:, LANES:]
        by_x[sx, TALL:] = flat


def cross_part(flip, merged, left):
    return call(
        functools.partial(cross_kernel, flip),
        [
            jax.ShapeDtypeStruct((RING, TALL + GRAM, LANES), F32),
            jax.ShapeDtypeStruct((RING, TALL, LANES), F32),
        ],
        in_specs=[VMEM] * 2,
        out_specs=[VMEM] * 2,
    )(merged, left)


def pack_kernel(own, received, *outs):
    for step, out in zip((0,) + PACKED, outs):
        out[...] = own[step] + received[step]


def scatter_kernel(own, two, three, one, *outs):
    def summed(rows):
        return (own[rows] + one[rows]) + (three[rows] + two[rows])

    for step, out in zip((0,) + PACKED, outs):
        out[...] = summed(slice(step * RANK, (step + 1) * RANK))
    if len(outs) > RING:
        outs[RING][...] = summed(slice(TALL, TALL + GRAM))


def join_kernel(own_a, two_a, three_a, one_a, own_b, two_b, three_b, one_b, gram, out):
    out[:RANK, :LANES] = (own_a[...] + one_a[...]) + (three_a[...] + two_a[...])
    out[:RANK, LANES:] = (own_b[...] + one_b[...]) + (three_b[...] + two_b[...])
    out[RANK:, :LANES] = gram[:EXTRA]
    out[RANK:, LANES:] = gram[EXTRA:]


def pair_kernel(own, other, out, gram):
    out[...] = own[:RANK] + other[:RANK]
    gram[...] = own[RANK:] + other[RANK:]


def factor_kernel(packed, left, inverse, left_out, wide_out):
    flat = jnp.concatenate([packed[:, :LANES], packed[:, LANES:]], 0)
    gram = jnp.concatenate([flat[:, :RANK], flat[:, RANK:]], 0)
    row = lax.broadcasted_iota(jnp.int32, (RANK, RANK), 0)
    col = lax.broadcasted_iota(jnp.int32, (RANK, RANK), 1)
    work = jnp.concatenate([gram, jnp.where(row == col, 1.0, 0.0).astype(F32)], 1)
    group = 4
    done = []
    for base in range(0, RANK, group):
        top = (base // 8) * 8
        low = work[top - top :, :]
        cols = [jnp.broadcast_to(low[:, base + j : base + j + 1], low.shape) for j in range(group)]
        rows = [low[base - top + j : base - top + j + 1, :] for j in range(group)]
        cells = [[cols[j][base - top + i : base - top + i + 1, :] for j in range(i + 1)] for i in range(group)]
        inverses, ratios = [], {}
        reduced = {}
        for j in range(group):
            for i in range(j, group):
                value = cells[i][j]
                for m in range(j):
                    value = value - ratios[i, m] * reduced[j, m]
                reduced[i, j] = value
            inverses.append(1.0 / reduced[j, j])
            for i in range(j + 1, group):
                ratios[i, j] = reduced[i, j] * inverses[j]
        update = None
        for j in range(group):
            for m in range(j):
                rows[j] = rows[j] - ratios[j, m] * rows[m]
                cols[j] = cols[j] - ratios[j, m] * cols[m]
            term = cols[j] * (rows[j] * inverses[j])
            update = term if update is None else update + term
        for j in range(group):
            done.append(rows[j] * lax.rsqrt(reduced[j, j]))
        if base + group < RANK:
            work = low - update
            drop = ((base + group) // 8) * 8 - top
            work = work[drop:, :]
    inv = jnp.concatenate(done, 0)[:, RANK:]
    inverse[...] = inv
    turned = dot(inv, left[...], precision=lax.Precision.HIGHEST)
    left_out[...] = turned
    high, low = split(turned.T)
    wide_out[...] = jnp.concatenate([high, high, low], 1)


def spread_kernel(own, one, three, two, inverse, out):
    value = ((own[...] + one[...]) + (three[...] + two[...])) * (1.0 / 16.0)
    right = dot(inverse[...], value, precision=lax.Precision.HIGHEST)
    for chunk in range(CHUNKS):
        out[chunk] = right


def error_kernel(last, *refs):
    refs = list(refs)
    before = refs.pop(0) if last else None
    merged, left, right = refs[:3]
    out, buffer, sems = refs[3 + last], refs[-2], refs[-1]
    half = lax.axis_index("core") ^ last
    copies = []
    if last:
        other, mine = refs[3], refs[5]
        block = lax.axis_index("x") * 4 + lax.axis_index("zhi") * 2 + lax.axis_index("core")
        here = block // 8 == half
        own_copies = [[], []]
        for source, into in zip((right, other), own_copies):
            for k in range(2):
                into.append(
                    pltpu.make_async_copy(
                        source.at[2 * (block % 8) + k],
                        mine.at[:, pl.ds(k * WIDE, WIDE)],
                        sems.at[CHUNKS + k],
                    )
                )

        @pl.when(here)
        def _():
            for copy in own_copies[0]:
                copy.start()

        @pl.when(jnp.logical_not(here))
        def _():
            for copy in own_copies[1]:
                copy.start()

    for chunk in range(CHUNKS):
        top, bottom = split(right[chunk])
        approx = dot(left[...], jnp.concatenate([top, bottom, top], 0))
        start = column(half, chunk)
        buffer[chunk] = merged[:, pl.ds(start, WIDE)] - approx
        copy = pltpu.make_async_copy(buffer.at[chunk], out.at[0, :, pl.ds(start, WIDE)], sems.at[chunk])
        copy.start()
        copies.append(copy)
    for copy in copies:
        copy.wait()
    if last:

        @pl.when(here)
        def _():
            for copy in own_copies[0]:
                copy.wait()

        @pl.when(jnp.logical_not(here))
        def _():
            for copy in own_copies[1]:
                copy.wait()


def error_part(merged, left, right, other=None, before=None):
    last = before is not None
    anywhere = pl.BlockSpec(memory_space=pl.ANY)
    args = ([before] if last else []) + [merged, left, right] + ([other] if last else [])
    out_shape = [jax.ShapeDtypeStruct((1, ROWS, COLS), F32)]
    if last:
        out_shape.append(jax.ShapeDtypeStruct((RANK, BLOCK), F32))
    return call(
        functools.partial(error_kernel, int(last)),
        out_shape,
        in_specs=([anywhere] if last else []) + [VMEM] * (4 if last else 3),
        out_specs=[anywhere] * len(out_shape),
        scratch_shapes=[pltpu.VMEM((CHUNKS, ROWS, WIDE), F32), pltpu.SemaphoreType.DMA((CHUNKS + 2,))],
        input_output_aliases={0: 0} if last else {},
    )(*args)


def exchange(value):
    return lax.all_to_all(value, ("x", "y"), split_axis=0, concat_axis=0, tiled=True)


def simple(kernel, shapes, *args):
    many = isinstance(shapes, list)
    structs = [jax.ShapeDtypeStruct(shape, F32) for shape in (shapes if many else [shapes])]
    specs = [VMEM] * len(structs)
    return call(
        kernel,
        structs if many else structs[0],
        in_specs=[VMEM] * len(args),
        out_specs=specs if many else VMEM,
    )(*args)


def body(gradient, error_feed, factor_old):
    merged = gradient[0].astype(F32) + error_feed[0]
    with jax.named_scope("gather_factor"):
        own = factor_old.T
        near = ring(own, "x")
        far = shift(own, zlo=2, zhi=1)
        far, _ = lax.optimization_barrier((far, merged))
        second = ring(far, "x")
        near[0], near[1], near[2], second[2] = lax.optimization_barrier((*near, second[2]))
    with jax.named_scope("left_sum"):
        held = near + [own] + [shift(value, core=1) for value in [own] + near] + [far, shift(far, core=1)]
        slots = [(s, 0, 0) for s in STEPS] + [(0, 0, 0), (0, 0, 1)] + [(s, 0, 1) for s in STEPS]
        part = left_part(slots + [(0, 1, 0), (0, 1, 1)], merged, held)
        held = second + [shift(value, core=1) for value in second]
        part = left_part([(s, 1, c) for c in (0, 1) for s in STEPS], merged, held, part)
        left_sum = total(total(part, "y"), "zlo")
    with jax.named_scope("right_sum"):
        sent = cross_part(1, merged, left_sum)
        received = [shift(value, core=1) for value in sent]
        kept = cross_part(0, merged, left_sum)
        axes, groups = ("x", "y"), []
        for axis, own, other, height in zip(axes, kept, received, (TALL + GRAM, TALL)):
            own, *outgoing = simple(pack_kernel, [(height, LANES)] * RING, own, other)
            groups.append([own] + [shift(v, **{axis: step}) for step, v in zip(PACKED, outgoing)])
        *part_a, gram = simple(scatter_kernel, [(RANK, LANES)] * RING + [(GRAM, LANES)], *groups[0])
        part_b = simple(scatter_kernel, [(RANK, LANES)] * RING, *groups[1])
        parts = []
        for axis, (own, *outgoing) in zip(("y", "x"), (part_a, part_b)):
            parts += [own] + [shift(v, **{axis: step}) for step, v in zip(PACKED, outgoing)]
        joined = simple(join_kernel, (RANK + EXTRA, WIDE), *parts, gram)
        other = shift(joined, zlo=2, zhi=1)
        summed, gram = simple(pair_kernel, [(RANK, WIDE), (EXTRA, WIDE)], joined, other)
        others = ring(summed, "zlo")
    with jax.named_scope("cholesky"):
        inverse, left_turned, left_wide = call(
            factor_kernel,
            [
                jax.ShapeDtypeStruct((RANK, RANK), F32),
                jax.ShapeDtypeStruct((RANK, ROWS), F32),
                jax.ShapeDtypeStruct((ROWS, 3 * RANK), BF16),
            ],
            in_specs=[VMEM] * 2,
            out_specs=[VMEM] * 3,
        )(gram, left_sum)
    with jax.named_scope("right_factor"):
        right = exchange(simple(spread_kernel, (CHUNKS, RANK, WIDE), summed, *others, inverse))
        right_other = shift(right, core=1)
    with jax.named_scope("error"):
        (part,) = error_part(merged, left_wide, right)
        error_new, right_turned = error_part(merged, left_wide, right_other, right, part)
    return (error_new, left_turned.T, right_turned.T)


def solution(mesh):
    fine = Mesh(mesh.devices.reshape(SIZES), AXES)
    rows = ("x", "zhi", "core")
    return jax.shard_map(
        body,
        mesh=fine,
        in_specs=(P(("zlo", "y"), rows, None), P(("zlo", "y"), rows, None), P(rows, None)),
        out_specs=(P(("zlo", "y"), rows, None), P(rows, None), P(rows, None)),
        check_vma=False,
    )
```

time: 123 us -> 106 us (0.86)
  blocking collectives: 42.1 us -> 15.6 us
  starting transfers between devices: 36.4 us -> 51.6 us
  Pallas kernels: 13.1 us -> 9.4 us
    all_to_all x2 -> x1, blocking collectives: 42.1 us -> 15.6 us  [exchange(): lax.all_to_all(value, ('x', 'y'), split_axis=0, concat_axis=0, tiled=True)]
    ppermute x20 -> x40, starting transfers between devices: 36.4 us -> 51.6 us  [shift(): return lax.ppermute(value, AXES, pairs)]
    pallas_call x7 -> x11, Pallas kernels: 8.54 us -> 4.81 us  [the longest x2 3.32 us: error_part(): call(functools.partial(error_kernel, int(last)), out_shape, in_specs=([an...]
    ppermute x20 -> x40, waiting for transfers between devices: 25.5 us -> 25 us  [shift(): return lax.ppermute(value, AXES, pairs)]
  transfers between devices with their start and end apart: 20 -> 40, of which waited for: 9 -> 16; matrix products, arithmetic and copies ran while one was open for 3% -> 3% of each run, Pallas kernels for 5% -> 6%
where the time goes in v2:
time: 106 us
  starting transfers between devices  51.6 us (49%)
  waiting for transfers between devices  25 us (24%)
  blocking collectives  15.6 us (15%)
  Pallas kernels  9.4 us (9%)
  other arithmetic  3.28 us (3%)
    ppermute x40, starting transfers between devices, shift(): return lax.ppermute(value, AXES, pairs)  51.6 us
    ppermute x40, waiting for transfers between devices, shift(): return lax.ppermute(value, AXES, pairs)  25 us
    all_to_all x1, blocking collectives, exchange(): lax.all_to_all(value, ('x', 'y'), split_axis=0, concat_axis=0, tiled=True)  15.6 us
    pallas_call x2, Pallas kernels, error_part(): call(functools.partial(error_kernel, int(last)), out_shape, in_specs=([an...  3.32 us
    add x1, other arithmetic, body(): merged = gradient[0].astype(F32) + error_feed[0]  3.26 us
    pallas_call x1, Pallas kernels, body(): call(factor_kernel, [jax.ShapeDtypeStruct((RANK, RANK), F32), jax.ShapeDt...  2.99 us
  transfers between devices with their start and end apart: 40, of which 16 were waited for; matrix products, arithmetic and copies ran while one was open for 3% of the time, Pallas kernels for 6%

profile of v2, /device:TPU:1, one launch (start us, length us, event | category | flops | bytes accessed | tf_op | source)
XLA Modules:
  0.0 105.8 jit_solution(4185289172203995906)
XLA Ops:
  0.6 6.9 %collective-permute-start.3 = (f32[64,512]{1,0:T(8,128)}, f32[64,512]{1,0:T(8,128)S(1)}, u32[]{:S(2)}, u32[]{:S(2)}) collective-permute-start(f32[64,512]{1,0:T(8,128)} %bitcast.5), channel_id=1, source_target_pairs={{0,130},{1,131},{2,128},{3,129},{4,134},{5,135},{6,132},{7,133},{8... | collective-permute-start | bytes 393224 | tf_op jit(solution)/shard_map/gather_factor/ppermute | solution.py:30
  7.6 2.7 %collective-permute-start.2 = (f32[64,512]{1,0:T(8,128)}, f32[64,512]{1,0:T(8,128)S(1)}, u32[]{:S(2)}, u32[]{:S(2)}) collective-permute-start(f32[64,512]{1,0:T(8,128)} %bitcast.6), channel_id=1, source_target_pairs={{0,8},{1,9},{2,10},{3,11},{4,12},{5,13},{6,14},{7,15},{8,0},{9,1},... | collective-permute-start | bytes 393224 | tf_op jit(solution)/shard_map/gather_factor/ppermute | solution.py:30
  11.2 3.3 %add_bitcast_fusion.refs_10_.refs_7_.merged.refs_0_.refs_1_ = f32[128,8192]{1,0:T(8,128)S(1)} fusion(f32[1,128,8192]{2,1,0:T(8,128)} %param.4, bf16[1,128,8192]{2,1,0:T(8,128)(2,1)} %param.3), kind=kLoop, calls=%fused_computation | loop fusion | flops 2097152 | bytes 10485760 | tf_op jit(solution)/shard_map/add | solution.py:291
  14.5 3.1 %collective-permute-start.4 = (f32[64,512]{1,0:T(8,128)S(1)}, f32[64,512]{1,0:T(8,128)S(1)}, u32[]{:S(2)}, u32[]{:S(2)}) collective-permute-start(f32[64,512]{1,0:T(8,128)S(1)} %collective-permute-done.3.refs_8_), channel_id=1, source_target_pairs={{0,8},{1,9},{2,10},{3,11},{4,12},{5,13},{6,14},{7,15},{8,0},{9,1},... | collective-permute-start | bytes 393224 | tf_op jit(solution)/shard_map/gather_factor/ppermute | solution.py:30
  17.6 2.1 %collective-permute-start.5 = (f32[64,512]{1,0:T(8,128)S(1)}, f32[64,512]{1,0:T(8,128)S(1)}, u32[]{:S(2)}, u32[]{:S(2)}) collective-permute-start(f32[64,512]{1,0:T(8,128)S(1)} %bitcast.9), channel_id=1, source_target_pairs={{0,1},{1,0},{2,3},{3,2},{4,5},{5,4},{6,7},{7,6},{8,9},{9,8},{10,11... | collective-permute-start | bytes 393224 | tf_op jit(solution)/shard_map/left_sum/ppermute | solution.py:30
  21.0 1.9 %collective-permute-start.6 = (f32[64,512]{1,0:T(8,128)S(1)}, f32[64,512]{1,0:T(8,128)S(1)}, u32[]{:S(2)}, u32[]{:S(2)}) collective-permute-start(f32[64,512]{1,0:T(8,128)S(1)} %collective-permute-done.refs_0_), channel_id=1, source_target_pairs={{0,1},{1,0},{2,3},{3,2},{4,5},{5,4},{6,7},{7,6},{8,9},{9,8},{10,11... | collective-permute-start | bytes 393224 | tf_op jit(solution)/shard_map/left_sum/ppermute | solution.py:30
  22.9 3.0 %collective-permute-done.11.refs_2_ = f32[64,512]{1,0:T(8,128)S(1)} collective-permute-done((f32[64,512]{1,0:T(8,128)S(1)}, f32[64,512]{1,0:T(8,128)S(1)}, u32[]{:S(2)}, u32[]{:S(2)}) %collective-permute-start.11) | collective-permute-done | bytes 131104 | tf_op jit(solution)/shard_map/gather_factor/ppermute | solution.py:30
  27.8 0.9 left_sum.2.refs_0_
  29.4 3.0 %collective-permute-start.17 = (f32[64,128]{1,0:T(8,128)S(1)}, f32[64,128]{1,0:T(8,128)S(1)}, u32[]{:S(2)}, u32[]{:S(2)}) collective-permute-start(f32[64,128]{1,0:T(8,128)S(1)} %left_sum.3), channel_id=1, source_target_pairs={{0,32},{1,33},{2,34},{3,35},{4,36},{5,37},{6,38},{7,39},{8,40},{9,... | collective-permute-start | bytes 98312 | tf_op jit(solution)/shard_map/left_sum/ppermute | solution.py:30
  33.8 2.6 %collective-permute-done.16 = f32[64,128]{1,0:T(8,128)S(1)} collective-permute-done((f32[64,128]{1,0:T(8,128)S(1)}, f32[64,128]{1,0:T(8,128)S(1)}, u32[]{:S(2)}, u32[]{:S(2)}) %collective-permute-start.16) | collective-permute-done | bytes 32800 | tf_op jit(solution)/shard_map/left_sum/ppermute | solution.py:30
  36.4 1.3 %collective-permute-start.20 = (f32[64,128]{1,0:T(8,128)S(1)}, f32[64,128]{1,0:T(8,128)S(1)}, u32[]{:S(2)}, u32[]{:S(2)}) collective-permute-start(f32[64,128]{1,0:T(8,128)S(1)} %add_add_fusion.1), channel_id=1, source_target_pairs={{0,128},{1,129},{2,130},{3,131},{4,132},{5,133},{6,134},{7,135},{8... | collective-permute-start | bytes 98312 | tf_op jit(solution)/shard_map/left_sum/ppermute | solution.py:30
  37.7 1.6 %collective-permute-start.19 = (f32[64,128]{1,0:T(8,128)S(1)}, f32[64,128]{1,0:T(8,128)S(1)}, u32[]{:S(2)}, u32[]{:S(2)}) collective-permute-start(f32[64,128]{1,0:T(8,128)S(1)} %add_add_fusion.1), channel_id=1, source_target_pairs={{0,192},{1,193},{2,194},{3,195},{4,196},{5,197},{6,198},{7,199},{8... | collective-permute-start | bytes 98312 | tf_op jit(solution)/shard_map/left_sum/ppermute | solution.py:30
  40.1 2.2 %collective-permute-done.19 = f32[64,128]{1,0:T(8,128)S(1)} collective-permute-done((f32[64,128]{1,0:T(8,128)S(1)}, f32[64,128]{1,0:T(8,128)S(1)}, u32[]{:S(2)}, u32[]{:S(2)}) %collective-permute-start.19) | collective-permute-done | bytes 32800 | tf_op jit(solution)/shard_map/left_sum/ppermute | solution.py:30
  43.5 2.9 %collective-permute-start.28 = (f32[4,256,128]{2,1,0:T(8,128)S(1)}, f32[4,256,128]{2,1,0:T(8,128)S(1)}, u32[]{:S(2)}, u32[]{:S(2)}) collective-permute-start(f32[4,256,128]{2,1,0:T(8,128)S(1)} %get-tuple-element.52), channel_id=1, source_target_pairs={{0,1},{1,0},{2,3},{3,2},{4,5},{5,4},{6,7},{7,6},{8,9},{9,8},{10,11... | collective-permute-start | bytes 1572872 | tf_op jit(solution)/shard_map/right_sum/ppermute | solution.py:30
  48.0 1.3 %collective-permute-start.29 = (f32[256,128]{1,0:T(8,128)S(1)}, f32[256,128]{1,0:T(8,128)S(1)}, u32[]{:S(2)}, u32[]{:S(2)}) collective-permute-start(f32[256,128]{1,0:T(8,128)S(1)} %get-tuple-element.54), channel_id=1, source_target_pairs={{0,32},{1,33},{2,34},{3,35},{4,36},{5,37},{6,38},{7,39},{8,40},{9,... | collective-permute-start | bytes 393224 | tf_op jit(solution)/shard_map/right_sum/ppermute | solution.py:30
  50.8 1.1 %collective-permute-start.22 = (f32[288,128]{1,0:T(8,128)S(1)}, f32[288,128]{1,0:T(8,128)S(1)}, u32[]{:S(2)}, u32[]{:S(2)}) collective-permute-start(f32[288,128]{1,0:T(8,128)S(1)} %get-tuple-element.44), channel_id=1, source_target_pairs={{0,8},{1,9},{2,10},{3,11},{4,12},{5,13},{6,14},{7,15},{8,0},{9,1},... | collective-permute-start | bytes 442376 | tf_op jit(solution)/shard_map/right_sum/ppermute | solution.py:30
  51.9 1.3 %collective-permute-start.23 = (f32[288,128]{1,0:T(8,128)S(1)}, f32[288,128]{1,0:T(8,128)S(1)}, u32[]{:S(2)}, u32[]{:S(2)}) collective-permute-start(f32[288,128]{1,0:T(8,128)S(1)} %get-tuple-element.45), channel_id=1, source_target_pairs={{0,12},{1,13},{2,14},{3,15},{4,8},{5,9},{6,10},{7,11},{8,4},{9,5},... | collective-permute-start | bytes 442376 | tf_op jit(solution)/shard_map/right_sum/ppermute | solution.py:30
  53.2 1.1 %collective-permute-done.29.two = f32[256,128]{1,0:T(8,128)S(1)} collective-permute-done((f32[256,128]{1,0:T(8,128)S(1)}, f32[256,128]{1,0:T(8,128)S(1)}, u32[]{:S(2)}, u32[]{:S(2)}) %collective-permute-start.29) | collective-permute-done | bytes 131104 | tf_op jit(solution)/shard_map/right_sum/ppermute | solution.py:30
  54.3 3.5 %collective-permute-done.30.three = f32[256,128]{1,0:T(8,128)S(1)} collective-permute-done((f32[256,128]{1,0:T(8,128)S(1)}, f32[256,128]{1,0:T(8,128)S(1)}, u32[]{:S(2)}, u32[]{:S(2)}) %collective-permute-start.30) | collective-permute-done | bytes 131104 | tf_op jit(solution)/shard_map/right_sum/ppermute | solution.py:30
  57.9 1.1 %collective-permute-start.32 = (f32[64,128]{1,0:T(8,128)S(1)}, f32[64,128]{1,0:T(8,128)S(1)}, u32[]{:S(2)}, u32[]{:S(2)}) collective-permute-start(f32[64,128]{1,0:T(8,128)S(1)} %get-tuple-element.58), channel_id=1, source_target_pairs={{0,8},{1,9},{2,10},{3,11},{4,12},{5,13},{6,14},{7,15},{8,0},{9,1},... | collective-permute-start | bytes 98312 | tf_op jit(solution)/shard_map/right_sum/ppermute | solution.py:30
  58.9 1.3 %collective-permute-start.33 = (f32[64,128]{1,0:T(8,128)S(1)}, f32[64,128]{1,0:T(8,128)S(1)}, u32[]{:S(2)}, u32[]{:S(2)}) collective-permute-start(f32[64,128]{1,0:T(8,128)S(1)} %get-tuple-element.59), channel_id=1, source_target_pairs={{0,12},{1,13},{2,14},{3,15},{4,8},{5,9},{6,10},{7,11},{8,4},{9,5},... | collective-permute-start | bytes 98312 | tf_op jit(solution)/shard_map/right_sum/ppermute | solution.py:30
  61.3 2.2 %collective-permute-start.25 = (f32[64,128]{1,0:T(8,128)S(1)}, f32[64,128]{1,0:T(8,128)S(1)}, u32[]{:S(2)}, u32[]{:S(2)}) collective-permute-start(f32[64,128]{1,0:T(8,128)S(1)} %get-tuple-element.48), channel_id=1, source_target_pairs={{0,32},{1,33},{2,34},{3,35},{4,36},{5,37},{6,38},{7,39},{8,40},{9,... | collective-permute-start | bytes 98312 | tf_op jit(solution)/shard_map/right_sum/ppermute | solution.py:30
  64.2 1.5 %collective-permute-done.25.two_a = f32[64,128]{1,0:T(8,128)S(1)} collective-permute-done((f32[64,128]{1,0:T(8,128)S(1)}, f32[64,128]{1,0:T(8,128)S(1)}, u32[]{:S(2)}, u32[]{:S(2)}) %collective-permute-start.25) | collective-permute-done | bytes 32800 | tf_op jit(solution)/shard_map/right_sum/ppermute | solution.py:30
  65.7 1.8 %collective-permute-done.26.three_a = f32[64,128]{1,0:T(8,128)S(1)} collective-permute-done((f32[64,128]{1,0:T(8,128)S(1)}, f32[64,128]{1,0:T(8,128)S(1)}, u32[]{:S(2)}, u32[]{:S(2)}) %collective-permute-start.26) | collective-permute-done | bytes 32800 | tf_op jit(solution)/shard_map/right_sum/ppermute | solution.py:30
  67.5 1.2 %collective-permute-start.35 = (f32[80,256]{1,0:T(8,128)S(1)}, f32[80,256]{1,0:T(8,128)S(1)}, u32[]{:S(2)}, u32[]{:S(2)}) collective-permute-start(f32[80,256]{1,0:T(8,128)S(1)} %right_sum.14.own), channel_id=1, source_target_pairs={{0,130},{1,131},{2,128},{3,129},{4,134},{5,135},{6,132},{7,133},{8... | collective-permute-start | bytes 245768 | tf_op jit(solution)/shard_map/right_sum/ppermute | solution.py:30
  68.7 4.3 %collective-permute-done.35.other = f32[80,256]{1,0:T(8,128)S(1)} collective-permute-done((f32[80,256]{1,0:T(8,128)S(1)}, f32[80,256]{1,0:T(8,128)S(1)}, u32[]{:S(2)}, u32[]{:S(2)}) %collective-permute-start.35) | collective-permute-done | bytes 81952 | tf_op jit(solution)/shard_map/right_sum/ppermute | solution.py:30
  73.3 1.6 %collective-permute-start.37 = (f32[64,256]{1,0:T(8,128)S(1)}, f32[64,256]{1,0:T(8,128)S(1)}, u32[]{:S(2)}, u32[]{:S(2)}) collective-permute-start(f32[64,256]{1,0:T(8,128)S(1)} %get-tuple-element.64.own), channel_id=1, source_target_pairs={{0,192},{1,193},{2,194},{3,195},{4,196},{5,197},{6,198},{7,199},{8... | collective-permute-start | bytes 196616 | tf_op jit(solution)/shard_map/right_sum/ppermute | solution.py:30
  75.7 3.0 %cholesky.1 = (f32[64,64]{1,0:T(8,128)S(1)}, f32[64,128]{1,0:T(8,128)}, bf16[128,192]{1,0:T(8,128)(2,1)S(1)}) custom-call(f32[16,256]{1,0:T(8,128)S(1)} %get-tuple-element.62.packed, f32[64,128]{1,0:T(8,128)S(1)} %add_add_fusion.left), custom_call_target="tpu_custom_call" | custom-call | tf_op jit(solution)/shard_map/cholesky/pallas_call | solution.py:324
  79.3 15.6 %all_to_all.5.refs_2_.refs_4_ = f32[16,64,256]{2,1,0:T(8,128)S(1)} all-to-all(f32[16,64,256]{2,1,0:T(8,128)S(1)} %right_factor.1), channel_id=1, replica_groups=mesh['zlo'=4,'y'=4,'x'=4,'zhi'=2,'core'=2] {'x','y'}, dimensions={0} | all-to-all | bytes 2097152 | tf_op jit(solution)/shard_map/right_factor/all_to_all | solution.py:275
  94.8 6.9 %collective-permute-start.39 = (f32[16,64,256]{2,1,0:T(8,128)S(1)}, f32[16,64,256]{2,1,0:T(8,128)S(1)}, u32[]{:S(2)}, u32[]{:S(2)}) collective-permute-start(f32[16,64,256]{2,1,0:T(8,128)S(1)} %all_to_all.5.refs_2_.refs_4_), channel_id=1, source_target_pairs={{0,1},{1,0},{2,3},{3,2},{4,5},{5,4},{6,7},{7,6},{8,9},{9,8},{10,11... | collective-permute-start | bytes 3145736 | tf_op jit(solution)/shard_map/right_factor/ppermute | solution.py:30
  101.7 1.7 %error.2.refs_0_ = f32[1,128,8192]{2,1,0:T(8,128)} custom-call(f32[128,8192]{1,0:T(8,128)S(1)} %add_bitcast_fusion.refs_10_.refs_7_.merged.refs_0_.refs_1_, bf16[128,192]{1,0:T(8,128)(2,1)S(1)} %get-tuple-element.63.refs_1_.refs_2_, f32[16,64,256]{2,1,0:T(8,128)S(1)} %all_to_all.5.refs_2_.refs_4_), custom_call_target="tpu_custom_call" | custom-call | tf_op jit(solution)/shard_map/error/pallas_call | solution.py:264
  104.0 1.7 %error.3 = (f32[1,128,8192]{2,1,0:T(8,128)}, f32[64,512]{1,0:T(8,128)}) custom-call(f32[1,128,8192]{2,1,0:T(8,128)} %error.2.refs_0_, f32[128,8192]{1,0:T(8,128)S(1)} %add_bitcast_fusion.refs_10_.refs_7_.merged.refs_0_.refs_1_, bf16[128,192]{1,0:T(8,128)(2,1)S(1)} %get-tuple-element.63.refs_1_.refs_2_, ...), custom_call_target="tpu_custom_call", output_to_operand_aliasing={{0}: (0, {})} | custom-call | tf_op jit(solution)/shard_map/error/pallas_call | solution.py:264
  (68 shorter events, 15.3 us)
Async XLA Ops:
  0.6 13.8 %collective-permute-start.3 = (f32[64,512]{1,0:T(8,128)}, f32[64,512]{1,0:T(8,128)S(1)}, u32[]{:S(2)}, u32[]{:S(2)}) collective-permute-start(f32[64,512]{1,0:T(8,128)} %bitcast.5), channel_id=1, source_target_pairs={{0,130},{1,131},{2,128},{3,129},{4,134},{5,135},{6,132},{7,133},{8... | collective-permute-start | bytes 393224 | tf_op jit(solution)/shard_map/gather_factor/ppermute | solution.py:30
  7.6 12.1 %collective-permute-start.2 = (f32[64,512]{1,0:T(8,128)}, f32[64,512]{1,0:T(8,128)S(1)}, u32[]{:S(2)}, u32[]{:S(2)}) collective-permute-start(f32[64,512]{1,0:T(8,128)} %bitcast.6), channel_id=1, source_target_pairs={{0,8},{1,9},{2,10},{3,11},{4,12},{5,13},{6,14},{7,15},{8,0},{9,1},... | collective-permute-start | bytes 393224 | tf_op jit(solution)/shard_map/gather_factor/ppermute | solution.py:30
  10.3 10.2 %collective-permute-start.1 = (f32[64,512]{1,0:T(8,128)}, f32[64,512]{1,0:T(8,128)S(1)}, u32[]{:S(2)}, u32[]{:S(2)}) collective-permute-start(f32[64,512]{1,0:T(8,128)} %bitcast.7), channel_id=1, source_target_pairs={{0,12},{1,13},{2,14},{3,15},{4,8},{5,9},{6,10},{7,11},{8,4},{9,5},... | collective-permute-start | bytes 393224 | tf_op jit(solution)/shard_map/gather_factor/ppermute | solution.py:30
  11.2 9.3 %collective-permute-start = (f32[64,512]{1,0:T(8,128)}, f32[64,512]{1,0:T(8,128)S(1)}, u32[]{:S(2)}, u32[]{:S(2)}) collective-permute-start(f32[64,512]{1,0:T(8,128)} %bitcast.8), channel_id=1, source_target_pairs={{0,4},{1,5},{2,6},{3,7},{4,0},{5,1},{6,2},{7,3},{8,12},{9,13},{10,... | collective-permute-start | bytes 393224 | tf_op jit(solution)/shard_map/gather_factor/ppermute | solution.py:30
  14.5 6.5 %collective-permute-start.4 = (f32[64,512]{1,0:T(8,128)S(1)}, f32[64,512]{1,0:T(8,128)S(1)}, u32[]{:S(2)}, u32[]{:S(2)}) collective-permute-start(f32[64,512]{1,0:T(8,128)S(1)} %collective-permute-done.3.refs_8_), channel_id=1, source_target_pairs={{0,8},{1,9},{2,10},{3,11},{4,12},{5,13},{6,14},{7,15},{8,0},{9,1},... | collective-permute-start | bytes 393224 | tf_op jit(solution)/shard_map/gather_factor/ppermute | solution.py:30
  17.6 5.3 %collective-permute-start.5 = (f32[64,512]{1,0:T(8,128)S(1)}, f32[64,512]{1,0:T(8,128)S(1)}, u32[]{:S(2)}, u32[]{:S(2)}) collective-permute-start(f32[64,512]{1,0:T(8,128)S(1)} %bitcast.9), channel_id=1, source_target_pairs={{0,1},{1,0},{2,3},{3,2},{4,5},{5,4},{6,7},{7,6},{8,9},{9,8},{10,11... | collective-permute-start | bytes 393224 | tf_op jit(solution)/shard_map/left_sum/ppermute | solution.py:30
  19.6 6.3 %collective-permute-start.11 = (f32[64,512]{1,0:T(8,128)S(1)}, f32[64,512]{1,0:T(8,128)S(1)}, u32[]{:S(2)}, u32[]{:S(2)}) collective-permute-start(f32[64,512]{1,0:T(8,128)S(1)} %collective-permute-done.3.refs_8_), channel_id=1, source_target_pairs={{0,12},{1,13},{2,14},{3,15},{4,8},{5,9},{6,10},{7,11},{8,4},{9,5},... | collective-permute-start | bytes 393224 | tf_op jit(solution)/shard_map/gather_factor/ppermute | solution.py:30
  20.5 6.3 %collective-permute-start.10 = (f32[64,512]{1,0:T(8,128)S(1)}, f32[64,512]{1,0:T(8,128)S(1)}, u32[]{:S(2)}, u32[]{:S(2)}) collective-permute-start(f32[64,512]{1,0:T(8,128)S(1)} %collective-permute-done.3.refs_8_), channel_id=1, source_target_pairs={{0,4},{1,5},{2,6},{3,7},{4,0},{5,1},{6,2},{7,3},{8,12},{9,13},{10,... | collective-permute-start | bytes 393224 | tf_op jit(solution)/shard_map/gather_factor/ppermute | solution.py:30
  20.5 6.3 %collective-permute-start.9 = (f32[64,512]{1,0:T(8,128)S(1)}, f32[64,512]{1,0:T(8,128)S(1)}, u32[]{:S(2)}, u32[]{:S(2)}) collective-permute-start(f32[64,512]{1,0:T(8,128)S(1)} %collective-permute-done.3.refs_8_), channel_id=1, source_target_pairs={{0,1},{1,0},{2,3},{3,2},{4,5},{5,4},{6,7},{7,6},{8,9},{9,8},{10,11... | collective-permute-start | bytes 393224 | tf_op jit(solution)/shard_map/left_sum/ppermute | solution.py:30
  21.0 6.3 %collective-permute-start.6 = (f32[64,512]{1,0:T(8,128)S(1)}, f32[64,512]{1,0:T(8,128)S(1)}, u32[]{:S(2)}, u32[]{:S(2)}) collective-permute-start(f32[64,512]{1,0:T(8,128)S(1)} %collective-permute-done.refs_0_), channel_id=1, source_target_pairs={{0,1},{1,0},{2,3},{3,2},{4,5},{5,4},{6,7},{7,6},{8,9},{9,8},{10,11... | collective-permute-start | bytes 393224 | tf_op jit(solution)/shard_map/left_sum/ppermute | solution.py:30
  22.8 4.5 %collective-permute-start.7 = (f32[64,512]{1,0:T(8,128)S(1)}, f32[64,512]{1,0:T(8,128)S(1)}, u32[]{:S(2)}, u32[]{:S(2)}) collective-permute-start(f32[64,512]{1,0:T(8,128)S(1)} %collective-permute-done.1.refs_1_), channel_id=1, source_target_pairs={{0,1},{1,0},{2,3},{3,2},{4,5},{5,4},{6,7},{7,6},{8,9},{9,8},{10,11... | collective-permute-start | bytes 393224 | tf_op jit(solution)/shard_map/left_sum/ppermute | solution.py:30
  29.4 4.4 %collective-permute-start.17 = (f32[64,128]{1,0:T(8,128)S(1)}, f32[64,128]{1,0:T(8,128)S(1)}, u32[]{:S(2)}, u32[]{:S(2)}) collective-permute-start(f32[64,128]{1,0:T(8,128)S(1)} %left_sum.3), channel_id=1, source_target_pairs={{0,32},{1,33},{2,34},{3,35},{4,36},{5,37},{6,38},{7,39},{8,40},{9,... | collective-permute-start | bytes 98312 | tf_op jit(solution)/shard_map/left_sum/ppermute | solution.py:30
  32.4 4.0 %collective-permute-start.16 = (f32[64,128]{1,0:T(8,128)S(1)}, f32[64,128]{1,0:T(8,128)S(1)}, u32[]{:S(2)}, u32[]{:S(2)}) collective-permute-start(f32[64,128]{1,0:T(8,128)S(1)} %left_sum.3), channel_id=1, source_target_pairs={{0,48},{1,49},{2,50},{3,51},{4,52},{5,53},{6,54},{7,55},{8,56},{9,... | collective-permute-start | bytes 98312 | tf_op jit(solution)/shard_map/left_sum/ppermute | solution.py:30
  37.7 4.7 %collective-permute-start.19 = (f32[64,128]{1,0:T(8,128)S(1)}, f32[64,128]{1,0:T(8,128)S(1)}, u32[]{:S(2)}, u32[]{:S(2)}) collective-permute-start(f32[64,128]{1,0:T(8,128)S(1)} %add_add_fusion.1), channel_id=1, source_target_pairs={{0,192},{1,193},{2,194},{3,195},{4,196},{5,197},{6,198},{7,199},{8... | collective-permute-start | bytes 98312 | tf_op jit(solution)/shard_map/left_sum/ppermute | solution.py:30
  43.5 4.4 %collective-permute-start.28 = (f32[4,256,128]{2,1,0:T(8,128)S(1)}, f32[4,256,128]{2,1,0:T(8,128)S(1)}, u32[]{:S(2)}, u32[]{:S(2)}) collective-permute-start(f32[4,256,128]{2,1,0:T(8,128)S(1)} %get-tuple-element.52), channel_id=1, source_target_pairs={{0,1},{1,0},{2,3},{3,2},{4,5},{5,4},{6,7},{7,6},{8,9},{9,8},{10,11... | collective-permute-start | bytes 1572872 | tf_op jit(solution)/shard_map/right_sum/ppermute | solution.py:30
  46.4 4.3 %collective-permute-start.21 = (f32[4,288,128]{2,1,0:T(8,128)S(1)}, f32[4,288,128]{2,1,0:T(8,128)S(1)}, u32[]{:S(2)}, u32[]{:S(2)}) collective-permute-start(f32[4,288,128]{2,1,0:T(8,128)S(1)} %get-tuple-element.42), channel_id=1, source_target_pairs={{0,1},{1,0},{2,3},{3,2},{4,5},{5,4},{6,7},{7,6},{8,9},{9,8},{10,11... | collective-permute-start | bytes 1769480 | tf_op jit(solution)/shard_map/right_sum/ppermute | solution.py:30
  48.0 6.3 %collective-permute-start.29 = (f32[256,128]{1,0:T(8,128)S(1)}, f32[256,128]{1,0:T(8,128)S(1)}, u32[]{:S(2)}, u32[]{:S(2)}) collective-permute-start(f32[256,128]{1,0:T(8,128)S(1)} %get-tuple-element.54), channel_id=1, source_target_pairs={{0,32},{1,33},{2,34},{3,35},{4,36},{5,37},{6,38},{7,39},{8,40},{9,... | collective-permute-start | bytes 393224 | tf_op jit(solution)/shard_map/right_sum/ppermute | solution.py:30
  49.3 8.5 %collective-permute-start.30 = (f32[256,128]{1,0:T(8,128)S(1)}, f32[256,128]{1,0:T(8,128)S(1)}, u32[]{:S(2)}, u32[]{:S(2)}) collective-permute-start(f32[256,128]{1,0:T(8,128)S(1)} %get-tuple-element.55), channel_id=1, source_target_pairs={{0,48},{1,49},{2,50},{3,51},{4,52},{5,53},{6,54},{7,55},{8,56},{9,... | collective-permute-start | bytes 393224 | tf_op jit(solution)/shard_map/right_sum/ppermute | solution.py:30
  50.0 7.8 %collective-permute-start.31 = (f32[256,128]{1,0:T(8,128)S(1)}, f32[256,128]{1,0:T(8,128)S(1)}, u32[]{:S(2)}, u32[]{:S(2)}) collective-permute-start(f32[256,128]{1,0:T(8,128)S(1)} %get-tuple-element.56), channel_id=1, source_target_pairs={{0,16},{1,17},{2,18},{3,19},{4,20},{5,21},{6,22},{7,23},{8,24},{9,... | collective-permute-start | bytes 393224 | tf_op jit(solution)/shard_map/right_sum/ppermute | solution.py:30
  50.8 9.4 %collective-permute-start.22 = (f32[288,128]{1,0:T(8,128)S(1)}, f32[288,128]{1,0:T(8,128)S(1)}, u32[]{:S(2)}, u32[]{:S(2)}) collective-permute-start(f32[288,128]{1,0:T(8,128)S(1)} %get-tuple-element.44), channel_id=1, source_target_pairs={{0,8},{1,9},{2,10},{3,11},{4,12},{5,13},{6,14},{7,15},{8,0},{9,1},... | collective-permute-start | bytes 442376 | tf_op jit(solution)/shard_map/right_sum/ppermute | solution.py:30
  51.9 9.4 %collective-permute-start.23 = (f32[288,128]{1,0:T(8,128)S(1)}, f32[288,128]{1,0:T(8,128)S(1)}, u32[]{:S(2)}, u32[]{:S(2)}) collective-permute-start(f32[288,128]{1,0:T(8,128)S(1)} %get-tuple-element.45), channel_id=1, source_target_pairs={{0,12},{1,13},{2,14},{3,15},{4,8},{5,9},{6,10},{7,11},{8,4},{9,5},... | collective-permute-start | bytes 442376 | tf_op jit(solution)/shard_map/right_sum/ppermute | solution.py:30
  54.3 7.0 %collective-permute-start.24 = (f32[288,128]{1,0:T(8,128)S(1)}, f32[288,128]{1,0:T(8,128)S(1)}, u32[]{:S(2)}, u32[]{:S(2)}) collective-permute-start(f32[288,128]{1,0:T(8,128)S(1)} %get-tuple-element.46), channel_id=1, source_target_pairs={{0,4},{1,5},{2,6},{3,7},{4,0},{5,1},{6,2},{7,3},{8,12},{9,13},{10,... | collective-permute-start | bytes 442376 | tf_op jit(solution)/shard_map/right_sum/ppermute | solution.py:30
  57.9 6.3 %collective-permute-start.32 = (f32[64,128]{1,0:T(8,128)S(1)}, f32[64,128]{1,0:T(8,128)S(1)}, u32[]{:S(2)}, u32[]{:S(2)}) collective-permute-start(f32[64,128]{1,0:T(8,128)S(1)} %get-tuple-element.58), channel_id=1, source_target_pairs={{0,8},{1,9},{2,10},{3,11},{4,12},{5,13},{6,14},{7,15},{8,0},{9,1},... | collective-permute-start | bytes 98312 | tf_op jit(solution)/shard_map/right_sum/ppermute | solution.py:30
  58.9 5.2 %collective-permute-start.33 = (f32[64,128]{1,0:T(8,128)S(1)}, f32[64,128]{1,0:T(8,128)S(1)}, u32[]{:S(2)}, u32[]{:S(2)}) collective-permute-start(f32[64,128]{1,0:T(8,128)S(1)} %get-tuple-element.59), channel_id=1, source_target_pairs={{0,12},{1,13},{2,14},{3,15},{4,8},{5,9},{6,10},{7,11},{8,4},{9,5},... | collective-permute-start | bytes 98312 | tf_op jit(solution)/shard_map/right_sum/ppermute | solution.py:30
  60.2 3.9 %collective-permute-start.34 = (f32[64,128]{1,0:T(8,128)S(1)}, f32[64,128]{1,0:T(8,128)S(1)}, u32[]{:S(2)}, u32[]{:S(2)}) collective-permute-start(f32[64,128]{1,0:T(8,128)S(1)} %get-tuple-element.60), channel_id=1, source_target_pairs={{0,4},{1,5},{2,6},{3,7},{4,0},{5,1},{6,2},{7,3},{8,12},{9,13},{10,... | collective-permute-start | bytes 98312 | tf_op jit(solution)/shard_map/right_sum/ppermute | solution.py:30
  61.3 4.4 %collective-permute-start.25 = (f32[64,128]{1,0:T(8,128)S(1)}, f32[64,128]{1,0:T(8,128)S(1)}, u32[]{:S(2)}, u32[]{:S(2)}) collective-permute-start(f32[64,128]{1,0:T(8,128)S(1)} %get-tuple-element.48), channel_id=1, source_target_pairs={{0,32},{1,33},{2,34},{3,35},{4,36},{5,37},{6,38},{7,39},{8,40},{9,... | collective-permute-start | bytes 98312 | tf_op jit(solution)/shard_map/right_sum/ppermute | solution.py:30
  63.5 4.0 %collective-permute-start.26 = (f32[64,128]{1,0:T(8,128)S(1)}, f32[64,128]{1,0:T(8,128)S(1)}, u32[]{:S(2)}, u32[]{:S(2)}) collective-permute-start(f32[64,128]{1,0:T(8,128)S(1)} %get-tuple-element.49), channel_id=1, source_target_pairs={{0,48},{1,49},{2,50},{3,51},{4,52},{5,53},{6,54},{7,55},{8,56},{9,... | collective-permute-start | bytes 98312 | tf_op jit(solution)/shard_map/right_sum/ppermute | solution.py:30
  67.5 5.5 %collective-permute-start.35 = (f32[80,256]{1,0:T(8,128)S(1)}, f32[80,256]{1,0:T(8,128)S(1)}, u32[]{:S(2)}, u32[]{:S(2)}) collective-permute-start(f32[80,256]{1,0:T(8,128)S(1)} %right_sum.14.own), channel_id=1, source_target_pairs={{0,130},{1,131},{2,128},{3,129},{4,134},{5,135},{6,132},{7,133},{8... | collective-permute-start | bytes 245768 | tf_op jit(solution)/shard_map/right_sum/ppermute | solution.py:30
  73.0 5.7 %collective-permute-start.38 = (f32[64,256]{1,0:T(8,128)S(1)}, f32[64,256]{1,0:T(8,128)S(1)}, u32[]{:S(2)}, u32[]{:S(2)}) collective-permute-start(f32[64,256]{1,0:T(8,128)S(1)} %get-tuple-element.64.own), channel_id=1, source_target_pairs={{0,128},{1,129},{2,130},{3,131},{4,132},{5,133},{6,134},{7,135},{8... | collective-permute-start | bytes 196616 | tf_op jit(solution)/shard_map/right_sum/ppermute | solution.py:30
  73.3 5.4 %collective-permute-start.37 = (f32[64,256]{1,0:T(8,128)S(1)}, f32[64,256]{1,0:T(8,128)S(1)}, u32[]{:S(2)}, u32[]{:S(2)}) collective-permute-start(f32[64,256]{1,0:T(8,128)S(1)} %get-tuple-element.64.own), channel_id=1, source_target_pairs={{0,192},{1,193},{2,194},{3,195},{4,196},{5,197},{6,198},{7,199},{8... | collective-permute-start | bytes 196616 | tf_op jit(solution)/shard_map/right_sum/ppermute | solution.py:30
  75.0 4.0 %collective-permute-start.36 = (f32[64,256]{1,0:T(8,128)S(1)}, f32[64,256]{1,0:T(8,128)S(1)}, u32[]{:S(2)}, u32[]{:S(2)}) collective-permute-start(f32[64,256]{1,0:T(8,128)S(1)} %get-tuple-element.64.own), channel_id=1, source_target_pairs={{0,64},{1,65},{2,66},{3,67},{4,68},{5,69},{6,70},{7,71},{8,72},{9,... | collective-permute-start | bytes 196616 | tf_op jit(solution)/shard_map/right_sum/ppermute | solution.py:30
  94.8 9.2 %collective-permute-start.39 = (f32[16,64,256]{2,1,0:T(8,128)S(1)}, f32[16,64,256]{2,1,0:T(8,128)S(1)}, u32[]{:S(2)}, u32[]{:S(2)}) collective-permute-start(f32[16,64,256]{2,1,0:T(8,128)S(1)} %all_to_all.5.refs_2_.refs_4_), channel_id=1, source_target_pairs={{0,1},{1,0},{2,3},{3,2},{4,5},{5,4},{6,7},{7,6},{8,9},{9,8},{10,11... | collective-permute-start | bytes 3145736 | tf_op jit(solution)/shard_map/right_factor/ppermute | solution.py:30
  (9 other events, 38.0 us)

commit v3 on v2

--- a/solution.py
+++ b/solution.py
@@ -12,22 +12,30 @@
 SIZES = (4, 4, 4, 2, 2)
 ROWS, COLS, RANK, BLOCK = 128, 8192, 64, 512
 HALF = COLS // 2
-WIDE, LANES, EXTRA, RING = 256, 128, 16, 4
+WIDE, EXTRA, RING = 256, 16, 4
 STEPS = (1, 3, 2)
 PACKED = (2, 3, 1)
-TALL, GRAM = RING * RANK, 2 * EXTRA
+TALL, FOLD = RING * RANK, RANK // EXTRA
 CHUNKS = HALF // WIDE
 LIMIT = 8 * 1024 * 1024
 F32, BF16 = jnp.float32, jnp.bfloat16
 VMEM = pl.BlockSpec(memory_space=pltpu.VMEM)
 
 
-def shift(value, zlo=0, y=0, x=0, zhi=0, core=0):
+def moved(value, flips):
     pairs = []
     for source in np.ndindex(*SIZES):
-        target = tuple(a ^ b for a, b in zip(source, (zlo, y, x, zhi, core)))
+        target = tuple(a ^ b for a, b in zip(source, flips(source[-1])))
         pairs.append((int(np.ravel_multi_index(source, SIZES)), int(np.ravel_multi_index(target, SIZES))))
     return lax.ppermute(value, AXES, pairs)
+
+
+def shift(value, zlo=0, y=0, x=0, zhi=0, core=0):
+    return moved(value, lambda _: (zlo, y, x, zhi, core))
+
+
+def mixed(value, step, second):
+    return moved(value, lambda core: (0, 0, step, 0, 0) if core == second else (0, step, 0, 0, 0))
 
 
 def ring(value, axis):
@@ -85,60 +93,52 @@
     )(*args)
 
 
-def column(half, chunk):
-    return pl.multiple_of(half * HALF + chunk * WIDE, WIDE)
-
-
-def cross_kernel(flip, merged, left, by_x, by_y):
+def column(half, first, second):
+    x, y = lax.axis_index("x"), lax.axis_index("y")
+    along_x = (x ^ first) * RING + (y ^ second)
+    along_y = (x ^ second) * RING + (y ^ first)
+    return pl.multiple_of(half * HALF + jnp.where(half == 0, along_x, along_y) * WIDE, WIDE)
+
+
+def cross_kernel(flip, merged, left, *outs):
     half = lax.axis_index("core") ^ flip
-    x, y = lax.axis_index("x"), lax.axis_index("y")
     high, low = split(left[...])
     lhs = jnp.concatenate([jnp.concatenate([high, high], 1), jnp.concatenate([low, low], 1)], 0)
     gram = dot(left[...], left[...], ((1,), (1,)), lax.Precision.HIGHEST)
-    flat = jnp.concatenate([gram[:GRAM], gram[GRAM:]], 1)
-    for sx in range(RING):
-        for sy in range(RING):
-            start = column(half, (x ^ sx) * RING + (y ^ sy))
-            rhs = jnp.concatenate(split(merged[:, pl.ds(start, WIDE)]), 0)
+    flat = jnp.concatenate([gram[q * EXTRA : (q + 1) * EXTRA] for q in range(FOLD)], 1)
+    for index, first in enumerate((2, 3, 1, 0)):
+        out, place = outs[index // 2], index % 2
+        for second in range(RING):
+            rhs = jnp.concatenate(split(merged[:, pl.ds(column(half, first, second), WIDE)]), 0)
             both = dot(lhs, rhs)
-            both = both[:RANK] + both[RANK:]
-            by_x[sx, sy * RANK : (sy + 1) * RANK] = both[:, :LANES]
-            by_y[sy, sx * RANK : (sx + 1) * RANK] = both[:, LANES:]
-        by_x[sx, TALL:] = flat
+            out[place, second * RANK : (second + 1) * RANK] = both[:RANK] + both[RANK:]
+        out[place, TALL:] = flat
 
 
 def cross_part(flip, merged, left):
-    return call(
-        functools.partial(cross_kernel, flip),
-        [
-            jax.ShapeDtypeStruct((RING, TALL + GRAM, LANES), F32),
-            jax.ShapeDtypeStruct((RING, TALL, LANES), F32),
-        ],
-        in_specs=[VMEM] * 2,
-        out_specs=[VMEM] * 2,
-    )(merged, left)
+    return simple(functools.partial(cross_kernel, flip), [(2, TALL + EXTRA, WIDE)] * 2, merged, left)
 
 
 def pack_kernel(own, received, *outs):
-    for step, out in zip((0,) + PACKED, outs):
-        out[...] = own[step] + received[step]
+    for place, out in enumerate(outs):
+        out[...] = own[place] + received[place]
 
 
 def scatter_kernel(own, two, three, one, *outs):
     def summed(rows):
         return (own[rows] + one[rows]) + (three[rows] + two[rows])
 
+    rows = slice(TALL, TALL + EXTRA)
+    gram = jnp.where(lax.axis_index("core") == 0, summed(rows), own[rows])
     for step, out in zip((0,) + PACKED, outs):
-        out[...] = summed(slice(step * RANK, (step + 1) * RANK))
-    if len(outs) > RING:
-        outs[RING][...] = summed(slice(TALL, TALL + GRAM))
-
-
-def join_kernel(own_a, two_a, three_a, one_a, own_b, two_b, three_b, one_b, gram, out):
-    out[:RANK, :LANES] = (own_a[...] + one_a[...]) + (three_a[...] + two_a[...])
-    out[:RANK, LANES:] = (own_b[...] + one_b[...]) + (three_b[...] + two_b[...])
-    out[RANK:, :LANES] = gram[:EXTRA]
-    out[RANK:, LANES:] = gram[EXTRA:]
+        out[:RANK] = summed(slice(step * RANK, (step + 1) * RANK))
+        out[RANK:] = gram
+
+
+def join_kernel(own, two, three, one, out):
+    summed = (own[...] + one[...]) + (three[...] + two[...])
+    out[:RANK] = summed[:RANK]
+    out[RANK:] = jnp.where(lax.axis_index("core") == 1, summed[RANK:], own[RANK:])
 
 
 def pair_kernel(own, other, out, gram):
@@ -147,12 +147,11 @@
 
 
 def factor_kernel(packed, left, inverse, left_out, wide_out):
-    flat = jnp.concatenate([packed[:, :LANES], packed[:, LANES:]], 0)
-    gram = jnp.concatenate([flat[:, :RANK], flat[:, RANK:]], 0)
+    gram = jnp.concatenate([packed[:, q * RANK : (q + 1) * RANK] for q in range(FOLD)], 0)
     row = lax.broadcasted_iota(jnp.int32, (RANK, RANK), 0)
     col = lax.broadcasted_iota(jnp.int32, (RANK, RANK), 1)
     work = jnp.concatenate([gram, jnp.where(row == col, 1.0, 0.0).astype(F32)], 1)
-    group = 4
+    group = 8
     done = []
     for base in range(0, RANK, group):
         top = (base // 8) * 8
@@ -234,7 +233,7 @@
     for chunk in range(CHUNKS):
         top, bottom = split(right[chunk])
         approx = dot(left[...], jnp.concatenate([top, bottom, top], 0))
-        start = column(half, chunk)
+        start = pl.multiple_of(half * HALF + chunk * WIDE, WIDE)
         buffer[chunk] = merged[:, pl.ds(start, WIDE)] - approx
         copy = pltpu.make_async_copy(buffer.at[chunk], out.at[0, :, pl.ds(start, WIDE)], sems.at[chunk])
         copy.start()
@@ -295,28 +294,31 @@
         far = shift(own, zlo=2, zhi=1)
         far, _ = lax.optimization_barrier((far, merged))
         second = ring(far, "x")
-        near[0], near[1], near[2], second[2] = lax.optimization_barrier((*near, second[2]))
     with jax.named_scope("left_sum"):
-        held = near + [own] + [shift(value, core=1) for value in [own] + near] + [far, shift(far, core=1)]
-        slots = [(s, 0, 0) for s in STEPS] + [(0, 0, 0), (0, 0, 1)] + [(s, 0, 1) for s in STEPS]
-        part = left_part(slots + [(0, 1, 0), (0, 1, 1)], merged, held)
-        held = second + [shift(value, core=1) for value in second]
-        part = left_part([(s, 1, c) for c in (0, 1) for s in STEPS], merged, held, part)
+        held = near + [own, far]
+        slots = [(s, 0) for s in STEPS] + [(0, 0), (0, 1)]
+        part = left_part([slot + (0,) for slot in slots], merged, held)
+        *held, last, part = lax.optimization_barrier((*held, second[2], part))
+        other = [shift(value, core=1) for value in held]
+        part = left_part([slot + (1,) for slot in slots] + [(2, 1, 0)], merged, other + [last], part)
+        second = second[:2] + [last]
+        other = [shift(value, core=1) for value in second]
+        slots = [(s, 1) for s in STEPS]
+        slots = [slot + (0,) for slot in slots[:2]] + [slot + (1,) for slot in slots]
+        part = left_part(slots, merged, second[:2] + other, part)
         left_sum = total(total(part, "y"), "zlo")
     with jax.named_scope("right_sum"):
         sent = cross_part(1, merged, left_sum)
         received = [shift(value, core=1) for value in sent]
         kept = cross_part(0, merged, left_sum)
-        axes, groups = ("x", "y"), []
-        for axis, own, other, height in zip(axes, kept, received, (TALL + GRAM, TALL)):
-            own, *outgoing = simple(pack_kernel, [(height, LANES)] * RING, own, other)
-            groups.append([own] + [shift(v, **{axis: step}) for step, v in zip(PACKED, outgoing)])
-        *part_a, gram = simple(scatter_kernel, [(RANK, LANES)] * RING + [(GRAM, LANES)], *groups[0])
-        part_b = simple(scatter_kernel, [(RANK, LANES)] * RING, *groups[1])
-        parts = []
-        for axis, (own, *outgoing) in zip(("y", "x"), (part_a, part_b)):
-            parts += [own] + [shift(v, **{axis: step}) for step, v in zip(PACKED, outgoing)]
-        joined = simple(join_kernel, (RANK + EXTRA, WIDE), *parts, gram)
+        packed = []
+        for mine, theirs in zip(kept, received):
+            packed += simple(pack_kernel, [(TALL + EXTRA, WIDE)] * 2, mine, theirs)
+        *outgoing, own = packed
+        incoming = [mixed(value, step, 0) for step, value in zip(PACKED, outgoing)]
+        own, *outgoing = simple(scatter_kernel, [(RANK + EXTRA, WIDE)] * RING, own, *incoming)
+        incoming = [mixed(value, step, 1) for step, value in zip(PACKED, outgoing)]
+        joined = simple(join_kernel, (RANK + EXTRA, WIDE), own, *incoming)
         other = shift(joined, zlo=2, zhi=1)
         summed, gram = simple(pair_kernel, [(RANK, WIDE), (EXTRA, WIDE)], joined, other)
         others = ring(summed, "zlo")

time: 106 us -> 102 us (0.962)
  starting transfers between devices: 51.6 us -> 48 us
    ppermute x40 -> x34, starting transfers between devices: 51.6 us -> 48 us  [moved(): return lax.ppermute(value, AXES, pairs)]
    ppermute x40 -> x34, waiting for transfers between devices: 25 us -> 25.1 us  [moved(): return lax.ppermute(value, AXES, pairs)]
  transfers between devices with their start and end apart: 40 -> 34, of which waited for: 16 -> 17; matrix products, arithmetic and copies ran while one was open for 3% -> 3% of each run, Pallas kernels for 6% -> 6%
where the time goes in v3:
time: 102 us
  starting transfers between devices  48 us (47%)
  waiting for transfers between devices  25.1 us (25%)
  blocking collectives  15.9 us (16%)
  Pallas kernels  9.09 us (9%)
  other arithmetic  3.28 us (3%)
    ppermute x34, starting transfers between devices, moved(): return lax.ppermute(value, AXES, pairs)  48 us
    ppermute x34, waiting for transfers between devices, moved(): return lax.ppermute(value, AXES, pairs)  25.1 us
    all_to_all x1, blocking collectives, exchange(): lax.all_to_all(value, ('x', 'y'), split_axis=0, concat_axis=0, tiled=True)  15.9 us
    pallas_call x2, Pallas kernels, error_part(): call(functools.partial(error_kernel, int(last)), out_shape, in_specs=([an...  3.32 us
    add x1, other arithmetic, body(): merged = gradient[0].astype(F32) + error_feed[0]  3.26 us
    pallas_call x1, Pallas kernels, body(): call(factor_kernel, [jax.ShapeDtypeStruct((RANK, RANK), F32), jax.ShapeDt...  2.43 us
  transfers between devices with their start and end apart: 34, of which 17 were waited for; matrix products, arithmetic and copies ran while one was open for 3% of the time, Pallas kernels for 6%

profile of v3, /device:TPU:1, one launch (start us, length us, event | category | flops | bytes accessed | tf_op | source)
XLA Modules:
  0.0 102.3 jit_solution(869006052510517579)
XLA Ops:
  0.6 6.9 %collective-permute-start.3 = (f32[64,512]{1,0:T(8,128)}, f32[64,512]{1,0:T(8,128)S(1)}, u32[]{:S(2)}, u32[]{:S(2)}) collective-permute-start(f32[64,512]{1,0:T(8,128)} %bitcast.5), channel_id=1, source_target_pairs={{0,130},{1,131},{2,128},{3,129},{4,134},{5,135},{6,132},{7,133},{8... | collective-permute-start | bytes 393224 | tf_op jit(solution)/shard_map/gather_factor/ppermute | solution.py:30
  7.6 2.7 %collective-permute-start.2 = (f32[64,512]{1,0:T(8,128)}, f32[64,512]{1,0:T(8,128)S(1)}, u32[]{:S(2)}, u32[]{:S(2)}) collective-permute-start(f32[64,512]{1,0:T(8,128)} %bitcast.6), channel_id=1, source_target_pairs={{0,8},{1,9},{2,10},{3,11},{4,12},{5,13},{6,14},{7,15},{8,0},{9,1},... | collective-permute-start | bytes 393224 | tf_op jit(solution)/shard_map/gather_factor/ppermute | solution.py:30
  10.3 0.9 collective-permute-start.1
  11.2 3.3 %add_bitcast_fusion.refs_5_.refs_7_.refs_6_.merged.refs_0_.refs_1_ = f32[128,8192]{1,0:T(8,128)S(1)} fusion(f32[1,128,8192]{2,1,0:T(8,128)} %param.4, bf16[1,128,8192]{2,1,0:T(8,128)(2,1)} %param.3), kind=kLoop, calls=%fused_computation | loop fusion | flops 2097152 | bytes 10485760 | tf_op jit(solution)/shard_map/add | solution.py:290
  14.5 3.1 %collective-permute-start.4 = (f32[64,512]{1,0:T(8,128)S(1)}, f32[64,512]{1,0:T(8,128)S(1)}, u32[]{:S(2)}, u32[]{:S(2)}) collective-permute-start(f32[64,512]{1,0:T(8,128)S(1)} %collective-permute-done.3.refs_4_), channel_id=1, source_target_pairs={{0,8},{1,9},{2,10},{3,11},{4,12},{5,13},{6,14},{7,15},{8,0},{9,1},... | collective-permute-start | bytes 393224 | tf_op jit(solution)/shard_map/gather_factor/ppermute | solution.py:30
  17.5 0.9 collective-permute-start.11
  19.0 1.1 %collective-permute-done.4.refs_6_ = f32[64,512]{1,0:T(8,128)S(1)} collective-permute-done((f32[64,512]{1,0:T(8,128)S(1)}, f32[64,512]{1,0:T(8,128)S(1)}, u32[]{:S(2)}, u32[]{:S(2)}) %collective-permute-start.4) | collective-permute-done | bytes 131104 | tf_op jit(solution)/shard_map/gather_factor/ppermute | solution.py:30
  20.1 2.5 %collective-permute-start.5 = (f32[64,512]{1,0:T(8,128)S(1)}, f32[64,512]{1,0:T(8,128)S(1)}, u32[]{:S(2)}, u32[]{:S(2)}) collective-permute-start(f32[64,512]{1,0:T(8,128)S(1)} %collective-permute-done.refs_0_), channel_id=1, source_target_pairs={{0,1},{1,0},{2,3},{3,2},{4,5},{5,4},{6,7},{7,6},{8,9},{9,8},{10,11... | collective-permute-start | bytes 393224 | tf_op jit(solution)/shard_map/left_sum/ppermute | solution.py:30
  23.3 2.5 %collective-permute-start.8 = (f32[64,512]{1,0:T(8,128)S(1)}, f32[64,512]{1,0:T(8,128)S(1)}, u32[]{:S(2)}, u32[]{:S(2)}) collective-permute-start(f32[64,512]{1,0:T(8,128)S(1)} %bitcast.10), channel_id=1, source_target_pairs={{0,1},{1,0},{2,3},{3,2},{4,5},{5,4},{6,7},{7,6},{8,9},{9,8},{10,11... | collective-permute-start | bytes 393224 | tf_op jit(solution)/shard_map/left_sum/ppermute | solution.py:30
  28.5 3.0 %collective-permute-start.17 = (f32[64,128]{1,0:T(8,128)S(1)}, f32[64,128]{1,0:T(8,128)S(1)}, u32[]{:S(2)}, u32[]{:S(2)}) collective-permute-start(f32[64,128]{1,0:T(8,128)S(1)} %left_sum.5), channel_id=1, source_target_pairs={{0,32},{1,33},{2,34},{3,35},{4,36},{5,37},{6,38},{7,39},{8,40},{9,... | collective-permute-start | bytes 98312 | tf_op jit(solution)/shard_map/left_sum/ppermute | solution.py:30
  32.8 2.6 %collective-permute-done.16 = f32[64,128]{1,0:T(8,128)S(1)} collective-permute-done((f32[64,128]{1,0:T(8,128)S(1)}, f32[64,128]{1,0:T(8,128)S(1)}, u32[]{:S(2)}, u32[]{:S(2)}) %collective-permute-start.16) | collective-permute-done | bytes 32800 | tf_op jit(solution)/shard_map/left_sum/ppermute | solution.py:30
  35.5 1.4 %collective-permute-start.20 = (f32[64,128]{1,0:T(8,128)S(1)}, f32[64,128]{1,0:T(8,128)S(1)}, u32[]{:S(2)}, u32[]{:S(2)}) collective-permute-start(f32[64,128]{1,0:T(8,128)S(1)} %add_add_fusion.1), channel_id=1, source_target_pairs={{0,128},{1,129},{2,130},{3,131},{4,132},{5,133},{6,134},{7,135},{8... | collective-permute-start | bytes 98312 | tf_op jit(solution)/shard_map/left_sum/ppermute | solution.py:30
  36.9 1.6 %collective-permute-start.19 = (f32[64,128]{1,0:T(8,128)S(1)}, f32[64,128]{1,0:T(8,128)S(1)}, u32[]{:S(2)}, u32[]{:S(2)}) collective-permute-start(f32[64,128]{1,0:T(8,128)S(1)} %add_add_fusion.1), channel_id=1, source_target_pairs={{0,192},{1,193},{2,194},{3,195},{4,196},{5,197},{6,198},{7,199},{8... | collective-permute-start | bytes 98312 | tf_op jit(solution)/shard_map/left_sum/ppermute | solution.py:30
  38.5 0.8 collective-permute-done.20
  39.4 2.2 %collective-permute-done.19 = f32[64,128]{1,0:T(8,128)S(1)} collective-permute-done((f32[64,128]{1,0:T(8,128)S(1)}, f32[64,128]{1,0:T(8,128)S(1)}, u32[]{:S(2)}, u32[]{:S(2)}) %collective-permute-start.19) | collective-permute-done | bytes 32800 | tf_op jit(solution)/shard_map/left_sum/ppermute | solution.py:30
  42.8 2.8 %collective-permute-start.22 = (f32[2,272,256]{2,1,0:T(8,128)S(1)}, f32[2,272,256]{2,1,0:T(8,128)S(1)}, u32[]{:S(2)}, u32[]{:S(2)}) collective-permute-start(f32[2,272,256]{2,1,0:T(8,128)S(1)} %get-tuple-element.42), channel_id=1, source_target_pairs={{0,1},{1,0},{2,3},{3,2},{4,5},{5,4},{6,7},{7,6},{8,9},{9,8},{10,11... | collective-permute-start | bytes 1671176 | tf_op jit(solution)/shard_map/right_sum/ppermute | solution.py:30
  46.2 1.0 collective-permute-done.22.received
  47.3 1.3 %collective-permute-start.23 = (f32[272,256]{1,0:T(8,128)S(1)}, f32[272,256]{1,0:T(8,128)S(1)}, u32[]{:S(2)}, u32[]{:S(2)}) collective-permute-start(f32[272,256]{1,0:T(8,128)S(1)} %get-tuple-element.43), channel_id=1, source_target_pairs={{0,8},{1,33},{2,10},{3,35},{4,12},{5,37},{6,14},{7,39},{8,0},{9,41... | collective-permute-start | bytes 835592 | tf_op jit(solution)/shard_map/right_sum/ppermute | solution.py:30
  50.2 4.4 %collective-permute-done.23.two = f32[272,256]{1,0:T(8,128)S(1)} collective-permute-done((f32[272,256]{1,0:T(8,128)S(1)}, f32[272,256]{1,0:T(8,128)S(1)}, u32[]{:S(2)}, u32[]{:S(2)}) %collective-permute-start.23) | collective-permute-done | bytes 278560 | tf_op jit(solution)/shard_map/right_sum/ppermute | solution.py:30
  54.6 2.9 %collective-permute-done.24.three = f32[272,256]{1,0:T(8,128)S(1)} collective-permute-done((f32[272,256]{1,0:T(8,128)S(1)}, f32[272,256]{1,0:T(8,128)S(1)}, u32[]{:S(2)}, u32[]{:S(2)}) %collective-permute-start.24) | collective-permute-done | bytes 278560 | tf_op jit(solution)/shard_map/right_sum/ppermute | solution.py:30
  57.6 1.2 %collective-permute-start.26 = (f32[80,256]{1,0:T(8,128)S(1)}, f32[80,256]{1,0:T(8,128)S(1)}, u32[]{:S(2)}, u32[]{:S(2)}) collective-permute-start(f32[80,256]{1,0:T(8,128)S(1)} %get-tuple-element.47), channel_id=1, source_target_pairs={{0,32},{1,9},{2,34},{3,11},{4,36},{5,13},{6,38},{7,15},{8,40},{9,1... | collective-permute-start | bytes 245768 | tf_op jit(solution)/shard_map/right_sum/ppermute | solution.py:30
  58.8 1.3 %collective-permute-start.27 = (f32[80,256]{1,0:T(8,128)S(1)}, f32[80,256]{1,0:T(8,128)S(1)}, u32[]{:S(2)}, u32[]{:S(2)}) collective-permute-start(f32[80,256]{1,0:T(8,128)S(1)} %get-tuple-element.48), channel_id=1, source_target_pairs={{0,48},{1,13},{2,50},{3,15},{4,52},{5,9},{6,54},{7,11},{8,56},{9,5... | collective-permute-start | bytes 245768 | tf_op jit(solution)/shard_map/right_sum/ppermute | solution.py:30
  60.3 2.2 %collective-permute-done.26.two = f32[80,256]{1,0:T(8,128)S(1)} collective-permute-done((f32[80,256]{1,0:T(8,128)S(1)}, f32[80,256]{1,0:T(8,128)S(1)}, u32[]{:S(2)}, u32[]{:S(2)}) %collective-permute-start.26) | collective-permute-done | bytes 81952 | tf_op jit(solution)/shard_map/right_sum/ppermute | solution.py:30
  62.5 1.2 %collective-permute-done.27.three = f32[80,256]{1,0:T(8,128)S(1)} collective-permute-done((f32[80,256]{1,0:T(8,128)S(1)}, f32[80,256]{1,0:T(8,128)S(1)}, u32[]{:S(2)}, u32[]{:S(2)}) %collective-permute-start.27) | collective-permute-done | bytes 81952 | tf_op jit(solution)/shard_map/right_sum/ppermute | solution.py:30
  63.7 2.2 %collective-permute-start.29 = (f32[80,256]{1,0:T(8,128)S(1)}, f32[80,256]{1,0:T(8,128)S(1)}, u32[]{:S(2)}, u32[]{:S(2)}) collective-permute-start(f32[80,256]{1,0:T(8,128)S(1)} %right_sum.12.own), channel_id=1, source_target_pairs={{0,130},{1,131},{2,128},{3,129},{4,134},{5,135},{6,132},{7,133},{8... | collective-permute-start | bytes 245768 | tf_op jit(solution)/shard_map/right_sum/ppermute | solution.py:30
  65.9 3.3 %collective-permute-done.29.other = f32[80,256]{1,0:T(8,128)S(1)} collective-permute-done((f32[80,256]{1,0:T(8,128)S(1)}, f32[80,256]{1,0:T(8,128)S(1)}, u32[]{:S(2)}, u32[]{:S(2)}) %collective-permute-start.29) | collective-permute-done | bytes 81952 | tf_op jit(solution)/shard_map/right_sum/ppermute | solution.py:30
  69.9 1.6 %collective-permute-start.31 = (f32[64,256]{1,0:T(8,128)S(1)}, f32[64,256]{1,0:T(8,128)S(1)}, u32[]{:S(2)}, u32[]{:S(2)}) collective-permute-start(f32[64,256]{1,0:T(8,128)S(1)} %get-tuple-element.52.own), channel_id=1, source_target_pairs={{0,192},{1,193},{2,194},{3,195},{4,196},{5,197},{6,198},{7,199},{8... | collective-permute-start | bytes 196616 | tf_op jit(solution)/shard_map/right_sum/ppermute | solution.py:30
  72.0 2.4 %cholesky.1 = (f32[64,64]{1,0:T(8,128)S(1)}, f32[64,128]{1,0:T(8,128)}, bf16[128,192]{1,0:T(8,128)(2,1)S(1)}) custom-call(f32[16,256]{1,0:T(8,128)S(1)} %get-tuple-element.50.packed, f32[64,128]{1,0:T(8,128)S(1)} %add_add_fusion.left), custom_call_target="tpu_custom_call" | custom-call | tf_op jit(solution)/shard_map/cholesky/pallas_call | solution.py:326
  75.6 15.9 %all_to_all.5.refs_2_.refs_4_ = f32[16,64,256]{2,1,0:T(8,128)S(1)} all-to-all(f32[16,64,256]{2,1,0:T(8,128)S(1)} %right_factor.1), channel_id=1, replica_groups=mesh['zlo'=4,'y'=4,'x'=4,'zhi'=2,'core'=2] {'x','y'}, dimensions={0} | all-to-all | bytes 2097152 | tf_op jit(solution)/shard_map/right_factor/all_to_all | solution.py:274
  91.6 6.7 %collective-permute-start.33 = (f32[16,64,256]{2,1,0:T(8,128)S(1)}, f32[16,64,256]{2,1,0:T(8,128)S(1)}, u32[]{:S(2)}, u32[]{:S(2)}) collective-permute-start(f32[16,64,256]{2,1,0:T(8,128)S(1)} %all_to_all.5.refs_2_.refs_4_), channel_id=1, source_target_pairs={{0,1},{1,0},{2,3},{3,2},{4,5},{5,4},{6,7},{7,6},{8,9},{9,8},{10,11... | collective-permute-start | bytes 3145736 | tf_op jit(solution)/shard_map/right_factor/ppermute | solution.py:30
  98.2 1.7 %error.2.refs_0_ = f32[1,128,8192]{2,1,0:T(8,128)} custom-call(f32[128,8192]{1,0:T(8,128)S(1)} %add_bitcast_fusion.refs_5_.refs_7_.refs_6_.merged.refs_0_.refs_1_, bf16[128,192]{1,0:T(8,128)(2,1)S(1)} %get-tuple-element.51.refs_1_.refs_2_, f32[16,64,256]{2,1,0:T(8,128)S(1)} %all_to_all.5.refs_2_.refs_4_), custom_call_target="tpu_custom_call" | custom-call | tf_op jit(solution)/shard_map/error/pallas_call | solution.py:263
  100.5 1.7 %error.3 = (f32[1,128,8192]{2,1,0:T(8,128)}, f32[64,512]{1,0:T(8,128)}) custom-call(f32[1,128,8192]{2,1,0:T(8,128)} %error.2.refs_0_, f32[128,8192]{1,0:T(8,128)S(1)} %add_bitcast_fusion.refs_5_.refs_7_.refs_6_.merged.refs_0_.refs_1_, bf16[128,192]{1,0:T(8,128)(2,1)S(1)} %get-tuple-element.51.refs_1_.refs_2_, ...), custom_call_target="tpu_custom_call", output_to_operand_aliasing={{0}: (0, {})} | custom-call | tf_op jit(solution)/shard_map/error/pallas_call | solution.py:263
  (56 shorter events, 11.9 us)
Async XLA Ops:
  0.6 13.8 %collective-permute-start.3 = (f32[64,512]{1,0:T(8,128)}, f32[64,512]{1,0:T(8,128)S(1)}, u32[]{:S(2)}, u32[]{:S(2)}) collective-permute-start(f32[64,512]{1,0:T(8,128)} %bitcast.5), channel_id=1, source_target_pairs={{0,130},{1,131},{2,128},{3,129},{4,134},{5,135},{6,132},{7,133},{8... | collective-permute-start | bytes 393224 | tf_op jit(solution)/shard_map/gather_factor/ppermute | solution.py:30
  7.6 10.8 %collective-permute-start.2 = (f32[64,512]{1,0:T(8,128)}, f32[64,512]{1,0:T(8,128)S(1)}, u32[]{:S(2)}, u32[]{:S(2)}) collective-permute-start(f32[64,512]{1,0:T(8,128)} %bitcast.6), channel_id=1, source_target_pairs={{0,8},{1,9},{2,10},{3,11},{4,12},{5,13},{6,14},{7,15},{8,0},{9,1},... | collective-permute-start | bytes 393224 | tf_op jit(solution)/shard_map/gather_factor/ppermute | solution.py:30
  10.3 8.1 %collective-permute-start.1 = (f32[64,512]{1,0:T(8,128)}, f32[64,512]{1,0:T(8,128)S(1)}, u32[]{:S(2)}, u32[]{:S(2)}) collective-permute-start(f32[64,512]{1,0:T(8,128)} %bitcast.7), channel_id=1, source_target_pairs={{0,12},{1,13},{2,14},{3,15},{4,8},{5,9},{6,10},{7,11},{8,4},{9,5},... | collective-permute-start | bytes 393224 | tf_op jit(solution)/shard_map/gather_factor/ppermute | solution.py:30
  11.2 7.2 %collective-permute-start = (f32[64,512]{1,0:T(8,128)}, f32[64,512]{1,0:T(8,128)S(1)}, u32[]{:S(2)}, u32[]{:S(2)}) collective-permute-start(f32[64,512]{1,0:T(8,128)} %bitcast.8), channel_id=1, source_target_pairs={{0,4},{1,5},{2,6},{3,7},{4,0},{5,1},{6,2},{7,3},{8,12},{9,13},{10,... | collective-permute-start | bytes 393224 | tf_op jit(solution)/shard_map/gather_factor/ppermute | solution.py:30
  14.5 5.7 %collective-permute-start.4 = (f32[64,512]{1,0:T(8,128)S(1)}, f32[64,512]{1,0:T(8,128)S(1)}, u32[]{:S(2)}, u32[]{:S(2)}) collective-permute-start(f32[64,512]{1,0:T(8,128)S(1)} %collective-permute-done.3.refs_4_), channel_id=1, source_target_pairs={{0,8},{1,9},{2,10},{3,11},{4,12},{5,13},{6,14},{7,15},{8,0},{9,1},... | collective-permute-start | bytes 393224 | tf_op jit(solution)/shard_map/gather_factor/ppermute | solution.py:30
  17.5 5.7 %collective-permute-start.11 = (f32[64,512]{1,0:T(8,128)S(1)}, f32[64,512]{1,0:T(8,128)S(1)}, u32[]{:S(2)}, u32[]{:S(2)}) collective-permute-start(f32[64,512]{1,0:T(8,128)S(1)} %collective-permute-done.3.refs_4_), channel_id=1, source_target_pairs={{0,12},{1,13},{2,14},{3,15},{4,8},{5,9},{6,10},{7,11},{8,4},{9,5},... | collective-permute-start | bytes 393224 | tf_op jit(solution)/shard_map/gather_factor/ppermute | solution.py:30
  18.4 7.4 %collective-permute-start.10 = (f32[64,512]{1,0:T(8,128)S(1)}, f32[64,512]{1,0:T(8,128)S(1)}, u32[]{:S(2)}, u32[]{:S(2)}) collective-permute-start(f32[64,512]{1,0:T(8,128)S(1)} %collective-permute-done.3.refs_4_), channel_id=1, source_target_pairs={{0,4},{1,5},{2,6},{3,7},{4,0},{5,1},{6,2},{7,3},{8,12},{9,13},{10,... | collective-permute-start | bytes 393224 | tf_op jit(solution)/shard_map/gather_factor/ppermute | solution.py:30
  20.1 5.7 %collective-permute-start.5 = (f32[64,512]{1,0:T(8,128)S(1)}, f32[64,512]{1,0:T(8,128)S(1)}, u32[]{:S(2)}, u32[]{:S(2)}) collective-permute-start(f32[64,512]{1,0:T(8,128)S(1)} %collective-permute-done.refs_0_), channel_id=1, source_target_pairs={{0,1},{1,0},{2,3},{3,2},{4,5},{5,4},{6,7},{7,6},{8,9},{9,8},{10,11... | collective-permute-start | bytes 393224 | tf_op jit(solution)/shard_map/left_sum/ppermute | solution.py:30
  22.7 3.7 %collective-permute-start.6 = (f32[64,512]{1,0:T(8,128)S(1)}, f32[64,512]{1,0:T(8,128)S(1)}, u32[]{:S(2)}, u32[]{:S(2)}) collective-permute-start(f32[64,512]{1,0:T(8,128)S(1)} %collective-permute-done.1.refs_1_), channel_id=1, source_target_pairs={{0,1},{1,0},{2,3},{3,2},{4,5},{5,4},{6,7},{7,6},{8,9},{9,8},{10,11... | collective-permute-start | bytes 393224 | tf_op jit(solution)/shard_map/left_sum/ppermute | solution.py:30
  22.7 3.8 %collective-permute-start.7 = (f32[64,512]{1,0:T(8,128)S(1)}, f32[64,512]{1,0:T(8,128)S(1)}, u32[]{:S(2)}, u32[]{:S(2)}) collective-permute-start(f32[64,512]{1,0:T(8,128)S(1)} %collective-permute-done.2.refs_2_), channel_id=1, source_target_pairs={{0,1},{1,0},{2,3},{3,2},{4,5},{5,4},{6,7},{7,6},{8,9},{9,8},{10,11... | collective-permute-start | bytes 393224 | tf_op jit(solution)/shard_map/left_sum/ppermute | solution.py:30
  23.3 3.6 %collective-permute-start.8 = (f32[64,512]{1,0:T(8,128)S(1)}, f32[64,512]{1,0:T(8,128)S(1)}, u32[]{:S(2)}, u32[]{:S(2)}) collective-permute-start(f32[64,512]{1,0:T(8,128)S(1)} %bitcast.10), channel_id=1, source_target_pairs={{0,1},{1,0},{2,3},{3,2},{4,5},{5,4},{6,7},{7,6},{8,9},{9,8},{10,11... | collective-permute-start | bytes 393224 | tf_op jit(solution)/shard_map/left_sum/ppermute | solution.py:30
  25.8 2.0 %collective-permute-start.13 = (f32[64,512]{1,0:T(8,128)S(1)}, f32[64,512]{1,0:T(8,128)S(1)}, u32[]{:S(2)}, u32[]{:S(2)}) collective-permute-start(f32[64,512]{1,0:T(8,128)S(1)} %collective-permute-done.11.refs_2_), channel_id=1, source_target_pairs={{0,1},{1,0},{2,3},{3,2},{4,5},{5,4},{6,7},{7,6},{8,9},{9,8},{10,11... | collective-permute-start | bytes 393224 | tf_op jit(solution)/shard_map/left_sum/ppermute | solution.py:30
  26.3 1.5 %collective-permute-start.12 = (f32[64,512]{1,0:T(8,128)S(1)}, f32[64,512]{1,0:T(8,128)S(1)}, u32[]{:S(2)}, u32[]{:S(2)}) collective-permute-start(f32[64,512]{1,0:T(8,128)S(1)} %collective-permute-done.10.refs_1_), channel_id=1, source_target_pairs={{0,1},{1,0},{2,3},{3,2},{4,5},{5,4},{6,7},{7,6},{8,9},{9,8},{10,11... | collective-permute-start | bytes 393224 | tf_op jit(solution)/shard_map/left_sum/ppermute | solution.py:30
  28.5 4.4 %collective-permute-start.17 = (f32[64,128]{1,0:T(8,128)S(1)}, f32[64,128]{1,0:T(8,128)S(1)}, u32[]{:S(2)}, u32[]{:S(2)}) collective-permute-start(f32[64,128]{1,0:T(8,128)S(1)} %left_sum.5), channel_id=1, source_target_pairs={{0,32},{1,33},{2,34},{3,35},{4,36},{5,37},{6,38},{7,39},{8,40},{9,... | collective-permute-start | bytes 98312 | tf_op jit(solution)/shard_map/left_sum/ppermute | solution.py:30
  31.5 4.0 %collective-permute-start.16 = (f32[64,128]{1,0:T(8,128)S(1)}, f32[64,128]{1,0:T(8,128)S(1)}, u32[]{:S(2)}, u32[]{:S(2)}) collective-permute-start(f32[64,128]{1,0:T(8,128)S(1)} %left_sum.5), channel_id=1, source_target_pairs={{0,48},{1,49},{2,50},{3,51},{4,52},{5,53},{6,54},{7,55},{8,56},{9,... | collective-permute-start | bytes 98312 | tf_op jit(solution)/shard_map/left_sum/ppermute | solution.py:30
  32.2 3.2 %collective-permute-start.15 = (f32[64,128]{1,0:T(8,128)S(1)}, f32[64,128]{1,0:T(8,128)S(1)}, u32[]{:S(2)}, u32[]{:S(2)}) collective-permute-start(f32[64,128]{1,0:T(8,128)S(1)} %left_sum.5), channel_id=1, source_target_pairs={{0,16},{1,17},{2,18},{3,19},{4,20},{5,21},{6,22},{7,23},{8,24},{9,... | collective-permute-start | bytes 98312 | tf_op jit(solution)/shard_map/left_sum/ppermute | solution.py:30
  35.5 3.9 %collective-permute-start.20 = (f32[64,128]{1,0:T(8,128)S(1)}, f32[64,128]{1,0:T(8,128)S(1)}, u32[]{:S(2)}, u32[]{:S(2)}) collective-permute-start(f32[64,128]{1,0:T(8,128)S(1)} %add_add_fusion.1), channel_id=1, source_target_pairs={{0,128},{1,129},{2,130},{3,131},{4,132},{5,133},{6,134},{7,135},{8... | collective-permute-start | bytes 98312 | tf_op jit(solution)/shard_map/left_sum/ppermute | solution.py:30
  36.9 4.7 %collective-permute-start.19 = (f32[64,128]{1,0:T(8,128)S(1)}, f32[64,128]{1,0:T(8,128)S(1)}, u32[]{:S(2)}, u32[]{:S(2)}) collective-permute-start(f32[64,128]{1,0:T(8,128)S(1)} %add_add_fusion.1), channel_id=1, source_target_pairs={{0,192},{1,193},{2,194},{3,195},{4,196},{5,197},{6,198},{7,199},{8... | collective-permute-start | bytes 98312 | tf_op jit(solution)/shard_map/left_sum/ppermute | solution.py:30
  38.5 3.7 %collective-permute-start.18 = (f32[64,128]{1,0:T(8,128)S(1)}, f32[64,128]{1,0:T(8,128)S(1)}, u32[]{:S(2)}, u32[]{:S(2)}) collective-permute-start(f32[64,128]{1,0:T(8,128)S(1)} %add_add_fusion.1), channel_id=1, source_target_pairs={{0,64},{1,65},{2,66},{3,67},{4,68},{5,69},{6,70},{7,71},{8,72},{9,... | collective-permute-start | bytes 98312 | tf_op jit(solution)/shard_map/left_sum/ppermute | solution.py:30
  42.8 4.4 %collective-permute-start.22 = (f32[2,272,256]{2,1,0:T(8,128)S(1)}, f32[2,272,256]{2,1,0:T(8,128)S(1)}, u32[]{:S(2)}, u32[]{:S(2)}) collective-permute-start(f32[2,272,256]{2,1,0:T(8,128)S(1)} %get-tuple-element.42), channel_id=1, source_target_pairs={{0,1},{1,0},{2,3},{3,2},{4,5},{5,4},{6,7},{7,6},{8,9},{9,8},{10,11... | collective-permute-start | bytes 1671176 | tf_op jit(solution)/shard_map/right_sum/ppermute | solution.py:30
  45.6 3.7 %collective-permute-start.21 = (f32[2,272,256]{2,1,0:T(8,128)S(1)}, f32[2,272,256]{2,1,0:T(8,128)S(1)}, u32[]{:S(2)}, u32[]{:S(2)}) collective-permute-start(f32[2,272,256]{2,1,0:T(8,128)S(1)} %get-tuple-element.39), channel_id=1, source_target_pairs={{0,1},{1,0},{2,3},{3,2},{4,5},{5,4},{6,7},{7,6},{8,9},{9,8},{10,11... | collective-permute-start | bytes 1671176 | tf_op jit(solution)/shard_map/right_sum/ppermute | solution.py:30
  47.3 7.3 %collective-permute-start.23 = (f32[272,256]{1,0:T(8,128)S(1)}, f32[272,256]{1,0:T(8,128)S(1)}, u32[]{:S(2)}, u32[]{:S(2)}) collective-permute-start(f32[272,256]{1,0:T(8,128)S(1)} %get-tuple-element.43), channel_id=1, source_target_pairs={{0,8},{1,33},{2,10},{3,35},{4,12},{5,37},{6,14},{7,39},{8,0},{9,41... | collective-permute-start | bytes 835592 | tf_op jit(solution)/shard_map/right_sum/ppermute | solution.py:30
  48.6 8.9 %collective-permute-start.24 = (f32[272,256]{1,0:T(8,128)S(1)}, f32[272,256]{1,0:T(8,128)S(1)}, u32[]{:S(2)}, u32[]{:S(2)}) collective-permute-start(f32[272,256]{1,0:T(8,128)S(1)} %get-tuple-element.44), channel_id=1, source_target_pairs={{0,12},{1,49},{2,14},{3,51},{4,8},{5,53},{6,10},{7,55},{8,4},{9,57... | collective-permute-start | bytes 835592 | tf_op jit(solution)/shard_map/right_sum/ppermute | solution.py:30
  49.4 8.2 %collective-permute-start.25 = (f32[272,256]{1,0:T(8,128)S(1)}, f32[272,256]{1,0:T(8,128)S(1)}, u32[]{:S(2)}, u32[]{:S(2)}) collective-permute-start(f32[272,256]{1,0:T(8,128)S(1)} %get-tuple-element.45), channel_id=1, source_target_pairs={{0,4},{1,17},{2,6},{3,19},{4,0},{5,21},{6,2},{7,23},{8,12},{9,25},... | collective-permute-start | bytes 835592 | tf_op jit(solution)/shard_map/right_sum/ppermute | solution.py:30
  57.6 4.9 %collective-permute-start.26 = (f32[80,256]{1,0:T(8,128)S(1)}, f32[80,256]{1,0:T(8,128)S(1)}, u32[]{:S(2)}, u32[]{:S(2)}) collective-permute-start(f32[80,256]{1,0:T(8,128)S(1)} %get-tuple-element.47), channel_id=1, source_target_pairs={{0,32},{1,9},{2,34},{3,11},{4,36},{5,13},{6,38},{7,15},{8,40},{9,1... | collective-permute-start | bytes 245768 | tf_op jit(solution)/shard_map/right_sum/ppermute | solution.py:30
  58.8 4.9 %collective-permute-start.27 = (f32[80,256]{1,0:T(8,128)S(1)}, f32[80,256]{1,0:T(8,128)S(1)}, u32[]{:S(2)}, u32[]{:S(2)}) collective-permute-start(f32[80,256]{1,0:T(8,128)S(1)} %get-tuple-element.48), channel_id=1, source_target_pairs={{0,48},{1,13},{2,50},{3,15},{4,52},{5,9},{6,54},{7,11},{8,56},{9,5... | collective-permute-start | bytes 245768 | tf_op jit(solution)/shard_map/right_sum/ppermute | solution.py:30
  60.1 3.6 %collective-permute-start.28 = (f32[80,256]{1,0:T(8,128)S(1)}, f32[80,256]{1,0:T(8,128)S(1)}, u32[]{:S(2)}, u32[]{:S(2)}) collective-permute-start(f32[80,256]{1,0:T(8,128)S(1)} %get-tuple-element.49), channel_id=1, source_target_pairs={{0,16},{1,5},{2,18},{3,7},{4,20},{5,1},{6,22},{7,3},{8,24},{9,13},... | collective-permute-start | bytes 245768 | tf_op jit(solution)/shard_map/right_sum/ppermute | solution.py:30
  63.7 5.5 %collective-permute-start.29 = (f32[80,256]{1,0:T(8,128)S(1)}, f32[80,256]{1,0:T(8,128)S(1)}, u32[]{:S(2)}, u32[]{:S(2)}) collective-permute-start(f32[80,256]{1,0:T(8,128)S(1)} %right_sum.12.own), channel_id=1, source_target_pairs={{0,130},{1,131},{2,128},{3,129},{4,134},{5,135},{6,132},{7,133},{8... | collective-permute-start | bytes 245768 | tf_op jit(solution)/shard_map/right_sum/ppermute | solution.py:30
  69.2 5.2 %collective-permute-start.32 = (f32[64,256]{1,0:T(8,128)S(1)}, f32[64,256]{1,0:T(8,128)S(1)}, u32[]{:S(2)}, u32[]{:S(2)}) collective-permute-start(f32[64,256]{1,0:T(8,128)S(1)} %get-tuple-element.52.own), channel_id=1, source_target_pairs={{0,128},{1,129},{2,130},{3,131},{4,132},{5,133},{6,134},{7,135},{8... | collective-permute-start | bytes 196616 | tf_op jit(solution)/shard_map/right_sum/ppermute | solution.py:30
  69.9 5.1 %collective-permute-start.31 = (f32[64,256]{1,0:T(8,128)S(1)}, f32[64,256]{1,0:T(8,128)S(1)}, u32[]{:S(2)}, u32[]{:S(2)}) collective-permute-start(f32[64,256]{1,0:T(8,128)S(1)} %get-tuple-element.52.own), channel_id=1, source_target_pairs={{0,192},{1,193},{2,194},{3,195},{4,196},{5,197},{6,198},{7,199},{8... | collective-permute-start | bytes 196616 | tf_op jit(solution)/shard_map/right_sum/ppermute | solution.py:30
  71.5 3.8 %collective-permute-start.30 = (f32[64,256]{1,0:T(8,128)S(1)}, f32[64,256]{1,0:T(8,128)S(1)}, u32[]{:S(2)}, u32[]{:S(2)}) collective-permute-start(f32[64,256]{1,0:T(8,128)S(1)} %get-tuple-element.52.own), channel_id=1, source_target_pairs={{0,64},{1,65},{2,66},{3,67},{4,68},{5,69},{6,70},{7,71},{8,72},{9,... | collective-permute-start | bytes 196616 | tf_op jit(solution)/shard_map/right_sum/ppermute | solution.py:30
  91.6 9.0 %collective-permute-start.33 = (f32[16,64,256]{2,1,0:T(8,128)S(1)}, f32[16,64,256]{2,1,0:T(8,128)S(1)}, u32[]{:S(2)}, u32[]{:S(2)}) collective-permute-start(f32[16,64,256]{2,1,0:T(8,128)S(1)} %all_to_all.5.refs_2_.refs_4_), channel_id=1, source_target_pairs={{0,1},{1,0},{2,3},{3,2},{4,5},{5,4},{6,7},{7,6},{8,9},{9,8},{10,11... | collective-permute-start | bytes 3145736 | tf_op jit(solution)/shard_map/right_factor/ppermute | solution.py:30
  (3 other events, 20.6 us)

commit v4 on v3

--- a/solution.py
+++ b/solution.py
@@ -42,8 +42,11 @@
     return [shift(value, **{axis: step}) for step in STEPS]
 
 
-def total(value, axis):
-    one, three, two = ring(value, axis)
+def total(value, on_y):
+    one, three, two = [
+        moved(value, lambda core: (0, step, 0, 0, 0) if core == on_y else (step, 0, 0, 0, 0))
+        for step in STEPS
+    ]
     return (value + one) + (three + two)
 
 
@@ -306,7 +309,7 @@
         slots = [(s, 1) for s in STEPS]
         slots = [slot + (0,) for slot in slots[:2]] + [slot + (1,) for slot in slots]
         part = left_part(slots, merged, second[:2] + other, part)
-        left_sum = total(total(part, "y"), "zlo")
+        left_sum = total(total(part, 1), 0)
     with jax.named_scope("right_sum"):
         sent = cross_part(1, merged, left_sum)
         received = [shift(value, core=1) for value in sent]

time: 102 us -> 102 us (level)
  transfers between devices with their start and end apart: 34 -> 34, of which waited for: 17 -> 16; matrix products, arithmetic and copies ran while one was open for 3% -> 3% of each run, Pallas kernels for 6% -> 6%
where the time goes in v4:
time: 102 us
  starting transfers between devices  48.4 us (47%)
  waiting for transfers between devices  24.7 us (24%)
  blocking collectives  15.9 us (16%)
  Pallas kernels  9.1 us (9%)
  other arithmetic  3.28 us (3%)
    ppermute x34, starting transfers between devices, moved(): return lax.ppermute(value, AXES, pairs)  48.4 us
    ppermute x34, waiting for transfers between devices, moved(): return lax.ppermute(value, AXES, pairs)  24.7 us
    all_to_all x1, blocking collectives, exchange(): lax.all_to_all(value, ('x', 'y'), split_axis=0, concat_axis=0, tiled=True)  15.9 us
    pallas_call x2, Pallas kernels, error_part(): call(functools.partial(error_kernel, int(last)), out_shape, in_specs=([an...  3.32 us
    add x1, other arithmetic, body(): merged = gradient[0].astype(F32) + error_feed[0]  3.26 us
    pallas_call x1, Pallas kernels, body(): call(factor_kernel, [jax.ShapeDtypeStruct((RANK, RANK), F32), jax.ShapeDt...  2.43 us
  transfers between devices with their start and end apart: 34, of which 16 were waited for; matrix products, arithmetic and copies ran while one was open for 3% of the time, Pallas kernels for 6%

profile of v4, /device:TPU:1, one launch (start us, length us, event | category | flops | bytes accessed | tf_op | source)
XLA Modules:
  0.0 102.3 jit_solution(9617483904494006493)
XLA Ops:
  0.6 6.9 %collective-permute-start.3 = (f32[64,512]{1,0:T(8,128)}, f32[64,512]{1,0:T(8,128)S(1)}, u32[]{:S(2)}, u32[]{:S(2)}) collective-permute-start(f32[64,512]{1,0:T(8,128)} %bitcast.5), channel_id=1, source_target_pairs={{0,130},{1,131},{2,128},{3,129},{4,134},{5,135},{6,132},{7,133},{8... | collective-permute-start | bytes 393224 | tf_op jit(solution)/shard_map/gather_factor/ppermute | solution.py:30
  7.6 2.7 %collective-permute-start.2 = (f32[64,512]{1,0:T(8,128)}, f32[64,512]{1,0:T(8,128)S(1)}, u32[]{:S(2)}, u32[]{:S(2)}) collective-permute-start(f32[64,512]{1,0:T(8,128)} %bitcast.6), channel_id=1, source_target_pairs={{0,8},{1,9},{2,10},{3,11},{4,12},{5,13},{6,14},{7,15},{8,0},{9,1},... | collective-permute-start | bytes 393224 | tf_op jit(solution)/shard_map/gather_factor/ppermute | solution.py:30
  10.3 0.9 collective-permute-start.1
  11.2 3.3 %add_bitcast_fusion.refs_5_.refs_7_.refs_6_.merged.refs_0_.refs_1_ = f32[128,8192]{1,0:T(8,128)S(1)} fusion(f32[1,128,8192]{2,1,0:T(8,128)} %param.4, bf16[1,128,8192]{2,1,0:T(8,128)(2,1)} %param.3), kind=kLoop, calls=%fused_computation | loop fusion | flops 2097152 | bytes 10485760 | tf_op jit(solution)/shard_map/add | solution.py:293
  14.5 3.1 %collective-permute-start.4 = (f32[64,512]{1,0:T(8,128)S(1)}, f32[64,512]{1,0:T(8,128)S(1)}, u32[]{:S(2)}, u32[]{:S(2)}) collective-permute-start(f32[64,512]{1,0:T(8,128)S(1)} %collective-permute-done.3.refs_4_), channel_id=1, source_target_pairs={{0,8},{1,9},{2,10},{3,11},{4,12},{5,13},{6,14},{7,15},{8,0},{9,1},... | collective-permute-start | bytes 393224 | tf_op jit(solution)/shard_map/gather_factor/ppermute | solution.py:30
  17.5 0.9 collective-permute-start.11
  19.0 1.1 %collective-permute-done.4.refs_6_ = f32[64,512]{1,0:T(8,128)S(1)} collective-permute-done((f32[64,512]{1,0:T(8,128)S(1)}, f32[64,512]{1,0:T(8,128)S(1)}, u32[]{:S(2)}, u32[]{:S(2)}) %collective-permute-start.4) | collective-permute-done | bytes 131104 | tf_op jit(solution)/shard_map/gather_factor/ppermute | solution.py:30
  20.1 2.5 %collective-permute-start.5 = (f32[64,512]{1,0:T(8,128)S(1)}, f32[64,512]{1,0:T(8,128)S(1)}, u32[]{:S(2)}, u32[]{:S(2)}) collective-permute-start(f32[64,512]{1,0:T(8,128)S(1)} %collective-permute-done.refs_0_), channel_id=1, source_target_pairs={{0,1},{1,0},{2,3},{3,2},{4,5},{5,4},{6,7},{7,6},{8,9},{9,8},{10,11... | collective-permute-start | bytes 393224 | tf_op jit(solution)/shard_map/left_sum/ppermute | solution.py:30
  23.3 2.5 %collective-permute-start.8 = (f32[64,512]{1,0:T(8,128)S(1)}, f32[64,512]{1,0:T(8,128)S(1)}, u32[]{:S(2)}, u32[]{:S(2)}) collective-permute-start(f32[64,512]{1,0:T(8,128)S(1)} %bitcast.10), channel_id=1, source_target_pairs={{0,1},{1,0},{2,3},{3,2},{4,5},{5,4},{6,7},{7,6},{8,9},{9,8},{10,11... | collective-permute-start | bytes 393224 | tf_op jit(solution)/shard_map/left_sum/ppermute | solution.py:30
  28.5 3.0 %collective-permute-start.17 = (f32[64,128]{1,0:T(8,128)S(1)}, f32[64,128]{1,0:T(8,128)S(1)}, u32[]{:S(2)}, u32[]{:S(2)}) collective-permute-start(f32[64,128]{1,0:T(8,128)S(1)} %left_sum.5), channel_id=1, source_target_pairs={{0,128},{1,33},{2,130},{3,35},{4,132},{5,37},{6,134},{7,39},{8,136... | collective-permute-start | bytes 98312 | tf_op jit(solution)/shard_map/left_sum/ppermute | solution.py:30
  32.8 2.8 %collective-permute-done.16 = f32[64,128]{1,0:T(8,128)S(1)} collective-permute-done((f32[64,128]{1,0:T(8,128)S(1)}, f32[64,128]{1,0:T(8,128)S(1)}, u32[]{:S(2)}, u32[]{:S(2)}) %collective-permute-start.16) | collective-permute-done | bytes 32800 | tf_op jit(solution)/shard_map/left_sum/ppermute | solution.py:30
  35.7 1.2 %collective-permute-start.20 = (f32[64,128]{1,0:T(8,128)S(1)}, f32[64,128]{1,0:T(8,128)S(1)}, u32[]{:S(2)}, u32[]{:S(2)}) collective-permute-start(f32[64,128]{1,0:T(8,128)S(1)} %add_add_fusion.1), channel_id=1, source_target_pairs={{0,32},{1,129},{2,34},{3,131},{4,36},{5,133},{6,38},{7,135},{8,40}... | collective-permute-start | bytes 98312 | tf_op jit(solution)/shard_map/left_sum/ppermute | solution.py:30
  36.9 1.6 %collective-permute-start.19 = (f32[64,128]{1,0:T(8,128)S(1)}, f32[64,128]{1,0:T(8,128)S(1)}, u32[]{:S(2)}, u32[]{:S(2)}) collective-permute-start(f32[64,128]{1,0:T(8,128)S(1)} %add_add_fusion.1), channel_id=1, source_target_pairs={{0,48},{1,193},{2,50},{3,195},{4,52},{5,197},{6,54},{7,199},{8,56}... | collective-permute-start | bytes 98312 | tf_op jit(solution)/shard_map/left_sum/ppermute | solution.py:30
  38.6 1.0 %collective-permute-done.20 = f32[64,128]{1,0:T(8,128)S(1)} collective-permute-done((f32[64,128]{1,0:T(8,128)S(1)}, f32[64,128]{1,0:T(8,128)S(1)}, u32[]{:S(2)}, u32[]{:S(2)}) %collective-permute-start.20) | collective-permute-done | bytes 32800 | tf_op jit(solution)/shard_map/left_sum/ppermute | solution.py:30
  39.6 2.1 %collective-permute-done.19 = f32[64,128]{1,0:T(8,128)S(1)} collective-permute-done((f32[64,128]{1,0:T(8,128)S(1)}, f32[64,128]{1,0:T(8,128)S(1)}, u32[]{:S(2)}, u32[]{:S(2)}) %collective-permute-start.19) | collective-permute-done | bytes 32800 | tf_op jit(solution)/shard_map/left_sum/ppermute | solution.py:30
  42.2 3.4 %collective-permute-start.22 = (f32[2,272,256]{2,1,0:T(8,128)S(1)}, f32[2,272,256]{2,1,0:T(8,128)S(1)}, u32[]{:S(2)}, u32[]{:S(2)}) collective-permute-start(f32[2,272,256]{2,1,0:T(8,128)S(1)} %get-tuple-element.42), channel_id=1, source_target_pairs={{0,1},{1,0},{2,3},{3,2},{4,5},{5,4},{6,7},{7,6},{8,9},{9,8},{10,11... | collective-permute-start | bytes 1671176 | tf_op jit(solution)/shard_map/right_sum/ppermute | solution.py:30
  46.2 1.0 collective-permute-done.22.received
  47.3 1.3 %collective-permute-start.23 = (f32[272,256]{1,0:T(8,128)S(1)}, f32[272,256]{1,0:T(8,128)S(1)}, u32[]{:S(2)}, u32[]{:S(2)}) collective-permute-start(f32[272,256]{1,0:T(8,128)S(1)} %get-tuple-element.43), channel_id=1, source_target_pairs={{0,8},{1,33},{2,10},{3,35},{4,12},{5,37},{6,14},{7,39},{8,0},{9,41... | collective-permute-start | bytes 835592 | tf_op jit(solution)/shard_map/right_sum/ppermute | solution.py:30
  50.2 4.4 %collective-permute-done.23.two = f32[272,256]{1,0:T(8,128)S(1)} collective-permute-done((f32[272,256]{1,0:T(8,128)S(1)}, f32[272,256]{1,0:T(8,128)S(1)}, u32[]{:S(2)}, u32[]{:S(2)}) %collective-permute-start.23) | collective-permute-done | bytes 278560 | tf_op jit(solution)/shard_map/right_sum/ppermute | solution.py:30
  54.6 2.9 %collective-permute-done.24.three = f32[272,256]{1,0:T(8,128)S(1)} collective-permute-done((f32[272,256]{1,0:T(8,128)S(1)}, f32[272,256]{1,0:T(8,128)S(1)}, u32[]{:S(2)}, u32[]{:S(2)}) %collective-permute-start.24) | collective-permute-done | bytes 278560 | tf_op jit(solution)/shard_map/right_sum/ppermute | solution.py:30
  57.6 1.2 %collective-permute-start.26 = (f32[80,256]{1,0:T(8,128)S(1)}, f32[80,256]{1,0:T(8,128)S(1)}, u32[]{:S(2)}, u32[]{:S(2)}) collective-permute-start(f32[80,256]{1,0:T(8,128)S(1)} %get-tuple-element.47), channel_id=1, source_target_pairs={{0,32},{1,9},{2,34},{3,11},{4,36},{5,13},{6,38},{7,15},{8,40},{9,1... | collective-permute-start | bytes 245768 | tf_op jit(solution)/shard_map/right_sum/ppermute | solution.py:30
  58.8 1.3 %collective-permute-start.27 = (f32[80,256]{1,0:T(8,128)S(1)}, f32[80,256]{1,0:T(8,128)S(1)}, u32[]{:S(2)}, u32[]{:S(2)}) collective-permute-start(f32[80,256]{1,0:T(8,128)S(1)} %get-tuple-element.48), channel_id=1, source_target_pairs={{0,48},{1,13},{2,50},{3,15},{4,52},{5,9},{6,54},{7,11},{8,56},{9,5... | collective-permute-start | bytes 245768 | tf_op jit(solution)/shard_map/right_sum/ppermute | solution.py:30
  60.3 2.2 %collective-permute-done.26.two = f32[80,256]{1,0:T(8,128)S(1)} collective-permute-done((f32[80,256]{1,0:T(8,128)S(1)}, f32[80,256]{1,0:T(8,128)S(1)}, u32[]{:S(2)}, u32[]{:S(2)}) %collective-permute-start.26) | collective-permute-done | bytes 81952 | tf_op jit(solution)/shard_map/right_sum/ppermute | solution.py:30
  62.5 1.2 %collective-permute-done.27.three = f32[80,256]{1,0:T(8,128)S(1)} collective-permute-done((f32[80,256]{1,0:T(8,128)S(1)}, f32[80,256]{1,0:T(8,128)S(1)}, u32[]{:S(2)}, u32[]{:S(2)}) %collective-permute-start.27) | collective-permute-done | bytes 81952 | tf_op jit(solution)/shard_map/right_sum/ppermute | solution.py:30
  63.7 2.2 %collective-permute-start.29 = (f32[80,256]{1,0:T(8,128)S(1)}, f32[80,256]{1,0:T(8,128)S(1)}, u32[]{:S(2)}, u32[]{:S(2)}) collective-permute-start(f32[80,256]{1,0:T(8,128)S(1)} %right_sum.12.own), channel_id=1, source_target_pairs={{0,130},{1,131},{2,128},{3,129},{4,134},{5,135},{6,132},{7,133},{8... | collective-permute-start | bytes 245768 | tf_op jit(solution)/shard_map/right_sum/ppermute | solution.py:30
  65.9 3.3 %collective-permute-done.29.other = f32[80,256]{1,0:T(8,128)S(1)} collective-permute-done((f32[80,256]{1,0:T(8,128)S(1)}, f32[80,256]{1,0:T(8,128)S(1)}, u32[]{:S(2)}, u32[]{:S(2)}) %collective-permute-start.29) | collective-permute-done | bytes 81952 | tf_op jit(solution)/shard_map/right_sum/ppermute | solution.py:30
  69.9 1.6 %collective-permute-start.31 = (f32[64,256]{1,0:T(8,128)S(1)}, f32[64,256]{1,0:T(8,128)S(1)}, u32[]{:S(2)}, u32[]{:S(2)}) collective-permute-start(f32[64,256]{1,0:T(8,128)S(1)} %get-tuple-element.52.own), channel_id=1, source_target_pairs={{0,192},{1,193},{2,194},{3,195},{4,196},{5,197},{6,198},{7,199},{8... | collective-permute-start | bytes 196616 | tf_op jit(solution)/shard_map/right_sum/ppermute | solution.py:30
  72.0 2.4 %cholesky.1 = (f32[64,64]{1,0:T(8,128)S(1)}, f32[64,128]{1,0:T(8,128)}, bf16[128,192]{1,0:T(8,128)(2,1)S(1)}) custom-call(f32[16,256]{1,0:T(8,128)S(1)} %get-tuple-element.50.packed, f32[64,128]{1,0:T(8,128)S(1)} %add_add_fusion.left), custom_call_target="tpu_custom_call" | custom-call | tf_op jit(solution)/shard_map/cholesky/pallas_call | solution.py:329
  75.6 15.9 %all_to_all.5.refs_2_.refs_4_ = f32[16,64,256]{2,1,0:T(8,128)S(1)} all-to-all(f32[16,64,256]{2,1,0:T(8,128)S(1)} %right_factor.1), channel_id=1, replica_groups=mesh['zlo'=4,'y'=4,'x'=4,'zhi'=2,'core'=2] {'x','y'}, dimensions={0} | all-to-all | bytes 2097152 | tf_op jit(solution)/shard_map/right_factor/all_to_all | solution.py:277
  91.6 6.7 %collective-permute-start.33 = (f32[16,64,256]{2,1,0:T(8,128)S(1)}, f32[16,64,256]{2,1,0:T(8,128)S(1)}, u32[]{:S(2)}, u32[]{:S(2)}) collective-permute-start(f32[16,64,256]{2,1,0:T(8,128)S(1)} %all_to_all.5.refs_2_.refs_4_), channel_id=1, source_target_pairs={{0,1},{1,0},{2,3},{3,2},{4,5},{5,4},{6,7},{7,6},{8,9},{9,8},{10,11... | collective-permute-start | bytes 3145736 | tf_op jit(solution)/shard_map/right_factor/ppermute | solution.py:30
  98.2 1.7 %error.2.refs_0_ = f32[1,128,8192]{2,1,0:T(8,128)} custom-call(f32[128,8192]{1,0:T(8,128)S(1)} %add_bitcast_fusion.refs_5_.refs_7_.refs_6_.merged.refs_0_.refs_1_, bf16[128,192]{1,0:T(8,128)(2,1)S(1)} %get-tuple-element.51.refs_1_.refs_2_, f32[16,64,256]{2,1,0:T(8,128)S(1)} %all_to_all.5.refs_2_.refs_4_), custom_call_target="tpu_custom_call" | custom-call | tf_op jit(solution)/shard_map/error/pallas_call | solution.py:266
  100.5 1.7 %error.3 = (f32[1,128,8192]{2,1,0:T(8,128)}, f32[64,512]{1,0:T(8,128)}) custom-call(f32[1,128,8192]{2,1,0:T(8,128)} %error.2.refs_0_, f32[128,8192]{1,0:T(8,128)S(1)} %add_bitcast_fusion.refs_5_.refs_7_.refs_6_.merged.refs_0_.refs_1_, bf16[128,192]{1,0:T(8,128)(2,1)S(1)} %get-tuple-element.51.refs_1_.refs_2_, ...), custom_call_target="tpu_custom_call", output_to_operand_aliasing={{0}: (0, {})} | custom-call | tf_op jit(solution)/shard_map/error/pallas_call | solution.py:266
  (56 shorter events, 11.3 us)
Async XLA Ops:
  0.6 13.8 %collective-permute-start.3 = (f32[64,512]{1,0:T(8,128)}, f32[64,512]{1,0:T(8,128)S(1)}, u32[]{:S(2)}, u32[]{:S(2)}) collective-permute-start(f32[64,512]{1,0:T(8,128)} %bitcast.5), channel_id=1, source_target_pairs={{0,130},{1,131},{2,128},{3,129},{4,134},{5,135},{6,132},{7,133},{8... | collective-permute-start | bytes 393224 | tf_op jit(solution)/shard_map/gather_factor/ppermute | solution.py:30
  7.6 10.8 %collective-permute-start.2 = (f32[64,512]{1,0:T(8,128)}, f32[64,512]{1,0:T(8,128)S(1)}, u32[]{:S(2)}, u32[]{:S(2)}) collective-permute-start(f32[64,512]{1,0:T(8,128)} %bitcast.6), channel_id=1, source_target_pairs={{0,8},{1,9},{2,10},{3,11},{4,12},{5,13},{6,14},{7,15},{8,0},{9,1},... | collective-permute-start | bytes 393224 | tf_op jit(solution)/shard_map/gather_factor/ppermute | solution.py:30
  10.3 8.1 %collective-permute-start.1 = (f32[64,512]{1,0:T(8,128)}, f32[64,512]{1,0:T(8,128)S(1)}, u32[]{:S(2)}, u32[]{:S(2)}) collective-permute-start(f32[64,512]{1,0:T(8,128)} %bitcast.7), channel_id=1, source_target_pairs={{0,12},{1,13},{2,14},{3,15},{4,8},{5,9},{6,10},{7,11},{8,4},{9,5},... | collective-permute-start | bytes 393224 | tf_op jit(solution)/shard_map/gather_factor/ppermute | solution.py:30
  11.2 7.2 %collective-permute-start = (f32[64,512]{1,0:T(8,128)}, f32[64,512]{1,0:T(8,128)S(1)}, u32[]{:S(2)}, u32[]{:S(2)}) collective-permute-start(f32[64,512]{1,0:T(8,128)} %bitcast.8), channel_id=1, source_target_pairs={{0,4},{1,5},{2,6},{3,7},{4,0},{5,1},{6,2},{7,3},{8,12},{9,13},{10,... | collective-permute-start | bytes 393224 | tf_op jit(solution)/shard_map/gather_factor/ppermute | solution.py:30
  14.5 5.7 %collective-permute-start.4 = (f32[64,512]{1,0:T(8,128)S(1)}, f32[64,512]{1,0:T(8,128)S(1)}, u32[]{:S(2)}, u32[]{:S(2)}) collective-permute-start(f32[64,512]{1,0:T(8,128)S(1)} %collective-permute-done.3.refs_4_), channel_id=1, source_target_pairs={{0,8},{1,9},{2,10},{3,11},{4,12},{5,13},{6,14},{7,15},{8,0},{9,1},... | collective-permute-start | bytes 393224 | tf_op jit(solution)/shard_map/gather_factor/ppermute | solution.py:30
  17.5 5.7 %collective-permute-start.11 = (f32[64,512]{1,0:T(8,128)S(1)}, f32[64,512]{1,0:T(8,128)S(1)}, u32[]{:S(2)}, u32[]{:S(2)}) collective-permute-start(f32[64,512]{1,0:T(8,128)S(1)} %collective-permute-done.3.refs_4_), channel_id=1, source_target_pairs={{0,12},{1,13},{2,14},{3,15},{4,8},{5,9},{6,10},{7,11},{8,4},{9,5},... | collective-permute-start | bytes 393224 | tf_op jit(solution)/shard_map/gather_factor/ppermute | solution.py:30
  18.4 7.4 %collective-permute-start.10 = (f32[64,512]{1,0:T(8,128)S(1)}, f32[64,512]{1,0:T(8,128)S(1)}, u32[]{:S(2)}, u32[]{:S(2)}) collective-permute-start(f32[64,512]{1,0:T(8,128)S(1)} %collective-permute-done.3.refs_4_), channel_id=1, source_target_pairs={{0,4},{1,5},{2,6},{3,7},{4,0},{5,1},{6,2},{7,3},{8,12},{9,13},{10,... | collective-permute-start | bytes 393224 | tf_op jit(solution)/shard_map/gather_factor/ppermute | solution.py:30
  20.1 5.7 %collective-permute-start.5 = (f32[64,512]{1,0:T(8,128)S(1)}, f32[64,512]{1,0:T(8,128)S(1)}, u32[]{:S(2)}, u32[]{:S(2)}) collective-permute-start(f32[64,512]{1,0:T(8,128)S(1)} %collective-permute-done.refs_0_), channel_id=1, source_target_pairs={{0,1},{1,0},{2,3},{3,2},{4,5},{5,4},{6,7},{7,6},{8,9},{9,8},{10,11... | collective-permute-start | bytes 393224 | tf_op jit(solution)/shard_map/left_sum/ppermute | solution.py:30
  22.7 3.7 %collective-permute-start.6 = (f32[64,512]{1,0:T(8,128)S(1)}, f32[64,512]{1,0:T(8,128)S(1)}, u32[]{:S(2)}, u32[]{:S(2)}) collective-permute-start(f32[64,512]{1,0:T(8,128)S(1)} %collective-permute-done.1.refs_1_), channel_id=1, source_target_pairs={{0,1},{1,0},{2,3},{3,2},{4,5},{5,4},{6,7},{7,6},{8,9},{9,8},{10,11... | collective-permute-start | bytes 393224 | tf_op jit(solution)/shard_map/left_sum/ppermute | solution.py:30
  22.7 3.8 %collective-permute-start.7 = (f32[64,512]{1,0:T(8,128)S(1)}, f32[64,512]{1,0:T(8,128)S(1)}, u32[]{:S(2)}, u32[]{:S(2)}) collective-permute-start(f32[64,512]{1,0:T(8,128)S(1)} %collective-permute-done.2.refs_2_), channel_id=1, source_target_pairs={{0,1},{1,0},{2,3},{3,2},{4,5},{5,4},{6,7},{7,6},{8,9},{9,8},{10,11... | collective-permute-start | bytes 393224 | tf_op jit(solution)/shard_map/left_sum/ppermute | solution.py:30
  23.3 3.6 %collective-permute-start.8 = (f32[64,512]{1,0:T(8,128)S(1)}, f32[64,512]{1,0:T(8,128)S(1)}, u32[]{:S(2)}, u32[]{:S(2)}) collective-permute-start(f32[64,512]{1,0:T(8,128)S(1)} %bitcast.10), channel_id=1, source_target_pairs={{0,1},{1,0},{2,3},{3,2},{4,5},{5,4},{6,7},{7,6},{8,9},{9,8},{10,11... | collective-permute-start | bytes 393224 | tf_op jit(solution)/shard_map/left_sum/ppermute | solution.py:30
  25.8 2.0 %collective-permute-start.13 = (f32[64,512]{1,0:T(8,128)S(1)}, f32[64,512]{1,0:T(8,128)S(1)}, u32[]{:S(2)}, u32[]{:S(2)}) collective-permute-start(f32[64,512]{1,0:T(8,128)S(1)} %collective-permute-done.11.refs_2_), channel_id=1, source_target_pairs={{0,1},{1,0},{2,3},{3,2},{4,5},{5,4},{6,7},{7,6},{8,9},{9,8},{10,11... | collective-permute-start | bytes 393224 | tf_op jit(solution)/shard_map/left_sum/ppermute | solution.py:30
  26.3 1.5 %collective-permute-start.12 = (f32[64,512]{1,0:T(8,128)S(1)}, f32[64,512]{1,0:T(8,128)S(1)}, u32[]{:S(2)}, u32[]{:S(2)}) collective-permute-start(f32[64,512]{1,0:T(8,128)S(1)} %collective-permute-done.10.refs_1_), channel_id=1, source_target_pairs={{0,1},{1,0},{2,3},{3,2},{4,5},{5,4},{6,7},{7,6},{8,9},{9,8},{10,11... | collective-permute-start | bytes 393224 | tf_op jit(solution)/shard_map/left_sum/ppermute | solution.py:30
  28.5 4.4 %collective-permute-start.17 = (f32[64,128]{1,0:T(8,128)S(1)}, f32[64,128]{1,0:T(8,128)S(1)}, u32[]{:S(2)}, u32[]{:S(2)}) collective-permute-start(f32[64,128]{1,0:T(8,128)S(1)} %left_sum.5), channel_id=1, source_target_pairs={{0,128},{1,33},{2,130},{3,35},{4,132},{5,37},{6,134},{7,39},{8,136... | collective-permute-start | bytes 98312 | tf_op jit(solution)/shard_map/left_sum/ppermute | solution.py:30
  31.5 4.2 %collective-permute-start.16 = (f32[64,128]{1,0:T(8,128)S(1)}, f32[64,128]{1,0:T(8,128)S(1)}, u32[]{:S(2)}, u32[]{:S(2)}) collective-permute-start(f32[64,128]{1,0:T(8,128)S(1)} %left_sum.5), channel_id=1, source_target_pairs={{0,192},{1,49},{2,194},{3,51},{4,196},{5,53},{6,198},{7,55},{8,200... | collective-permute-start | bytes 98312 | tf_op jit(solution)/shard_map/left_sum/ppermute | solution.py:30
  32.2 3.4 %collective-permute-start.15 = (f32[64,128]{1,0:T(8,128)S(1)}, f32[64,128]{1,0:T(8,128)S(1)}, u32[]{:S(2)}, u32[]{:S(2)}) collective-permute-start(f32[64,128]{1,0:T(8,128)S(1)} %left_sum.5), channel_id=1, source_target_pairs={{0,64},{1,17},{2,66},{3,19},{4,68},{5,21},{6,70},{7,23},{8,72},{9,... | collective-permute-start | bytes 98312 | tf_op jit(solution)/shard_map/left_sum/ppermute | solution.py:30
  35.7 3.9 %collective-permute-start.20 = (f32[64,128]{1,0:T(8,128)S(1)}, f32[64,128]{1,0:T(8,128)S(1)}, u32[]{:S(2)}, u32[]{:S(2)}) collective-permute-start(f32[64,128]{1,0:T(8,128)S(1)} %add_add_fusion.1), channel_id=1, source_target_pairs={{0,32},{1,129},{2,34},{3,131},{4,36},{5,133},{6,38},{7,135},{8,40}... | collective-permute-start | bytes 98312 | tf_op jit(solution)/shard_map/left_sum/ppermute | solution.py:30
  36.9 4.8 %collective-permute-start.19 = (f32[64,128]{1,0:T(8,128)S(1)}, f32[64,128]{1,0:T(8,128)S(1)}, u32[]{:S(2)}, u32[]{:S(2)}) collective-permute-start(f32[64,128]{1,0:T(8,128)S(1)} %add_add_fusion.1), channel_id=1, source_target_pairs={{0,48},{1,193},{2,50},{3,195},{4,52},{5,197},{6,54},{7,199},{8,56}... | collective-permute-start | bytes 98312 | tf_op jit(solution)/shard_map/left_sum/ppermute | solution.py:30
  38.5 3.2 %collective-permute-start.18 = (f32[64,128]{1,0:T(8,128)S(1)}, f32[64,128]{1,0:T(8,128)S(1)}, u32[]{:S(2)}, u32[]{:S(2)}) collective-permute-start(f32[64,128]{1,0:T(8,128)S(1)} %add_add_fusion.1), channel_id=1, source_target_pairs={{0,16},{1,65},{2,18},{3,67},{4,20},{5,69},{6,22},{7,71},{8,24},{9,... | collective-permute-start | bytes 98312 | tf_op jit(solution)/shard_map/left_sum/ppermute | solution.py:30
  42.2 5.0 %collective-permute-start.22 = (f32[2,272,256]{2,1,0:T(8,128)S(1)}, f32[2,272,256]{2,1,0:T(8,128)S(1)}, u32[]{:S(2)}, u32[]{:S(2)}) collective-permute-start(f32[2,272,256]{2,1,0:T(8,128)S(1)} %get-tuple-element.42), channel_id=1, source_target_pairs={{0,1},{1,0},{2,3},{3,2},{4,5},{5,4},{6,7},{7,6},{8,9},{9,8},{10,11... | collective-permute-start | bytes 1671176 | tf_op jit(solution)/shard_map/right_sum/ppermute | solution.py:30
  45.6 3.7 %collective-permute-start.21 = (f32[2,272,256]{2,1,0:T(8,128)S(1)}, f32[2,272,256]{2,1,0:T(8,128)S(1)}, u32[]{:S(2)}, u32[]{:S(2)}) collective-permute-start(f32[2,272,256]{2,1,0:T(8,128)S(1)} %get-tuple-element.39), channel_id=1, source_target_pairs={{0,1},{1,0},{2,3},{3,2},{4,5},{5,4},{6,7},{7,6},{8,9},{9,8},{10,11... | collective-permute-start | bytes 1671176 | tf_op jit(solution)/shard_map/right_sum/ppermute | solution.py:30
  47.3 7.3 %collective-permute-start.23 = (f32[272,256]{1,0:T(8,128)S(1)}, f32[272,256]{1,0:T(8,128)S(1)}, u32[]{:S(2)}, u32[]{:S(2)}) collective-permute-start(f32[272,256]{1,0:T(8,128)S(1)} %get-tuple-element.43), channel_id=1, source_target_pairs={{0,8},{1,33},{2,10},{3,35},{4,12},{5,37},{6,14},{7,39},{8,0},{9,41... | collective-permute-start | bytes 835592 | tf_op jit(solution)/shard_map/right_sum/ppermute | solution.py:30
  48.6 8.9 %collective-permute-start.24 = (f32[272,256]{1,0:T(8,128)S(1)}, f32[272,256]{1,0:T(8,128)S(1)}, u32[]{:S(2)}, u32[]{:S(2)}) collective-permute-start(f32[272,256]{1,0:T(8,128)S(1)} %get-tuple-element.44), channel_id=1, source_target_pairs={{0,12},{1,49},{2,14},{3,51},{4,8},{5,53},{6,10},{7,55},{8,4},{9,57... | collective-permute-start | bytes 835592 | tf_op jit(solution)/shard_map/right_sum/ppermute | solution.py:30
  49.4 8.2 %collective-permute-start.25 = (f32[272,256]{1,0:T(8,128)S(1)}, f32[272,256]{1,0:T(8,128)S(1)}, u32[]{:S(2)}, u32[]{:S(2)}) collective-permute-start(f32[272,256]{1,0:T(8,128)S(1)} %get-tuple-element.45), channel_id=1, source_target_pairs={{0,4},{1,17},{2,6},{3,19},{4,0},{5,21},{6,2},{7,23},{8,12},{9,25},... | collective-permute-start | bytes 835592 | tf_op jit(solution)/shard_map/right_sum/ppermute | solution.py:30
  57.6 4.9 %collective-permute-start.26 = (f32[80,256]{1,0:T(8,128)S(1)}, f32[80,256]{1,0:T(8,128)S(1)}, u32[]{:S(2)}, u32[]{:S(2)}) collective-permute-start(f32[80,256]{1,0:T(8,128)S(1)} %get-tuple-element.47), channel_id=1, source_target_pairs={{0,32},{1,9},{2,34},{3,11},{4,36},{5,13},{6,38},{7,15},{8,40},{9,1... | collective-permute-start | bytes 245768 | tf_op jit(solution)/shard_map/right_sum/ppermute | solution.py:30
  58.8 4.9 %collective-permute-start.27 = (f32[80,256]{1,0:T(8,128)S(1)}, f32[80,256]{1,0:T(8,128)S(1)}, u32[]{:S(2)}, u32[]{:S(2)}) collective-permute-start(f32[80,256]{1,0:T(8,128)S(1)} %get-tuple-element.48), channel_id=1, source_target_pairs={{0,48},{1,13},{2,50},{3,15},{4,52},{5,9},{6,54},{7,11},{8,56},{9,5... | collective-permute-start | bytes 245768 | tf_op jit(solution)/shard_map/right_sum/ppermute | solution.py:30
  60.1 3.6 %collective-permute-start.28 = (f32[80,256]{1,0:T(8,128)S(1)}, f32[80,256]{1,0:T(8,128)S(1)}, u32[]{:S(2)}, u32[]{:S(2)}) collective-permute-start(f32[80,256]{1,0:T(8,128)S(1)} %get-tuple-element.49), channel_id=1, source_target_pairs={{0,16},{1,5},{2,18},{3,7},{4,20},{5,1},{6,22},{7,3},{8,24},{9,13},... | collective-permute-start | bytes 245768 | tf_op jit(solution)/shard_map/right_sum/ppermute | solution.py:30
  63.7 5.5 %collective-permute-start.29 = (f32[80,256]{1,0:T(8,128)S(1)}, f32[80,256]{1,0:T(8,128)S(1)}, u32[]{:S(2)}, u32[]{:S(2)}) collective-permute-start(f32[80,256]{1,0:T(8,128)S(1)} %right_sum.12.own), channel_id=1, source_target_pairs={{0,130},{1,131},{2,128},{3,129},{4,134},{5,135},{6,132},{7,133},{8... | collective-permute-start | bytes 245768 | tf_op jit(solution)/shard_map/right_sum/ppermute | solution.py:30
  69.2 5.2 %collective-permute-start.32 = (f32[64,256]{1,0:T(8,128)S(1)}, f32[64,256]{1,0:T(8,128)S(1)}, u32[]{:S(2)}, u32[]{:S(2)}) collective-permute-start(f32[64,256]{1,0:T(8,128)S(1)} %get-tuple-element.52.own), channel_id=1, source_target_pairs={{0,128},{1,129},{2,130},{3,131},{4,132},{5,133},{6,134},{7,135},{8... | collective-permute-start | bytes 196616 | tf_op jit(solution)/shard_map/right_sum/ppermute | solution.py:30
  69.9 5.1 %collective-permute-start.31 = (f32[64,256]{1,0:T(8,128)S(1)}, f32[64,256]{1,0:T(8,128)S(1)}, u32[]{:S(2)}, u32[]{:S(2)}) collective-permute-start(f32[64,256]{1,0:T(8,128)S(1)} %get-tuple-element.52.own), channel_id=1, source_target_pairs={{0,192},{1,193},{2,194},{3,195},{4,196},{5,197},{6,198},{7,199},{8... | collective-permute-start | bytes 196616 | tf_op jit(solution)/shard_map/right_sum/ppermute | solution.py:30
  71.5 3.8 %collective-permute-start.30 = (f32[64,256]{1,0:T(8,128)S(1)}, f32[64,256]{1,0:T(8,128)S(1)}, u32[]{:S(2)}, u32[]{:S(2)}) collective-permute-start(f32[64,256]{1,0:T(8,128)S(1)} %get-tuple-element.52.own), channel_id=1, source_target_pairs={{0,64},{1,65},{2,66},{3,67},{4,68},{5,69},{6,70},{7,71},{8,72},{9,... | collective-permute-start | bytes 196616 | tf_op jit(solution)/shard_map/right_sum/ppermute | solution.py:30
  91.6 9.0 %collective-permute-start.33 = (f32[16,64,256]{2,1,0:T(8,128)S(1)}, f32[16,64,256]{2,1,0:T(8,128)S(1)}, u32[]{:S(2)}, u32[]{:S(2)}) collective-permute-start(f32[16,64,256]{2,1,0:T(8,128)S(1)} %all_to_all.5.refs_2_.refs_4_), channel_id=1, source_target_pairs={{0,1},{1,0},{2,3},{3,2},{4,5},{5,4},{6,7},{7,6},{8,9},{9,8},{10,11... | collective-permute-start | bytes 3145736 | tf_op jit(solution)/shard_map/right_factor/ppermute | solution.py:30
  (3 other events, 20.6 us)

commit v5 on v4

--- a/solution.py
+++ b/solution.py
@@ -115,24 +115,25 @@
             rhs = jnp.concatenate(split(merged[:, pl.ds(column(half, first, second), WIDE)]), 0)
             both = dot(lhs, rhs)
             out[place, second * RANK : (second + 1) * RANK] = both[:RANK] + both[RANK:]
-        out[place, TALL:] = flat
+        if first == 0:
+            out[place, TALL:] = flat
 
 
 def cross_part(flip, merged, left):
-    return simple(functools.partial(cross_kernel, flip), [(2, TALL + EXTRA, WIDE)] * 2, merged, left)
+    return simple(functools.partial(cross_kernel, flip), [(2, TALL, WIDE), (2, TALL + EXTRA, WIDE)], merged, left)
 
 
 def pack_kernel(own, received, *outs):
     for place, out in enumerate(outs):
-        out[...] = own[place] + received[place]
+        rows = slice(0, out.shape[0])
+        out[...] = own[place, rows] + received[place, rows]
 
 
 def scatter_kernel(own, two, three, one, *outs):
     def summed(rows):
         return (own[rows] + one[rows]) + (three[rows] + two[rows])
 
-    rows = slice(TALL, TALL + EXTRA)
-    gram = jnp.where(lax.axis_index("core") == 0, summed(rows), own[rows])
+    gram = own[TALL:]
     for step, out in zip((0,) + PACKED, outs):
         out[:RANK] = summed(slice(step * RANK, (step + 1) * RANK))
         out[RANK:] = gram
@@ -141,7 +142,7 @@
 def join_kernel(own, two, three, one, out):
     summed = (own[...] + one[...]) + (three[...] + two[...])
     out[:RANK] = summed[:RANK]
-    out[RANK:] = jnp.where(lax.axis_index("core") == 1, summed[RANK:], own[RANK:])
+    out[RANK:] = summed[RANK:]
 
 
 def pair_kernel(own, other, out, gram):
@@ -149,7 +150,8 @@
     gram[...] = own[RANK:] + other[RANK:]
 
 
-def factor_kernel(packed, left, inverse, left_out, wide_out):
+def factor_kernel(own, other, left, inverse, left_out, wide_out):
+    packed = jnp.where(lax.axis_index("core") == 1, own[...], other[...])
     gram = jnp.concatenate([packed[:, q * RANK : (q + 1) * RANK] for q in range(FOLD)], 0)
     row = lax.broadcasted_iota(jnp.int32, (RANK, RANK), 0)
     col = lax.broadcasted_iota(jnp.int32, (RANK, RANK), 1)
@@ -316,7 +318,7 @@
         kept = cross_part(0, merged, left_sum)
         packed = []
         for mine, theirs in zip(kept, received):
-            packed += simple(pack_kernel, [(TALL + EXTRA, WIDE)] * 2, mine, theirs)
+            packed += simple(pack_kernel, [(TALL, WIDE), (mine.shape[1], WIDE)], mine, theirs)
         *outgoing, own = packed
         incoming = [mixed(value, step, 0) for step, value in zip(PACKED, outgoing)]
         own, *outgoing = simple(scatter_kernel, [(RANK + EXTRA, WIDE)] * RING, own, *incoming)
@@ -325,6 +327,7 @@
         other = shift(joined, zlo=2, zhi=1)
         summed, gram = simple(pair_kernel, [(RANK, WIDE), (EXTRA, WIDE)], joined, other)
         others = ring(summed, "zlo")
+        gram_other = shift(gram, core=1)
     with jax.named_scope("cholesky"):
         inverse, left_turned, left_wide = call(
             factor_kernel,
@@ -333,9 +336,9 @@
                 jax.ShapeDtypeStruct((RANK, ROWS), F32),
                 jax.ShapeDtypeStruct((ROWS, 3 * RANK), BF16),
             ],
-            in_specs=[VMEM] * 2,
+            in_specs=[VMEM] * 3,
             out_specs=[VMEM] * 3,
-        )(gram, left_sum)
+        )(gram, gram_other, left_sum)
     with jax.named_scope("right_factor"):
         right = exchange(simple(spread_kernel, (CHUNKS, RANK, WIDE), summed, *others, inverse))
         right_other = shift(right, core=1)

time: 102 us -> 107 us (1.049)
  blocking collectives: 15.9 us -> 20 us
    all_to_all x1, blocking collectives: 15.9 us -> 20 us  [exchange(): lax.all_to_all(value, ('x', 'y'), split_axis=0, concat_axis=0, tiled=True)]
    ppermute x34 -> x35, waiting for transfers between devices: 24.7 us -> 25 us  [moved(): return lax.ppermute(value, AXES, pairs)]
    ppermute x34 -> x35, starting transfers between devices: 48.4 us -> 48.4 us  [moved(): return lax.ppermute(value, AXES, pairs)]
  transfers between devices with their start and end apart: 34 -> 35, of which waited for: 16 -> 15; matrix products, arithmetic and copies ran while one was open for 3% -> 3% of each run, Pallas kernels for 6% -> 6%
where the time goes in v5:
time: 107 us
  starting transfers between devices  48.4 us (45%)
  waiting for transfers between devices  25 us (23%)
  blocking collectives  20 us (19%)
  Pallas kernels  9.09 us (8%)
  other arithmetic  3.28 us (3%)
    ppermute x35, starting transfers between devices, moved(): return lax.ppermute(value, AXES, pairs)  48.4 us
    ppermute x35, waiting for transfers between devices, moved(): return lax.ppermute(value, AXES, pairs)  25 us
    all_to_all x1, blocking collectives, exchange(): lax.all_to_all(value, ('x', 'y'), split_axis=0, concat_axis=0, tiled=True)  20 us
    pallas_call x2, Pallas kernels, error_part(): call(functools.partial(error_kernel, int(last)), out_shape, in_specs=([an...  3.32 us
    add x1, other arithmetic, body(): merged = gradient[0].astype(F32) + error_feed[0]  3.26 us
    pallas_call x1, Pallas kernels, body(): call(factor_kernel, [jax.ShapeDtypeStruct((RANK, RANK), F32), jax.ShapeDt...  2.43 us
  transfers between devices with their start and end apart: 35, of which 15 were waited for; matrix products, arithmetic and copies ran while one was open for 3% of the time, Pallas kernels for 6%

profile of v5, /device:TPU:1, one launch (start us, length us, event | category | flops | bytes accessed | tf_op | source)
XLA Modules:
  0.0 106.7 jit_solution(14361104499295879781)
XLA Ops:
  0.6 6.9 %collective-permute-start.3 = (f32[64,512]{1,0:T(8,128)}, f32[64,512]{1,0:T(8,128)S(1)}, u32[]{:S(2)}, u32[]{:S(2)}) collective-permute-start(f32[64,512]{1,0:T(8,128)} %bitcast.5), channel_id=1, source_target_pairs={{0,130},{1,131},{2,128},{3,129},{4,134},{5,135},{6,132},{7,133},{8... | collective-permute-start | bytes 393224 | tf_op jit(solution)/shard_map/gather_factor/ppermute | solution.py:30
  7.6 2.7 %collective-permute-start.2 = (f32[64,512]{1,0:T(8,128)}, f32[64,512]{1,0:T(8,128)S(1)}, u32[]{:S(2)}, u32[]{:S(2)}) collective-permute-start(f32[64,512]{1,0:T(8,128)} %bitcast.6), channel_id=1, source_target_pairs={{0,8},{1,9},{2,10},{3,11},{4,12},{5,13},{6,14},{7,15},{8,0},{9,1},... | collective-permute-start | bytes 393224 | tf_op jit(solution)/shard_map/gather_factor/ppermute | solution.py:30
  10.3 0.9 collective-permute-start.1
  11.2 3.3 %add_bitcast_fusion.refs_5_.refs_7_.refs_6_.merged.refs_0_.refs_1_ = f32[128,8192]{1,0:T(8,128)S(1)} fusion(f32[1,128,8192]{2,1,0:T(8,128)} %param.4, bf16[1,128,8192]{2,1,0:T(8,128)(2,1)} %param.3), kind=kLoop, calls=%fused_computation | loop fusion | flops 2097152 | bytes 10485760 | tf_op jit(solution)/shard_map/add | solution.py:295
  14.5 3.1 %collective-permute-start.4 = (f32[64,512]{1,0:T(8,128)S(1)}, f32[64,512]{1,0:T(8,128)S(1)}, u32[]{:S(2)}, u32[]{:S(2)}) collective-permute-start(f32[64,512]{1,0:T(8,128)S(1)} %collective-permute-done.3.refs_4_), channel_id=1, source_target_pairs={{0,8},{1,9},{2,10},{3,11},{4,12},{5,13},{6,14},{7,15},{8,0},{9,1},... | collective-permute-start | bytes 393224 | tf_op jit(solution)/shard_map/gather_factor/ppermute | solution.py:30
  19.0 1.1 %collective-permute-done.4.refs_6_ = f32[64,512]{1,0:T(8,128)S(1)} collective-permute-done((f32[64,512]{1,0:T(8,128)S(1)}, f32[64,512]{1,0:T(8,128)S(1)}, u32[]{:S(2)}, u32[]{:S(2)}) %collective-permute-start.4) | collective-permute-done | bytes 131104 | tf_op jit(solution)/shard_map/gather_factor/ppermute | solution.py:30
  20.1 2.5 %collective-permute-start.5 = (f32[64,512]{1,0:T(8,128)S(1)}, f32[64,512]{1,0:T(8,128)S(1)}, u32[]{:S(2)}, u32[]{:S(2)}) collective-permute-start(f32[64,512]{1,0:T(8,128)S(1)} %collective-permute-done.refs_0_), channel_id=1, source_target_pairs={{0,1},{1,0},{2,3},{3,2},{4,5},{5,4},{6,7},{7,6},{8,9},{9,8},{10,11... | collective-permute-start | bytes 393224 | tf_op jit(solution)/shard_map/left_sum/ppermute | solution.py:30
  23.3 2.5 %collective-permute-start.8 = (f32[64,512]{1,0:T(8,128)S(1)}, f32[64,512]{1,0:T(8,128)S(1)}, u32[]{:S(2)}, u32[]{:S(2)}) collective-permute-start(f32[64,512]{1,0:T(8,128)S(1)} %bitcast.10), channel_id=1, source_target_pairs={{0,1},{1,0},{2,3},{3,2},{4,5},{5,4},{6,7},{7,6},{8,9},{9,8},{10,11... | collective-permute-start | bytes 393224 | tf_op jit(solution)/shard_map/left_sum/ppermute | solution.py:30
  28.5 3.0 %collective-permute-start.17 = (f32[64,128]{1,0:T(8,128)S(1)}, f32[64,128]{1,0:T(8,128)S(1)}, u32[]{:S(2)}, u32[]{:S(2)}) collective-permute-start(f32[64,128]{1,0:T(8,128)S(1)} %left_sum.5), channel_id=1, source_target_pairs={{0,128},{1,33},{2,130},{3,35},{4,132},{5,37},{6,134},{7,39},{8,136... | collective-permute-start | bytes 98312 | tf_op jit(solution)/shard_map/left_sum/ppermute | solution.py:30
  32.8 2.8 %collective-permute-done.16 = f32[64,128]{1,0:T(8,128)S(1)} collective-permute-done((f32[64,128]{1,0:T(8,128)S(1)}, f32[64,128]{1,0:T(8,128)S(1)}, u32[]{:S(2)}, u32[]{:S(2)}) %collective-permute-start.16) | collective-permute-done | bytes 32800 | tf_op jit(solution)/shard_map/left_sum/ppermute | solution.py:30
  35.7 1.2 %collective-permute-start.20 = (f32[64,128]{1,0:T(8,128)S(1)}, f32[64,128]{1,0:T(8,128)S(1)}, u32[]{:S(2)}, u32[]{:S(2)}) collective-permute-start(f32[64,128]{1,0:T(8,128)S(1)} %add_add_fusion.1), channel_id=1, source_target_pairs={{0,32},{1,129},{2,34},{3,131},{4,36},{5,133},{6,38},{7,135},{8,40}... | collective-permute-start | bytes 98312 | tf_op jit(solution)/shard_map/left_sum/ppermute | solution.py:30
  36.9 1.6 %collective-permute-start.19 = (f32[64,128]{1,0:T(8,128)S(1)}, f32[64,128]{1,0:T(8,128)S(1)}, u32[]{:S(2)}, u32[]{:S(2)}) collective-permute-start(f32[64,128]{1,0:T(8,128)S(1)} %add_add_fusion.1), channel_id=1, source_target_pairs={{0,48},{1,193},{2,50},{3,195},{4,52},{5,197},{6,54},{7,199},{8,56}... | collective-permute-start | bytes 98312 | tf_op jit(solution)/shard_map/left_sum/ppermute | solution.py:30
  38.6 1.0 collective-permute-done.20
  39.6 2.1 %collective-permute-done.19 = f32[64,128]{1,0:T(8,128)S(1)} collective-permute-done((f32[64,128]{1,0:T(8,128)S(1)}, f32[64,128]{1,0:T(8,128)S(1)}, u32[]{:S(2)}, u32[]{:S(2)}) %collective-permute-start.19) | collective-permute-done | bytes 32800 | tf_op jit(solution)/shard_map/left_sum/ppermute | solution.py:30
  42.2 3.4 %collective-permute-start.21 = (f32[2,272,256]{2,1,0:T(8,128)S(1)}, f32[2,272,256]{2,1,0:T(8,128)S(1)}, u32[]{:S(2)}, u32[]{:S(2)}) collective-permute-start(f32[2,272,256]{2,1,0:T(8,128)S(1)} %get-tuple-element.39), channel_id=1, source_target_pairs={{0,1},{1,0},{2,3},{3,2},{4,5},{5,4},{6,7},{7,6},{8,9},{9,8},{10,11... | collective-permute-start | bytes 1671176 | tf_op jit(solution)/shard_map/right_sum/ppermute | solution.py:30
  46.2 1.7 %collective-permute-done.22.received = f32[2,256,256]{2,1,0:T(8,128)S(1)} collective-permute-done((f32[2,256,256]{2,1,0:T(8,128)S(1)}, f32[2,256,256]{2,1,0:T(8,128)S(1)}, u32[]{:S(2)}, u32[]{:S(2)}) %collective-permute-start.22) | collective-permute-done | bytes 524320 | tf_op jit(solution)/shard_map/right_sum/ppermute | solution.py:30
  48.0 1.3 %collective-permute-start.23 = (f32[256,256]{1,0:T(8,128)S(1)}, f32[256,256]{1,0:T(8,128)S(1)}, u32[]{:S(2)}, u32[]{:S(2)}) collective-permute-start(f32[256,256]{1,0:T(8,128)S(1)} %get-tuple-element.43), channel_id=1, source_target_pairs={{0,8},{1,33},{2,10},{3,35},{4,12},{5,37},{6,14},{7,39},{8,0},{9,41... | collective-permute-start | bytes 786440 | tf_op jit(solution)/shard_map/right_sum/ppermute | solution.py:30
  50.9 4.3 %collective-permute-done.23.two = f32[256,256]{1,0:T(8,128)S(1)} collective-permute-done((f32[256,256]{1,0:T(8,128)S(1)}, f32[256,256]{1,0:T(8,128)S(1)}, u32[]{:S(2)}, u32[]{:S(2)}) %collective-permute-start.23) | collective-permute-done | bytes 262176 | tf_op jit(solution)/shard_map/right_sum/ppermute | solution.py:30
  55.2 2.8 %collective-permute-done.24.three = f32[256,256]{1,0:T(8,128)S(1)} collective-permute-done((f32[256,256]{1,0:T(8,128)S(1)}, f32[256,256]{1,0:T(8,128)S(1)}, u32[]{:S(2)}, u32[]{:S(2)}) %collective-permute-start.24) | collective-permute-done | bytes 262176 | tf_op jit(solution)/shard_map/right_sum/ppermute | solution.py:30
  58.0 1.2 %collective-permute-start.26 = (f32[80,256]{1,0:T(8,128)S(1)}, f32[80,256]{1,0:T(8,128)S(1)}, u32[]{:S(2)}, u32[]{:S(2)}) collective-permute-start(f32[80,256]{1,0:T(8,128)S(1)} %get-tuple-element.47), channel_id=1, source_target_pairs={{0,32},{1,9},{2,34},{3,11},{4,36},{5,13},{6,38},{7,15},{8,40},{9,1... | collective-permute-start | bytes 245768 | tf_op jit(solution)/shard_map/right_sum/ppermute | solution.py:30
  59.2 1.3 %collective-permute-start.27 = (f32[80,256]{1,0:T(8,128)S(1)}, f32[80,256]{1,0:T(8,128)S(1)}, u32[]{:S(2)}, u32[]{:S(2)}) collective-permute-start(f32[80,256]{1,0:T(8,128)S(1)} %get-tuple-element.48), channel_id=1, source_target_pairs={{0,48},{1,13},{2,50},{3,15},{4,52},{5,9},{6,54},{7,11},{8,56},{9,5... | collective-permute-start | bytes 245768 | tf_op jit(solution)/shard_map/right_sum/ppermute | solution.py:30
  60.7 2.2 %collective-permute-done.26.two = f32[80,256]{1,0:T(8,128)S(1)} collective-permute-done((f32[80,256]{1,0:T(8,128)S(1)}, f32[80,256]{1,0:T(8,128)S(1)}, u32[]{:S(2)}, u32[]{:S(2)}) %collective-permute-start.26) | collective-permute-done | bytes 81952 | tf_op jit(solution)/shard_map/right_sum/ppermute | solution.py:30
  62.9 1.2 %collective-permute-done.27.three = f32[80,256]{1,0:T(8,128)S(1)} collective-permute-done((f32[80,256]{1,0:T(8,128)S(1)}, f32[80,256]{1,0:T(8,128)S(1)}, u32[]{:S(2)}, u32[]{:S(2)}) %collective-permute-start.27) | collective-permute-done | bytes 81952 | tf_op jit(solution)/shard_map/right_sum/ppermute | solution.py:30
  64.1 2.1 %collective-permute-start.29 = (f32[80,256]{1,0:T(8,128)S(1)}, f32[80,256]{1,0:T(8,128)S(1)}, u32[]{:S(2)}, u32[]{:S(2)}) collective-permute-start(f32[80,256]{1,0:T(8,128)S(1)} %right_sum.12.own), channel_id=1, source_target_pairs={{0,130},{1,131},{2,128},{3,129},{4,134},{5,135},{6,132},{7,133},{8... | collective-permute-start | bytes 245768 | tf_op jit(solution)/shard_map/right_sum/ppermute | solution.py:30
  66.2 3.3 %collective-permute-done.29.other = f32[80,256]{1,0:T(8,128)S(1)} collective-permute-done((f32[80,256]{1,0:T(8,128)S(1)}, f32[80,256]{1,0:T(8,128)S(1)}, u32[]{:S(2)}, u32[]{:S(2)}) %collective-permute-start.29) | collective-permute-done | bytes 81952 | tf_op jit(solution)/shard_map/right_sum/ppermute | solution.py:30
  70.3 1.6 %collective-permute-start.32 = (f32[64,256]{1,0:T(8,128)S(1)}, f32[64,256]{1,0:T(8,128)S(1)}, u32[]{:S(2)}, u32[]{:S(2)}) collective-permute-start(f32[64,256]{1,0:T(8,128)S(1)} %get-tuple-element.52.own), channel_id=1, source_target_pairs={{0,192},{1,193},{2,194},{3,195},{4,196},{5,197},{6,198},{7,199},{8... | collective-permute-start | bytes 196616 | tf_op jit(solution)/shard_map/right_sum/ppermute | solution.py:30
  72.3 4.4 %collective-permute-start.30 = (f32[16,256]{1,0:T(8,128)S(1)}, f32[16,256]{1,0:T(8,128)S(1)}, u32[]{:S(2)}, u32[]{:S(2)}) collective-permute-start(f32[16,256]{1,0:T(8,128)S(1)} %get-tuple-element.50.own), channel_id=1, source_target_pairs={{0,1},{1,0},{2,3},{3,2},{4,5},{5,4},{6,7},{7,6},{8,9},{9,8},{10,11... | collective-permute-start | bytes 49160 | tf_op jit(solution)/shard_map/right_sum/ppermute | solution.py:30
  77.6 2.4 %cholesky.1 = (f32[64,64]{1,0:T(8,128)S(1)}, f32[64,128]{1,0:T(8,128)}, bf16[128,192]{1,0:T(8,128)(2,1)S(1)}) custom-call(f32[16,256]{1,0:T(8,128)S(1)} %get-tuple-element.50.own, f32[16,256]{1,0:T(8,128)S(1)} %collective-permute-done.30.other, f32[64,128]{1,0:T(8,128)S(1)} %add_add_fusion.left), custom_call_target="tpu_custom_call" | custom-call | tf_op jit(solution)/shard_map/cholesky/pallas_call | solution.py:332
  80.3 20.0 %all_to_all.5.refs_2_.refs_4_ = f32[16,64,256]{2,1,0:T(8,128)S(1)} all-to-all(f32[16,64,256]{2,1,0:T(8,128)S(1)} %right_factor.1), channel_id=1, replica_groups=mesh['zlo'=4,'y'=4,'x'=4,'zhi'=2,'core'=2] {'x','y'}, dimensions={0} | all-to-all | bytes 2097152 | tf_op jit(solution)/shard_map/right_factor/all_to_all | solution.py:279
  100.3 2.3 %collective-permute-start.34 = (f32[16,64,256]{2,1,0:T(8,128)S(1)}, f32[16,64,256]{2,1,0:T(8,128)S(1)}, u32[]{:S(2)}, u32[]{:S(2)}) collective-permute-start(f32[16,64,256]{2,1,0:T(8,128)S(1)} %all_to_all.5.refs_2_.refs_4_), channel_id=1, source_target_pairs={{0,1},{1,0},{2,3},{3,2},{4,5},{5,4},{6,7},{7,6},{8,9},{9,8},{10,11... | collective-permute-start | bytes 3145736 | tf_op jit(solution)/shard_map/right_factor/ppermute | solution.py:30
  102.6 1.7 %error.2.refs_0_ = f32[1,128,8192]{2,1,0:T(8,128)} custom-call(f32[128,8192]{1,0:T(8,128)S(1)} %add_bitcast_fusion.refs_5_.refs_7_.refs_6_.merged.refs_0_.refs_1_, bf16[128,192]{1,0:T(8,128)(2,1)S(1)} %get-tuple-element.51.refs_1_.refs_2_, f32[16,64,256]{2,1,0:T(8,128)S(1)} %all_to_all.5.refs_2_.refs_4_), custom_call_target="tpu_custom_call" | custom-call | tf_op jit(solution)/shard_map/error/pallas_call | solution.py:268
  104.9 1.7 %error.3 = (f32[1,128,8192]{2,1,0:T(8,128)}, f32[64,512]{1,0:T(8,128)}) custom-call(f32[1,128,8192]{2,1,0:T(8,128)} %error.2.refs_0_, f32[128,8192]{1,0:T(8,128)S(1)} %add_bitcast_fusion.refs_5_.refs_7_.refs_6_.merged.refs_0_.refs_1_, bf16[128,192]{1,0:T(8,128)(2,1)S(1)} %get-tuple-element.51.refs_1_.refs_2_, ...), custom_call_target="tpu_custom_call", output_to_operand_aliasing={{0}: (0, {})} | custom-call | tf_op jit(solution)/shard_map/error/pallas_call | solution.py:268
  (58 shorter events, 12.0 us)
Async XLA Ops:
  0.6 13.8 %collective-permute-start.3 = (f32[64,512]{1,0:T(8,128)}, f32[64,512]{1,0:T(8,128)S(1)}, u32[]{:S(2)}, u32[]{:S(2)}) collective-permute-start(f32[64,512]{1,0:T(8,128)} %bitcast.5), channel_id=1, source_target_pairs={{0,130},{1,131},{2,128},{3,129},{4,134},{5,135},{6,132},{7,133},{8... | collective-permute-start | bytes 393224 | tf_op jit(solution)/shard_map/gather_factor/ppermute | solution.py:30
  7.6 10.8 %collective-permute-start.2 = (f32[64,512]{1,0:T(8,128)}, f32[64,512]{1,0:T(8,128)S(1)}, u32[]{:S(2)}, u32[]{:S(2)}) collective-permute-start(f32[64,512]{1,0:T(8,128)} %bitcast.6), channel_id=1, source_target_pairs={{0,8},{1,9},{2,10},{3,11},{4,12},{5,13},{6,14},{7,15},{8,0},{9,1},... | collective-permute-start | bytes 393224 | tf_op jit(solution)/shard_map/gather_factor/ppermute | solution.py:30
  10.3 8.1 %collective-permute-start.1 = (f32[64,512]{1,0:T(8,128)}, f32[64,512]{1,0:T(8,128)S(1)}, u32[]{:S(2)}, u32[]{:S(2)}) collective-permute-start(f32[64,512]{1,0:T(8,128)} %bitcast.7), channel_id=1, source_target_pairs={{0,12},{1,13},{2,14},{3,15},{4,8},{5,9},{6,10},{7,11},{8,4},{9,5},... | collective-permute-start | bytes 393224 | tf_op jit(solution)/shard_map/gather_factor/ppermute | solution.py:30
  11.2 7.2 %collective-permute-start = (f32[64,512]{1,0:T(8,128)}, f32[64,512]{1,0:T(8,128)S(1)}, u32[]{:S(2)}, u32[]{:S(2)}) collective-permute-start(f32[64,512]{1,0:T(8,128)} %bitcast.8), channel_id=1, source_target_pairs={{0,4},{1,5},{2,6},{3,7},{4,0},{5,1},{6,2},{7,3},{8,12},{9,13},{10,... | collective-permute-start | bytes 393224 | tf_op jit(solution)/shard_map/gather_factor/ppermute | solution.py:30
  14.5 5.7 %collective-permute-start.4 = (f32[64,512]{1,0:T(8,128)S(1)}, f32[64,512]{1,0:T(8,128)S(1)}, u32[]{:S(2)}, u32[]{:S(2)}) collective-permute-start(f32[64,512]{1,0:T(8,128)S(1)} %collective-permute-done.3.refs_4_), channel_id=1, source_target_pairs={{0,8},{1,9},{2,10},{3,11},{4,12},{5,13},{6,14},{7,15},{8,0},{9,1},... | collective-permute-start | bytes 393224 | tf_op jit(solution)/shard_map/gather_factor/ppermute | solution.py:30
  17.5 5.7 %collective-permute-start.11 = (f32[64,512]{1,0:T(8,128)S(1)}, f32[64,512]{1,0:T(8,128)S(1)}, u32[]{:S(2)}, u32[]{:S(2)}) collective-permute-start(f32[64,512]{1,0:T(8,128)S(1)} %collective-permute-done.3.refs_4_), channel_id=1, source_target_pairs={{0,12},{1,13},{2,14},{3,15},{4,8},{5,9},{6,10},{7,11},{8,4},{9,5},... | collective-permute-start | bytes 393224 | tf_op jit(solution)/shard_map/gather_factor/ppermute | solution.py:30
  18.4 7.4 %collective-permute-start.10 = (f32[64,512]{1,0:T(8,128)S(1)}, f32[64,512]{1,0:T(8,128)S(1)}, u32[]{:S(2)}, u32[]{:S(2)}) collective-permute-start(f32[64,512]{1,0:T(8,128)S(1)} %collective-permute-done.3.refs_4_), channel_id=1, source_target_pairs={{0,4},{1,5},{2,6},{3,7},{4,0},{5,1},{6,2},{7,3},{8,12},{9,13},{10,... | collective-permute-start | bytes 393224 | tf_op jit(solution)/shard_map/gather_factor/ppermute | solution.py:30
  20.1 5.7 %collective-permute-start.5 = (f32[64,512]{1,0:T(8,128)S(1)}, f32[64,512]{1,0:T(8,128)S(1)}, u32[]{:S(2)}, u32[]{:S(2)}) collective-permute-start(f32[64,512]{1,0:T(8,128)S(1)} %collective-permute-done.refs_0_), channel_id=1, source_target_pairs={{0,1},{1,0},{2,3},{3,2},{4,5},{5,4},{6,7},{7,6},{8,9},{9,8},{10,11... | collective-permute-start | bytes 393224 | tf_op jit(solution)/shard_map/left_sum/ppermute | solution.py:30
  22.7 3.7 %collective-permute-start.6 = (f32[64,512]{1,0:T(8,128)S(1)}, f32[64,512]{1,0:T(8,128)S(1)}, u32[]{:S(2)}, u32[]{:S(2)}) collective-permute-start(f32[64,512]{1,0:T(8,128)S(1)} %collective-permute-done.1.refs_1_), channel_id=1, source_target_pairs={{0,1},{1,0},{2,3},{3,2},{4,5},{5,4},{6,7},{7,6},{8,9},{9,8},{10,11... | collective-permute-start | bytes 393224 | tf_op jit(solution)/shard_map/left_sum/ppermute | solution.py:30
  22.7 3.8 %collective-permute-start.7 = (f32[64,512]{1,0:T(8,128)S(1)}, f32[64,512]{1,0:T(8,128)S(1)}, u32[]{:S(2)}, u32[]{:S(2)}) collective-permute-start(f32[64,512]{1,0:T(8,128)S(1)} %collective-permute-done.2.refs_2_), channel_id=1, source_target_pairs={{0,1},{1,0},{2,3},{3,2},{4,5},{5,4},{6,7},{7,6},{8,9},{9,8},{10,11... | collective-permute-start | bytes 393224 | tf_op jit(solution)/shard_map/left_sum/ppermute | solution.py:30
  23.3 3.6 %collective-permute-start.8 = (f32[64,512]{1,0:T(8,128)S(1)}, f32[64,512]{1,0:T(8,128)S(1)}, u32[]{:S(2)}, u32[]{:S(2)}) collective-permute-start(f32[64,512]{1,0:T(8,128)S(1)} %bitcast.10), channel_id=1, source_target_pairs={{0,1},{1,0},{2,3},{3,2},{4,5},{5,4},{6,7},{7,6},{8,9},{9,8},{10,11... | collective-permute-start | bytes 393224 | tf_op jit(solution)/shard_map/left_sum/ppermute | solution.py:30
  25.8 2.0 %collective-permute-start.13 = (f32[64,512]{1,0:T(8,128)S(1)}, f32[64,512]{1,0:T(8,128)S(1)}, u32[]{:S(2)}, u32[]{:S(2)}) collective-permute-start(f32[64,512]{1,0:T(8,128)S(1)} %collective-permute-done.11.refs_2_), channel_id=1, source_target_pairs={{0,1},{1,0},{2,3},{3,2},{4,5},{5,4},{6,7},{7,6},{8,9},{9,8},{10,11... | collective-permute-start | bytes 393224 | tf_op jit(solution)/shard_map/left_sum/ppermute | solution.py:30
  28.5 4.4 %collective-permute-start.17 = (f32[64,128]{1,0:T(8,128)S(1)}, f32[64,128]{1,0:T(8,128)S(1)}, u32[]{:S(2)}, u32[]{:S(2)}) collective-permute-start(f32[64,128]{1,0:T(8,128)S(1)} %left_sum.5), channel_id=1, source_target_pairs={{0,128},{1,33},{2,130},{3,35},{4,132},{5,37},{6,134},{7,39},{8,136... | collective-permute-start | bytes 98312 | tf_op jit(solution)/shard_map/left_sum/ppermute | solution.py:30
  31.5 4.2 %collective-permute-start.16 = (f32[64,128]{1,0:T(8,128)S(1)}, f32[64,128]{1,0:T(8,128)S(1)}, u32[]{:S(2)}, u32[]{:S(2)}) collective-permute-start(f32[64,128]{1,0:T(8,128)S(1)} %left_sum.5), channel_id=1, source_target_pairs={{0,192},{1,49},{2,194},{3,51},{4,196},{5,53},{6,198},{7,55},{8,200... | collective-permute-start | bytes 98312 | tf_op jit(solution)/shard_map/left_sum/ppermute | solution.py:30
  32.2 3.4 %collective-permute-start.15 = (f32[64,128]{1,0:T(8,128)S(1)}, f32[64,128]{1,0:T(8,128)S(1)}, u32[]{:S(2)}, u32[]{:S(2)}) collective-permute-start(f32[64,128]{1,0:T(8,128)S(1)} %left_sum.5), channel_id=1, source_target_pairs={{0,64},{1,17},{2,66},{3,19},{4,68},{5,21},{6,70},{7,23},{8,72},{9,... | collective-permute-start | bytes 98312 | tf_op jit(solution)/shard_map/left_sum/ppermute | solution.py:30
  35.7 3.9 %collective-permute-start.20 = (f32[64,128]{1,0:T(8,128)S(1)}, f32[64,128]{1,0:T(8,128)S(1)}, u32[]{:S(2)}, u32[]{:S(2)}) collective-permute-start(f32[64,128]{1,0:T(8,128)S(1)} %add_add_fusion.1), channel_id=1, source_target_pairs={{0,32},{1,129},{2,34},{3,131},{4,36},{5,133},{6,38},{7,135},{8,40}... | collective-permute-start | bytes 98312 | tf_op jit(solution)/shard_map/left_sum/ppermute | solution.py:30
  36.9 4.8 %collective-permute-start.19 = (f32[64,128]{1,0:T(8,128)S(1)}, f32[64,128]{1,0:T(8,128)S(1)}, u32[]{:S(2)}, u32[]{:S(2)}) collective-permute-start(f32[64,128]{1,0:T(8,128)S(1)} %add_add_fusion.1), channel_id=1, source_target_pairs={{0,48},{1,193},{2,50},{3,195},{4,52},{5,197},{6,54},{7,199},{8,56}... | collective-permute-start | bytes 98312 | tf_op jit(solution)/shard_map/left_sum/ppermute | solution.py:30
  38.5 3.2 %collective-permute-start.18 = (f32[64,128]{1,0:T(8,128)S(1)}, f32[64,128]{1,0:T(8,128)S(1)}, u32[]{:S(2)}, u32[]{:S(2)}) collective-permute-start(f32[64,128]{1,0:T(8,128)S(1)} %add_add_fusion.1), channel_id=1, source_target_pairs={{0,16},{1,65},{2,18},{3,67},{4,20},{5,69},{6,22},{7,71},{8,24},{9,... | collective-permute-start | bytes 98312 | tf_op jit(solution)/shard_map/left_sum/ppermute | solution.py:30
  42.2 7.8 %collective-permute-start.21 = (f32[2,272,256]{2,1,0:T(8,128)S(1)}, f32[2,272,256]{2,1,0:T(8,128)S(1)}, u32[]{:S(2)}, u32[]{:S(2)}) collective-permute-start(f32[2,272,256]{2,1,0:T(8,128)S(1)} %get-tuple-element.39), channel_id=1, source_target_pairs={{0,1},{1,0},{2,3},{3,2},{4,5},{5,4},{6,7},{7,6},{8,9},{9,8},{10,11... | collective-permute-start | bytes 1671176 | tf_op jit(solution)/shard_map/right_sum/ppermute | solution.py:30
  45.6 2.3 %collective-permute-start.22 = (f32[2,256,256]{2,1,0:T(8,128)S(1)}, f32[2,256,256]{2,1,0:T(8,128)S(1)}, u32[]{:S(2)}, u32[]{:S(2)}) collective-permute-start(f32[2,256,256]{2,1,0:T(8,128)S(1)} %get-tuple-element.42), channel_id=1, source_target_pairs={{0,1},{1,0},{2,3},{3,2},{4,5},{5,4},{6,7},{7,6},{8,9},{9,8},{10,11... | collective-permute-start | bytes 1572872 | tf_op jit(solution)/shard_map/right_sum/ppermute | solution.py:30
  48.0 7.1 %collective-permute-start.23 = (f32[256,256]{1,0:T(8,128)S(1)}, f32[256,256]{1,0:T(8,128)S(1)}, u32[]{:S(2)}, u32[]{:S(2)}) collective-permute-start(f32[256,256]{1,0:T(8,128)S(1)} %get-tuple-element.43), channel_id=1, source_target_pairs={{0,8},{1,33},{2,10},{3,35},{4,12},{5,37},{6,14},{7,39},{8,0},{9,41... | collective-permute-start | bytes 786440 | tf_op jit(solution)/shard_map/right_sum/ppermute | solution.py:30
  49.3 8.6 %collective-permute-start.24 = (f32[256,256]{1,0:T(8,128)S(1)}, f32[256,256]{1,0:T(8,128)S(1)}, u32[]{:S(2)}, u32[]{:S(2)}) collective-permute-start(f32[256,256]{1,0:T(8,128)S(1)} %get-tuple-element.44), channel_id=1, source_target_pairs={{0,12},{1,49},{2,14},{3,51},{4,8},{5,53},{6,10},{7,55},{8,4},{9,57... | collective-permute-start | bytes 786440 | tf_op jit(solution)/shard_map/right_sum/ppermute | solution.py:30
  50.1 7.8 %collective-permute-start.25 = (f32[256,256]{1,0:T(8,128)S(1)}, f32[256,256]{1,0:T(8,128)S(1)}, u32[]{:S(2)}, u32[]{:S(2)}) collective-permute-start(f32[256,256]{1,0:T(8,128)S(1)} %get-tuple-element.45), channel_id=1, source_target_pairs={{0,4},{1,17},{2,6},{3,19},{4,0},{5,21},{6,2},{7,23},{8,12},{9,25},... | collective-permute-start | bytes 786440 | tf_op jit(solution)/shard_map/right_sum/ppermute | solution.py:30
  58.0 4.9 %collective-permute-start.26 = (f32[80,256]{1,0:T(8,128)S(1)}, f32[80,256]{1,0:T(8,128)S(1)}, u32[]{:S(2)}, u32[]{:S(2)}) collective-permute-start(f32[80,256]{1,0:T(8,128)S(1)} %get-tuple-element.47), channel_id=1, source_target_pairs={{0,32},{1,9},{2,34},{3,11},{4,36},{5,13},{6,38},{7,15},{8,40},{9,1... | collective-permute-start | bytes 245768 | tf_op jit(solution)/shard_map/right_sum/ppermute | solution.py:30
  59.2 4.9 %collective-permute-start.27 = (f32[80,256]{1,0:T(8,128)S(1)}, f32[80,256]{1,0:T(8,128)S(1)}, u32[]{:S(2)}, u32[]{:S(2)}) collective-permute-start(f32[80,256]{1,0:T(8,128)S(1)} %get-tuple-element.48), channel_id=1, source_target_pairs={{0,48},{1,13},{2,50},{3,15},{4,52},{5,9},{6,54},{7,11},{8,56},{9,5... | collective-permute-start | bytes 245768 | tf_op jit(solution)/shard_map/right_sum/ppermute | solution.py:30
  60.5 3.6 %collective-permute-start.28 = (f32[80,256]{1,0:T(8,128)S(1)}, f32[80,256]{1,0:T(8,128)S(1)}, u32[]{:S(2)}, u32[]{:S(2)}) collective-permute-start(f32[80,256]{1,0:T(8,128)S(1)} %get-tuple-element.49), channel_id=1, source_target_pairs={{0,16},{1,5},{2,18},{3,7},{4,20},{5,1},{6,22},{7,3},{8,24},{9,13},... | collective-permute-start | bytes 245768 | tf_op jit(solution)/shard_map/right_sum/ppermute | solution.py:30
  64.1 5.5 %collective-permute-start.29 = (f32[80,256]{1,0:T(8,128)S(1)}, f32[80,256]{1,0:T(8,128)S(1)}, u32[]{:S(2)}, u32[]{:S(2)}) collective-permute-start(f32[80,256]{1,0:T(8,128)S(1)} %right_sum.12.own), channel_id=1, source_target_pairs={{0,130},{1,131},{2,128},{3,129},{4,134},{5,135},{6,132},{7,133},{8... | collective-permute-start | bytes 245768 | tf_op jit(solution)/shard_map/right_sum/ppermute | solution.py:30
  69.6 10.4 %collective-permute-start.33 = (f32[64,256]{1,0:T(8,128)S(1)}, f32[64,256]{1,0:T(8,128)S(1)}, u32[]{:S(2)}, u32[]{:S(2)}) collective-permute-start(f32[64,256]{1,0:T(8,128)S(1)} %get-tuple-element.52.own), channel_id=1, source_target_pairs={{0,128},{1,129},{2,130},{3,131},{4,132},{5,133},{6,134},{7,135},{8... | collective-permute-start | bytes 196616 | tf_op jit(solution)/shard_map/right_sum/ppermute | solution.py:30
  70.3 9.8 %collective-permute-start.32 = (f32[64,256]{1,0:T(8,128)S(1)}, f32[64,256]{1,0:T(8,128)S(1)}, u32[]{:S(2)}, u32[]{:S(2)}) collective-permute-start(f32[64,256]{1,0:T(8,128)S(1)} %get-tuple-element.52.own), channel_id=1, source_target_pairs={{0,192},{1,193},{2,194},{3,195},{4,196},{5,197},{6,198},{7,199},{8... | collective-permute-start | bytes 196616 | tf_op jit(solution)/shard_map/right_sum/ppermute | solution.py:30
  71.9 8.1 %collective-permute-start.31 = (f32[64,256]{1,0:T(8,128)S(1)}, f32[64,256]{1,0:T(8,128)S(1)}, u32[]{:S(2)}, u32[]{:S(2)}) collective-permute-start(f32[64,256]{1,0:T(8,128)S(1)} %get-tuple-element.52.own), channel_id=1, source_target_pairs={{0,64},{1,65},{2,66},{3,67},{4,68},{5,69},{6,70},{7,71},{8,72},{9,... | collective-permute-start | bytes 196616 | tf_op jit(solution)/shard_map/right_sum/ppermute | solution.py:30
  72.3 5.2 %collective-permute-start.30 = (f32[16,256]{1,0:T(8,128)S(1)}, f32[16,256]{1,0:T(8,128)S(1)}, u32[]{:S(2)}, u32[]{:S(2)}) collective-permute-start(f32[16,256]{1,0:T(8,128)S(1)} %get-tuple-element.50.own), channel_id=1, source_target_pairs={{0,1},{1,0},{2,3},{3,2},{4,5},{5,4},{6,7},{7,6},{8,9},{9,8},{10,11... | collective-permute-start | bytes 49160 | tf_op jit(solution)/shard_map/right_sum/ppermute | solution.py:30
  100.3 4.6 %collective-permute-start.34 = (f32[16,64,256]{2,1,0:T(8,128)S(1)}, f32[16,64,256]{2,1,0:T(8,128)S(1)}, u32[]{:S(2)}, u32[]{:S(2)}) collective-permute-start(f32[16,64,256]{2,1,0:T(8,128)S(1)} %all_to_all.5.refs_2_.refs_4_), channel_id=1, source_target_pairs={{0,1},{1,0},{2,3},{3,2},{4,5},{5,4},{6,7},{7,6},{8,9},{9,8},{10,11... | collective-permute-start | bytes 3145736 | tf_op jit(solution)/shard_map/right_factor/ppermute | solution.py:30
  (4 other events, 22.1 us)
